TPU v7x, 128 devices: a whole 4x4x4 slice. The times are simulated.
128 devices in a mesh: item: 8 (over z, core), list: 16 (over y, x).
Axes of the slice: x: 4, y: 4, z: 4, core: 2. Of those that a mesh axis runs over, the one named last changes fastest.
Arguments:
- items: bfloat16 [32768, 256], P('item', 'list'), may hold values from -6 to 6
- item_weight: float32 [32768], P('item'), may hold values from 1 to 10
- list_capacity: float32 [32768], P('list'), may hold values from 1 to 10
- centroids: bfloat16 [32768, 256], P('list'), may hold values from -6 to 6
Outputs:
- new_centroids: bfloat16 [32768, 256], P('list')
All inputs are finite; a program needn't handle non-finite values.
Results may differ from a plain program's by a relative error of at most 0.015.
Values may be sent and summed in bfloat16 or wider, within the bound.
No kernel may reach another device: no remote copies, remote signals or barrier semaphores. Data moves between devices by JAX's collectives and lax.ppermute only.
A program may use at most 128 MiB of HBM per device.

v0:
```python
import math

import jax
import jax.numpy as jnp
from jax import lax
from jax.sharding import PartitionSpec as P

E = 256
ITERS = 3


epsilon = 1e-06


def unit_rows(values):
    values = values.astype(jnp.float32)
    square = jnp.mean(values * values, axis=-1, keepdims=True)
    return values * lax.rsqrt(square + epsilon) * values.shape[-1] ** (-0.5)


def finish(totals, list_unit, capacity):
    mixed = 0.1 * list_unit.astype(jnp.float32) + totals / capacity[:, None]
    return unit_rows(mixed).astype(jnp.bfloat16)


def local(items, item_weight, list_capacity, centroids):
    sharpness = 2.5 * math.sqrt(E)
    whole = lax.all_gather(items, "list", axis=1, tiled=True)
    item_unit = unit_rows(whole).astype(jnp.bfloat16)
    list_unit = unit_rows(centroids).astype(jnp.bfloat16)
    scores = jnp.dot(item_unit, list_unit.T, preferred_element_type=jnp.float32)
    stored = jnp.exp(sharpness * scores)

    def tile_of():
        return stored

    col_scale = jnp.ones((centroids.shape[0],), jnp.float32)
    row_scale = item_weight
    for step in range(ITERS):
        tile = tile_of()
        row_total = lax.psum(jnp.dot(tile, col_scale, precision=lax.Precision.HIGHEST), "list")
        row_scale = item_weight / row_total
        col_total = lax.psum(jnp.dot(row_scale, tile, precision=lax.Precision.HIGHEST), "item")
        col_scale = list_capacity / col_total
    plan = (row_scale[:, None] * tile_of() * col_scale[None, :]).astype(jnp.bfloat16)
    term = lax.dot_general(
        plan, item_unit, (((0,), (0,)), ((), ())), preferred_element_type=jnp.float32
    )
    totals = lax.psum(term.astype(jnp.bfloat16), "item").astype(jnp.float32)
    return finish(totals, list_unit, list_capacity)


def solution(mesh):
    placed = (P("item", "list"), P("item"), P("list"), P("list", None))
    return jax.shard_map(
        local, mesh=mesh, in_specs=placed, out_specs=P("list", None), check_vma=False
    )
```

profile of v0, /device:TPU:1, one launch (start us, length us, event | category | flops | bytes accessed | tf_op | source)
XLA Modules:
  0.0 559.0 jit_solution(797836832884275622)
XLA Ops:
  6.5 0.0 all-gather.2.cloned.1.call-start
  6.5 0.7 all-gather.2.cloned.1.call-update
  7.3 0.0 all-reduce.2.cloned.1.call-start
  7.3 1.6 fusion.7
  8.9 47.8 %all-gather.2.cloned.1.call-done = bf16[4096,256]{0,1:T(8,128)(2,1)} async-done(((bf16[4096,16]{0,1:T(8,128)(2,1)}), bf16[4096,256]{0,1:T(8,128)(2,1)}) %all-gather.2.cloned.1.call-update) | async-done | bytes 2097168 | tf_op jit(solution)/shard_map/all_gather | solution.py:28
  56.7 2.0 fusion.3
  58.8 15.9 %multiply_exponential_fusion = f32[4096,2048]{1,0:T(8,128)} fusion(bf16[4096,256]{0,1:T(8,128)(2,1)} %all-gather.2.cloned.1.call-done, f32[4096]{0:T(1024)S(1)} %add_rsqrt_fusion, bf16[2048,256]{1,0:T(8,128)(2,1)} %param.7, f32[2048]{0:T(1024)S(1)} %add_rsqrt_fusion.2), kind=kOutput, calls=%fused_computation.1 | convolution fusion | flops 4309647360 | bytes 36724736 | tf_op jit(solution)/shard_map/dot_general | solution.py:31
  74.7 0.0 copy-start.2
  74.7 31.8 %fusion.13 = f32[1,4096]{1,0:T(1,128)S(1)} fusion(f32[4096,2048]{1,0:T(8,128)} %multiply_exponential_fusion), kind=kOutput, calls=%fused_computation.22 | convolution fusion | flops 100663296 | bytes 33570816 | tf_op jit(solution)/shard_map/dot_general | solution.py:41
  106.5 58.4 %psum.49 = f32[4096]{0:T(1024)S(1)} all-reduce(f32[4096]{0:T(1024)S(1)} %bitcast.24), channel_id=1, replica_groups=mesh['item'=8,'list'=16] {'list'}, use_global_device_ids=true, to_apply=%region_2.0 | all-reduce | flops 4096 | bytes 32768 | tf_op jit(solution)/shard_map/psum | solution.py:41
  164.9 0.0 copy-done.2
  164.9 0.0 copy-start.3
  164.9 19.5 %fusion.18 = f32[1,2048]{1,0:T(1,128)S(1)} fusion(f32[4096,1]{0,1:T(1,128)S(1)} %bitcast.26, f32[4096,2048]{1,0:T(8,128)} %multiply_exponential_fusion), kind=kOutput, calls=%fused_computation.27 | convolution fusion | flops 100663296 | bytes 33579008 | tf_op jit(solution)/shard_map/dot_general | solution.py:43
  184.5 27.8 %psum.50 = f32[2048]{0:T(1024)S(1)} all-reduce(f32[2048]{0:T(1024)S(1)} %bitcast.30), channel_id=1, replica_groups=mesh['item'=8,'list'=16] {'item'}, use_global_device_ids=true, to_apply=%region_3.0 | all-reduce | flops 2048 | bytes 16384 | tf_op jit(solution)/shard_map/psum | solution.py:43
  212.3 0.0 copy-done.3
  212.3 31.6 %fusion.19 = f32[1,4096]{1,0:T(1,128)S(1)} fusion(f32[4096,2048]{1,0:T(8,128)} %multiply_exponential_fusion, f32[2048,1]{0,1:T(1,128)S(1)} %bitcast.28), kind=kOutput, calls=%fused_computation.28 | convolution fusion | flops 100663296 | bytes 33579008 | tf_op jit(solution)/shard_map/dot_general | solution.py:41
  243.9 56.5 %psum.51 = f32[4096]{0:T(1024)S(1)} all-reduce(f32[4096]{0:T(1024)S(1)} %bitcast.22), channel_id=1, replica_groups=mesh['item'=8,'list'=16] {'list'}, use_global_device_ids=true, to_apply=%region_4.0 | all-reduce | flops 4096 | bytes 32768 | tf_op jit(solution)/shard_map/psum | solution.py:41
  300.4 19.5 %fusion.20 = f32[1,2048]{1,0:T(1,128)S(1)} fusion(f32[4096,1]{0,1:T(1,128)S(1)} %bitcast.27, f32[4096,2048]{1,0:T(8,128)} %multiply_exponential_fusion), kind=kOutput, calls=%fused_computation.29 | convolution fusion | flops 100663296 | bytes 33579008 | tf_op jit(solution)/shard_map/dot_general | solution.py:43
  319.9 25.8 %psum.52 = f32[2048]{0:T(1024)S(1)} all-reduce(f32[2048]{0:T(1024)S(1)} %bitcast.31), channel_id=1, replica_groups=mesh['item'=8,'list'=16] {'item'}, use_global_device_ids=true, to_apply=%region_5.0 | all-reduce | flops 2048 | bytes 16384 | tf_op jit(solution)/shard_map/psum | solution.py:43
  345.7 31.6 %fusion.21 = f32[1,4096]{1,0:T(1,128)S(1)} fusion(f32[4096,2048]{1,0:T(8,128)} %multiply_exponential_fusion, f32[2048,1]{0,1:T(1,128)S(1)} %bitcast.29), kind=kOutput, calls=%fused_computation.30 | convolution fusion | flops 100663296 | bytes 33579008 | tf_op jit(solution)/shard_map/dot_general | solution.py:41
  377.3 55.8 %psum.53 = f32[4096]{0:T(1024)S(1)} all-reduce(f32[4096]{0:T(1024)S(1)} %bitcast.23), channel_id=1, replica_groups=mesh['item'=8,'list'=16] {'list'}, use_global_device_ids=true, to_apply=%region_6.0 | all-reduce | flops 4096 | bytes 32768 | tf_op jit(solution)/shard_map/psum | solution.py:41
  433.2 0.0 copy-start
  433.2 19.7 %fusion.22 = f32[1,2048]{1,0:T(1,128)S(1)} fusion(f32[4096,1]{0,1:T(1,128)S(1)} %bitcast.25, f32[4096,2048]{1,0:T(8,128)} %multiply_exponential_fusion), kind=kOutput, calls=%fused_computation.31 | convolution fusion | flops 100663296 | bytes 33579008 | tf_op jit(solution)/shard_map/dot_general | solution.py:43
  452.9 26.6 %psum.54 = f32[2048]{0:T(1024)S(1)} all-reduce(f32[2048]{0:T(1024)S(1)} %bitcast.32), channel_id=1, replica_groups=mesh['item'=8,'list'=16] {'item'}, use_global_device_ids=true, to_apply=%region_7.0 | all-reduce | flops 2048 | bytes 16384 | tf_op jit(solution)/shard_map/psum | solution.py:43
  479.5 0.0 copy-done
  479.5 0.0 copy-start.1
  479.5 14.7 %fusion.6 = bf16[2048,256]{1,0:T(8,128)(2,1)} fusion(f32[4096,2048]{1,0:T(8,128)} %multiply_exponential_fusion, f32[2048]{0:T(1024)S(1)} %div.46, f32[4096]{0:T(1024)S(1)} %div.45, bf16[4096,256]{0,1:T(8,128)(2,1)S(1)} %copy-done, f32[4096]{0:T(1024)S(1)} %add_rsqrt_fusion), kind=kOutput, calls=%fused_computation.12 | convolution fusion | flops 4324851712 | bytes 36741120 | tf_op jit(solution)/shard_map/dot_general | solution.py:46
  494.2 0.0 all-reduce.2.cloned.1.call-update
  494.2 54.2 %all-reduce.2.cloned.1.call-done = bf16[2048,256]{1,0:T(8,128)(2,1)} async-done(((bf16[2048,256]{1,0:T(8,128)(2,1)}), bf16[2048,256]{1,0:T(8,128)(2,1)}) %all-reduce.2.cloned.1.call-update) | async-done | bytes 1048592 | tf_op jit(solution)/shard_map/psum | solution.py:49
  548.4 0.0 copy-done.1
  548.4 2.2 multiply_reduce_fusion
  550.6 1.3 multiply_convert_fusion.4
  (9 shorter events, 0.1 us)
Async XLA Ops:
  6.5 50.2 %all-gather.2.cloned.1.call-start = ((), (), s32[]{:S(2)}) async-start(), calls=%async_computation | async-start | bytes 2228224 | tf_op jit(solution)/shard_map/all_gather | solution.py:28
  7.3 541.1 %all-reduce.2.cloned.1.call-start = ((), (), s32[]{:S(2)}) async-start(), calls=%async_computation.1 | async-start | bytes 2097152 | tf_op jit(solution)/shard_map/psum | solution.py:49
  74.7 90.2 %copy-start.2 = (f32[4096]{0:T(1024)S(1)}, f32[4096]{0:T(1024)}, u32[]{:S(2)}) copy-start(f32[4096]{0:T(1024)} %param.5) | copy-start | bytes 49156
  164.9 47.3 %copy-start.3 = (f32[2048]{0:T(1024)S(1)}, f32[2048]{0:T(1024)}, u32[]{:S(2)}) copy-start(f32[2048]{0:T(1024)} %param.6) | copy-start | bytes 24580
  433.2 46.3 %copy-start = (bf16[4096,256]{0,1:T(8,128)(2,1)S(1)}, bf16[4096,256]{0,1:T(8,128)(2,1)}, u32[]{:S(2)}) copy-start(bf16[4096,256]{0,1:T(8,128)(2,1)} %all-gather.2.cloned.1.call-done) | copy-start | bytes 6291460
  479.5 68.9 %copy-start.1 = (bf16[2048,256]{1,0:T(8,128)(2,1)S(1)}, bf16[2048,256]{1,0:T(8,128)(2,1)}, u32[]{:S(2)}) copy-start(bf16[2048,256]{1,0:T(8,128)(2,1)} %param.7) | copy-start | bytes 3145732
Sparse Core Ops, SparseCore 0:
  9.5 47.1 all-gather.1
  494.3 53.9 all-reduce.1
where the time goes:
time: 568 us; the launch traced here: 559 us
  blocking collectives  251 us (44%)
  matrix products  184 us (32%)
  waiting for transfers between devices  103 us (18%)
  between operations  13.8 us (2%)
  other arithmetic  7.2 us (1%)
    psum x3, blocking collectives, local(): lax.psum(jnp.dot(tile, col_scale, precision=lax.Precision.HIGHEST), 'list')  171 us
    dot_general x3, matrix products, local(): jnp.dot(tile, col_scale, precision=lax.Precision.HIGHEST)  95.1 us
    psum x3, blocking collectives, local(): lax.psum(jnp.dot(row_scale, tile, precision=lax.Precision.HIGHEST), 'item')  80.1 us
    dot_general x3, matrix products, local(): jnp.dot(row_scale, tile, precision=lax.Precision.HIGHEST)  58.7 us
    psum x1, waiting for transfers between devices, local(): totals = lax.psum(term.astype(jnp.bfloat16), 'item').astype(jnp.float32)  54.2 us
    all_gather x1, waiting for transfers between devices, local(): whole = lax.all_gather(items, 'list', axis=1, tiled=True)  47.8 us
    dot_general x1, matrix products, local(): scores = jnp.dot(item_unit, list_unit.T, preferred_element_type=jnp.float32)  15.9 us
    dot_general x1, matrix products, local(): lax.dot_general(plan, item_unit, (((0,), (0,)), ((), ())), preferred_elem...  14.7 us
  transfers between devices with their start and end apart: 2, of which 2 were waited for; matrix products, arithmetic and copies ran while one was open for 0% of the time, Pallas kernels for 0%

commit v1 on v0

v1 whole, which is shorter than its diff:
```python
import functools
import math

import jax
import jax.numpy as jnp
from jax import lax
from jax.experimental import pallas as pl
from jax.experimental.pallas import tpu as pltpu
from jax.sharding import PartitionSpec as P

E = 256
ITERS = 3
EPS = 1e-06
SHARP = 2.5 * math.sqrt(E) * math.log2(math.e)

ITEM_DEV = 4096
LIST_DEV = 2048
N_ITEM = 8
N_LIST = 16

F32 = jnp.float32
BF16 = jnp.bfloat16
VMEM = pltpu.VMEM
PARAMS = pltpu.CompilerParams(vmem_limit_bytes=12 << 20)


def whole():
    return pl.BlockSpec(memory_space=VMEM)


def in_vmem(x):
    return pltpu.with_memory_space_constraint(x, VMEM)


def unit(values, axis):
    square = jnp.mean(values * values, axis=axis, keepdims=True)
    return values * lax.rsqrt(square + EPS) * E ** (-0.5)


def put_rows(total, out_ref):
    for k in range(16):
        row = total[:, 256 * k : 256 * (k + 1)].astype(BF16)
        out_ref[:, k : k + 1, :] = jnp.broadcast_to(row[None], (N_LIST, 1, 256))


def gen_body(feat_ref, cent_ref, kern_ref, item_ref, list_ref, rows_ref, total_ref):
    @pl.loop(0, LIST_DEV // 256)
    def _(m):
        at = pl.ds(pl.multiple_of(m * 256, 256), 256)
        list_ref[at, :] = unit(cent_ref[at, :].astype(F32), 1).astype(BF16)

    @pl.loop(0, ITEM_DEV // 256)
    def _(n):
        at = pl.ds(pl.multiple_of(n * 256, 256), 256)
        block = unit(feat_ref[:, at].astype(F32), 0).astype(BF16)
        item_ref[:, at] = block
        total = jnp.zeros((8, 256), F32)
        for m in range(LIST_DEV // 256):
            rows = slice(256 * m, 256 * (m + 1))
            score = jnp.dot(list_ref[rows, :], block, preferred_element_type=F32)
            value = jnp.exp2(score * SHARP)
            kern_ref[rows, at] = value
            total = total + value.reshape(32, 8, 256).sum(0)
        total_ref[:, at] = total.sum(0, keepdims=True)

    put_rows(total_ref[...], rows_ref)


def gen(feat, cent):
    return pl.pallas_call(
        gen_body,
        out_shape=(
            VMEM((LIST_DEV, ITEM_DEV), F32),
            VMEM((E, ITEM_DEV), BF16),
            VMEM((LIST_DEV, E), BF16),
            VMEM((N_LIST, 16, 256), BF16),
        ),
        in_specs=[whole()] * 2,
        out_specs=(whole(),) * 4,
        scratch_shapes=[VMEM((1, ITEM_DEV), F32)],
        cost_estimate=pl.CostEstimate(flops=2 * LIST_DEV * ITEM_DEV * E, bytes_accessed=1 << 22, transcendentals=LIST_DEV * ITEM_DEV),
        compiler_params=PARAMS,
        name="generate",
    )(feat, cent)


def spread_rows(parts_ref, weight_ref, scale_ref):
    total = parts_ref[...].astype(F32).sum(0)
    scale = weight_ref[...] / total
    for k in range(16):
        scale_ref[:, 256 * k : 256 * (k + 1)] = jnp.broadcast_to(scale[k : k + 1, :], (8, 256))


def lanes_of(partial):
    m = partial.shape[0] // 128
    return jnp.concatenate([partial[128 * k : 128 * (k + 1)].T.sum(0, keepdims=True) for k in range(m)], 0)


def col_sums(kern_ref, scale_ref, partial_ref):
    @pl.loop(0, LIST_DEV // 64)
    def _(m):
        at = pl.ds(pl.multiple_of(m * 64, 64), 64)
        total = jnp.zeros((8, 8, 128), F32)
        for n in range(ITEM_DEV // 128):
            lanes = slice(128 * n, 128 * (n + 1))
            total = total + kern_ref[at, lanes].reshape(8, 8, 128) * scale_ref[:, lanes][None]
        partial_ref[at, :] = total.reshape(64, 128)


def col_body(kern_ref, parts_ref, weight_ref, out_ref, scale_ref, partial_ref):
    spread_rows(parts_ref, weight_ref, scale_ref)
    col_sums(kern_ref, scale_ref, partial_ref)
    out_ref[...] = lanes_of(partial_ref[...])


def col_pass(kern, parts, weight):
    return pl.pallas_call(
        col_body,
        out_shape=VMEM((16, 128), F32),
        in_specs=[whole()] * 3,
        out_specs=whole(),
        scratch_shapes=[VMEM((8, ITEM_DEV), F32), VMEM((LIST_DEV, 128), F32)],
        cost_estimate=pl.CostEstimate(flops=2 * LIST_DEV * ITEM_DEV, bytes_accessed=1 << 22, transcendentals=0),
        compiler_params=PARAMS,
        name="columns",
    )(in_vmem(kern), parts, weight)


def row_body(kern_ref, cols_ref, cap_ref, out_ref, scale_ref, total_ref):
    scale = cap_ref[...] / cols_ref[...]
    for k in range(16):
        scale_ref[128 * k : 128 * (k + 1), :] = jnp.broadcast_to(scale[k : k + 1, :], (128, 128)).T

    @pl.loop(0, ITEM_DEV // 1024)
    def _(n):
        first = pl.multiple_of(n * 1024, 1024)
        total = tuple(jnp.zeros((8, 128), F32) for _ in range(8))

        def step(m, total):
            at = pl.ds(pl.multiple_of(m * 64, 64), 64)
            by = scale_ref[at, :].reshape(8, 8, 128)
            block = kern_ref[at, pl.ds(first, 1024)].reshape(8, 8, 1024)
            total = list(total)
            for j in range(8):
                for k in range(8):
                    total[k] = total[k] + block[j, :, 128 * k : 128 * (k + 1)] * by[j]
            return tuple(total)

        total = lax.fori_loop(0, LIST_DEV // 64, step, total)
        for k in range(8):
            total_ref[:, pl.ds(pl.multiple_of(first + 128 * k, 128), 128)] = total[k].sum(0, keepdims=True)

    put_rows(total_ref[...], out_ref)


def row_pass(kern, cols, cap):
    return pl.pallas_call(
        row_body,
        out_shape=VMEM((N_LIST, 16, 256), BF16),
        in_specs=[whole()] * 3,
        out_specs=whole(),
        scratch_shapes=[VMEM((LIST_DEV, 128), F32), VMEM((1, ITEM_DEV), F32)],
        cost_estimate=pl.CostEstimate(flops=2 * LIST_DEV * ITEM_DEV, bytes_accessed=1 << 22, transcendentals=0),
        compiler_params=PARAMS,
        name="rows",
    )(in_vmem(kern), cols, cap)


def last_body(kern_ref, item_ref, parts_ref, weight_ref, out_ref, cols_ref, scale_ref, mixed_ref):
    spread_rows(parts_ref, weight_ref, scale_ref)

    @pl.loop(0, ITEM_DEV // 256)
    def _(n):
        at = pl.ds(pl.multiple_of(n * 256, 256), 256)
        mixed_ref[at, :] = (item_ref[:, at].astype(F32) * scale_ref[:1, at]).T.astype(BF16)

    for b in range(LIST_DEV // 128):
        rows = slice(128 * b, 128 * (b + 1))
        block = kern_ref[rows, :]
        out_ref[rows, :] = jnp.dot(block.astype(BF16), mixed_ref[...], preferred_element_type=F32).astype(BF16)
        total = jnp.zeros((16, 8, 128), F32)
        for n in range(ITEM_DEV // 128):
            lanes = slice(128 * n, 128 * (n + 1))
            total = total + kern_ref[rows, lanes].reshape(16, 8, 128) * scale_ref[:, lanes][None]
        cols_ref[b : b + 1, :] = total.reshape(128, 128).T.sum(0, keepdims=True)


def last_pass(kern, item, parts, weight):
    return pl.pallas_call(
        last_body,
        out_shape=(VMEM((LIST_DEV, E), BF16), VMEM((16, 128), F32)),
        in_specs=[whole()] * 4,
        out_specs=(whole(),) * 2,
        scratch_shapes=[VMEM((8, ITEM_DEV), F32), VMEM((ITEM_DEV, E), BF16)],
        cost_estimate=pl.CostEstimate(flops=2 * LIST_DEV * ITEM_DEV * E, bytes_accessed=1 << 22, transcendentals=0),
        compiler_params=PARAMS,
        name="totals",
    )(in_vmem(kern), item, parts, weight)


def swap_core(x):
    return lax.ppermute(x, "item", [(i, i ^ 1) for i in range(N_ITEM)])


def along_z(x, step):
    return lax.ppermute(x, "item", [(i, (i + 2 * step) % N_ITEM) for i in range(N_ITEM)])


def sum_cols(x):
    x = x + swap_core(x)
    return x + along_z(x, 1) + along_z(x, 3) + along_z(x, 2)


def share_rows(parts):
    return lax.all_to_all(parts, "list", 0, 0)


def local(items, item_weight, list_capacity, centroids):
    core = lax.axis_index("item") % 2
    z = lax.axis_index("item") // 2
    feat = items.T
    feat = lax.all_to_all(jnp.broadcast_to(feat[None], (N_LIST,) + feat.shape), "list", 0, 0)
    feat = feat.reshape(E, ITEM_DEV)
    weight = item_weight.reshape(16, 256)
    cap = list_capacity.reshape(16, 128)

    kern, item, lists, parts = gen(feat, centroids)
    for step in range(ITERS - 1):
        cols = sum_cols(col_pass(kern, share_rows(parts), weight))
        parts = row_pass(kern, cols, cap)
    mixed, cols = last_pass(kern, item, share_rows(parts), weight)

    mixed = mixed.reshape(2, 4, 256, E)
    cols = cols.reshape(2, 4, 256)
    half = lax.dynamic_index_in_dim(mixed, core, 0, False).astype(F32)
    half = half + swap_core(lax.dynamic_index_in_dim(mixed, 1 - core, 0, False)).astype(F32)
    tops = lax.dynamic_index_in_dim(cols, core, 0, False) + swap_core(lax.dynamic_index_in_dim(cols, 1 - core, 0, False))
    high = tops.astype(BF16)
    low = (tops - high.astype(F32)).astype(BF16)
    pad = jnp.zeros((4, 14, E), BF16)
    sent = jnp.concatenate([half.astype(BF16), high[:, None], low[:, None], pad], 1)

    def piece(d):
        return lax.dynamic_index_in_dim(sent, (z + d) % 4, 0, False)

    mine = [piece(0)] + [along_z(piece(d), d) for d in (1, 3, 2)]
    mine = sum(m.astype(F32) for m in mine)
    totals, col_total = mine[:256], mine[256] + mine[257]
    first = core * 1024 + z * 256
    own = lax.dynamic_slice_in_dim(lists, first, 256, 0)
    done = unit(0.1 * own.astype(F32) + totals / col_total[:, None], 1).astype(BF16)

    out = jnp.zeros((4, 256, E), BF16)
    out = lax.dynamic_update_index_in_dim(out, done, z, 0)
    for d in (1, 3, 2):
        out = lax.dynamic_update_index_in_dim(out, along_z(done, d), (z - d) % 4, 0)
    other = swap_core(out)
    both = jnp.zeros((2, 4, 256, E), BF16)
    both = lax.dynamic_update_index_in_dim(both, out, core, 0)
    both = lax.dynamic_update_index_in_dim(both, other, 1 - core, 0)
    return both.reshape(LIST_DEV, E)


def solution(mesh):
    placed = (P("item", "list"), P("item"), P("list"), P("list", None))
    return jax.shard_map(
        local, mesh=mesh, in_specs=placed, out_specs=P("list", None), check_vma=False
    )
```

time: 568 us -> 185 us (0.33); the launches traced: 559 us -> 185 us
  blocking collectives: 251 us -> 44.5 us
  matrix products: 184 us -> 0 us
  waiting for transfers between devices: 103 us -> 35.7 us
  local copies, waits for them, and re-layouts: 0.02 us -> 35.6 us
  starting transfers between devices: 0.04 us -> 34.1 us
  Pallas kernels: 0 us -> 32.7 us
  between operations: 13.8 us -> 0.31 us
    psum x6 -> x0, blocking collectives: 251 us -> none  [the longest x3 171 us: local(): lax.psum(jnp.dot(tile, col_scale, precision=lax.Precision.HIGHEST), 'list')]
    dot_general x8 -> x0, matrix products: 184 us -> none  [the longest x3 95.1 us: local(): jnp.dot(tile, col_scale, precision=lax.Precision.HIGHEST)]
    psum x1 -> x0, waiting for transfers between devices: 54.2 us -> none  [local(): totals = lax.psum(term.astype(jnp.bfloat16), 'item').astype(jnp.float32)]
    all_gather x1 -> x0, waiting for transfers between devices: 47.8 us -> none  [local(): whole = lax.all_gather(items, 'list', axis=1, tiled=True)]
    all_to_all x0 -> x2, blocking collectives: none -> 44.5 us  [the longest x1 34.9 us: local(): lax.all_to_all(jnp.broadcast_to(feat[None], (N_LIST,) + feat.shape), 'lis...]
    unnamed x8 -> x16, local copies, waits for them, and re-layouts: 0.02 us -> 34.1 us
    pallas_call x0 -> x6, Pallas kernels: none -> 32.7 us  [the longest x1 10.3 us: gen(): pl.pallas_call(gen_body, out_shape=(VMEM((LIST_DEV, ITEM_DEV), F32), VMEM...]
    ppermute x0 -> x17, starting transfers between devices: none -> 26.9 us  [the longest x12 15.3 us: along_z(): lax.ppermute(x, 'item', [(i, (i + 2 * step) % N_ITEM) for i in range(N_IT...]
  transfers between devices with their start and end apart: 2 -> 19, of which waited for: 2 -> 14; matrix products, arithmetic and copies ran while one was open for 0% -> 0% of each run, Pallas kernels for 0% -> 0%
where the time goes in v1:
time: 185 us
  blocking collectives  44.5 us (24%)
  waiting for transfers between devices  35.7 us (19%)
  local copies, waits for them, and re-layouts  35.6 us (19%)
  starting transfers between devices  34.1 us (18%)
  Pallas kernels  32.7 us (18%)
    all_to_all x1, blocking collectives, local(): lax.all_to_all(jnp.broadcast_to(feat[None], (N_LIST,) + feat.shape), 'lis...  34.9 us
    unnamed x16, local copies, waits for them, and re-layouts  34.1 us
    ppermute x12, waiting for transfers between devices, along_z(): lax.ppermute(x, 'item', [(i, (i + 2 * step) % N_ITEM) for i in range(N_IT...  18 us
    ppermute x12, starting transfers between devices, along_z(): lax.ppermute(x, 'item', [(i, (i + 2 * step) % N_ITEM) for i in range(N_IT...  15.3 us
    all_to_all x2, waiting for transfers between devices, share_rows(): return lax.all_to_all(parts, 'list', 0, 0)  13.4 us
    ppermute x5, starting transfers between devices, swap_core(): return lax.ppermute(x, 'item', [(i, i ^ 1) for i in range(N_ITEM)])  11.6 us
    pallas_call x1, Pallas kernels, gen(): pl.pallas_call(gen_body, out_shape=(VMEM((LIST_DEV, ITEM_DEV), F32), VMEM...  10.3 us
    all_to_all x1, blocking collectives, share_rows(): return lax.all_to_all(parts, 'list', 0, 0)  9.64 us
  transfers between devices with their start and end apart: 19, of which 14 were waited for; matrix products, arithmetic and copies ran while one was open for 0% of the time, Pallas kernels for 0%

profile of v1, /device:TPU:1, one launch (start us, length us, event | category | flops | bytes accessed | tf_op | source)
XLA Modules:
  0.0 184.6 jit_solution(12424079105391910998)
XLA Ops:
  0.0 1.1 broadcast_in_dim.45
  1.2 34.9 %all_to_all.20 = bf16[16,16,4096]{2,1,0:T(8,128)(2,1)S(1)} all-to-all(bf16[16,16,4096]{2,1,0:T(8,128)(2,1)S(1)} %broadcast_in_dim.45), channel_id=1, replica_groups=mesh['item'=8,'list'=16] {'list'}, dimensions={0} | all-to-all | bytes 4194304 | tf_op jit(solution)/shard_map/all_to_all | solution.py:222
  36.0 10.3 %generate.1 = (f32[2048,4096]{1,0:T(8,128)S(1)}, bf16[256,4096]{1,0:T(8,128)(2,1)S(1)}, bf16[2048,256]{1,0:T(8,128)(2,1)S(1)}, bf16[16,16,256]{2,1,0:T(8,128)(2,1)}) custom-call(bf16[256,4096]{1,0:T(8,128)(2,1)S(1)} %bitcast.44, bf16[2048,256]{1,0:T(8,128)(2,1)S(1)} %copy-done.5), custom_call_target="tpu_custom_call" | custom-call | flops 4294967296 | bytes 4194304 | tf_op jit(solution)/shard_map/generate/pallas_call | solution.py:70
  46.3 11.1 %copy-done = f32[2048,4096]{1,0:T(8,128)} copy-done((f32[2048,4096]{1,0:T(8,128)}, f32[2048,4096]{1,0:T(8,128)S(1)}, u32[]{:S(2)}) %copy-start) | copy-done | bytes 33554456
  57.4 1.0 copy-done.4
  58.4 3.5 %all-to-all-start.1 = ((bf16[16,16,256]{2,1,0:T(8,128)(2,1)}), bf16[16,16,256]{2,1,0:T(8,128)(2,1)S(1)}, u32[]{:S(2)}, u32[]{:S(2)}) async-start(bf16[16,16,256]{2,1,0:T(8,128)(2,1)} %get-tuple-element.14), calls=%async_computation.1 | async-start | bytes 262144 | tf_op jit(solution)/shard_map/all_to_all | solution.py:215
  61.9 6.8 %all-to-all-done.1.parts_ref = bf16[16,16,256]{2,1,0:T(8,128)(2,1)S(1)} async-done(((bf16[16,16,256]{2,1,0:T(8,128)(2,1)}), bf16[16,16,256]{2,1,0:T(8,128)(2,1)S(1)}, u32[]{:S(2)}, u32[]{:S(2)}) %all-to-all-start.1) | async-done | bytes 131104 | tf_op jit(solution)/shard_map/all_to_all | solution.py:215
  68.7 10.5 %copy-done.1 = f32[2048,4096]{1,0:T(8,128)S(1)} copy-done((f32[2048,4096]{1,0:T(8,128)S(1)}, f32[2048,4096]{1,0:T(8,128)}, u32[]{:S(2)}) %copy-start.1) | copy-done | bytes 33554456
  79.2 3.3 %columns.2 = f32[16,128]{1,0:T(8,128)S(1)} custom-call(f32[2048,4096]{1,0:T(8,128)S(1)} %copy-done.1, bf16[16,16,256]{2,1,0:T(8,128)(2,1)S(1)} %all-to-all-done.1.parts_ref, f32[16,256]{1,0:T(8,128)S(1)} %reshape.42.weight_ref), custom_call_target="tpu_custom_call" | custom-call | flops 16777216 | bytes 4194304 | tf_op jit(solution)/shard_map/columns/pallas_call | solution.py:117
  82.5 3.2 %collective-permute-start = (f32[16,128]{1,0:T(8,128)S(1)}, f32[16,128]{1,0:T(8,128)S(1)}, u32[]{:S(2)}, u32[]{:S(2)}) collective-permute-start(f32[16,128]{1,0:T(8,128)S(1)} %columns.2), channel_id=1, source_target_pairs={{0,16},{16,0},{32,48},{48,32},{64,80},{80,64},{96,112},{112,96},{1... | collective-permute-start | bytes 24584 | tf_op jit(solution)/shard_map/ppermute | solution.py:202
  85.7 0.8 collective-permute-done
  86.6 1.6 collective-permute-start.1
  88.2 2.1 %collective-permute-start.2 = (f32[16,128]{1,0:T(8,128)S(1)}, f32[16,128]{1,0:T(8,128)S(1)}, u32[]{:S(2)}, u32[]{:S(2)}) collective-permute-start(f32[16,128]{1,0:T(8,128)S(1)} %add.150), channel_id=1, source_target_pairs={{0,96},{16,112},{32,0},{48,16},{64,32},{80,48},{96,64},{112,80},{1... | collective-permute-start | bytes 24584 | tf_op jit(solution)/shard_map/ppermute | solution.py:206
  90.3 1.3 collective-permute-start.3
  91.6 2.7 %collective-permute-done.3 = f32[16,128]{1,0:T(8,128)S(1)} collective-permute-done((f32[16,128]{1,0:T(8,128)S(1)}, f32[16,128]{1,0:T(8,128)S(1)}, u32[]{:S(2)}, u32[]{:S(2)}) %collective-permute-start.3) | collective-permute-done | bytes 8224 | tf_op jit(solution)/shard_map/ppermute | solution.py:206
  94.3 3.5 %rows.2 = bf16[16,16,256]{2,1,0:T(8,128)(2,1)S(1)} custom-call(f32[2048,4096]{1,0:T(8,128)S(1)} %copy-done.1, f32[16,128]{1,0:T(8,128)S(1)} %add_add_fusion.1.cols_ref, f32[16,128]{1,0:T(8,128)S(1)} %bitcast.47), custom_call_target="tpu_custom_call" | custom-call | flops 16777216 | bytes 4194304 | tf_op jit(solution)/shard_map/rows/pallas_call | solution.py:157
  97.8 9.6 %all_to_all.21.parts_ref = bf16[16,16,256]{2,1,0:T(8,128)(2,1)S(1)} all-to-all(bf16[16,16,256]{2,1,0:T(8,128)(2,1)S(1)} %rows.2), channel_id=1, replica_groups=mesh['item'=8,'list'=16] {'list'}, dimensions={0} | all-to-all | bytes 262144 | tf_op jit(solution)/shard_map/all_to_all | solution.py:215
  107.4 3.3 %columns.3 = f32[16,128]{1,0:T(8,128)S(1)} custom-call(f32[2048,4096]{1,0:T(8,128)S(1)} %copy-done.1, bf16[16,16,256]{2,1,0:T(8,128)(2,1)S(1)} %all_to_all.21.parts_ref, f32[16,256]{1,0:T(8,128)S(1)} %reshape.42.weight_ref), custom_call_target="tpu_custom_call" | custom-call | flops 16777216 | bytes 4194304 | tf_op jit(solution)/shard_map/columns/pallas_call | solution.py:117
  110.7 3.3 %collective-permute-start.4 = (f32[16,128]{1,0:T(8,128)S(1)}, f32[16,128]{1,0:T(8,128)S(1)}, u32[]{:S(2)}, u32[]{:S(2)}) collective-permute-start(f32[16,128]{1,0:T(8,128)S(1)} %columns.3), channel_id=1, source_target_pairs={{0,16},{16,0},{32,48},{48,32},{64,80},{80,64},{96,112},{112,96},{1... | collective-permute-start | bytes 24584 | tf_op jit(solution)/shard_map/ppermute | solution.py:202
  114.0 0.8 collective-permute-done.4
  114.9 2.7 %collective-permute-start.6 = (f32[16,128]{1,0:T(8,128)S(1)}, f32[16,128]{1,0:T(8,128)S(1)}, u32[]{:S(2)}, u32[]{:S(2)}) collective-permute-start(f32[16,128]{1,0:T(8,128)S(1)} %add.154), channel_id=1, source_target_pairs={{0,96},{16,112},{32,0},{48,16},{64,32},{80,48},{96,64},{112,80},{1... | collective-permute-start | bytes 24584 | tf_op jit(solution)/shard_map/ppermute | solution.py:206
  117.5 0.4 collective-permute-start.7
  117.9 0.7 collective-permute-done.5
  118.6 3.0 %collective-permute-done.7 = f32[16,128]{1,0:T(8,128)S(1)} collective-permute-done((f32[16,128]{1,0:T(8,128)S(1)}, f32[16,128]{1,0:T(8,128)S(1)}, u32[]{:S(2)}, u32[]{:S(2)}) %collective-permute-start.7) | collective-permute-done | bytes 8224 | tf_op jit(solution)/shard_map/ppermute | solution.py:206
  121.5 4.1 %rows.3 = bf16[16,16,256]{2,1,0:T(8,128)(2,1)} custom-call(f32[2048,4096]{1,0:T(8,128)S(1)} %copy-done.1, f32[16,128]{1,0:T(8,128)S(1)} %add_add_fusion.cols_ref, f32[16,128]{1,0:T(8,128)S(1)} %bitcast.48), custom_call_target="tpu_custom_call" | custom-call | flops 16777216 | bytes 4194304 | tf_op jit(solution)/shard_map/rows/pallas_call | solution.py:157
  125.6 3.7 %all-to-all-start.3 = ((bf16[16,16,256]{2,1,0:T(8,128)(2,1)}), bf16[16,16,256]{2,1,0:T(8,128)(2,1)S(1)}, u32[]{:S(2)}, u32[]{:S(2)}) async-start(bf16[16,16,256]{2,1,0:T(8,128)(2,1)} %rows.3), calls=%async_computation.3 | async-start | bytes 262144 | tf_op jit(solution)/shard_map/all_to_all | solution.py:215
  129.4 6.6 %all-to-all-done.3.parts_ref = bf16[16,16,256]{2,1,0:T(8,128)(2,1)S(1)} async-done(((bf16[16,16,256]{2,1,0:T(8,128)(2,1)}), bf16[16,16,256]{2,1,0:T(8,128)(2,1)S(1)}, u32[]{:S(2)}, u32[]{:S(2)}) %all-to-all-start.3) | async-done | bytes 131104 | tf_op jit(solution)/shard_map/all_to_all | solution.py:215
  136.0 10.5 %copy-done.2 = f32[2048,4096]{1,0:T(8,128)S(1)} copy-done((f32[2048,4096]{1,0:T(8,128)S(1)}, f32[2048,4096]{1,0:T(8,128)}, u32[]{:S(2)}) %copy-start.2) | copy-done | bytes 33554456
  146.5 8.2 %totals.1 = (bf16[2048,256]{1,0:T(8,128)(2,1)S(1)}, f32[16,128]{1,0:T(8,128)S(1)}) custom-call(f32[2048,4096]{1,0:T(8,128)S(1)} %copy-done.2, bf16[256,4096]{1,0:T(8,128)(2,1)S(1)} %get-tuple-element.13.item_ref, bf16[16,16,256]{2,1,0:T(8,128)(2,1)S(1)} %all-to-all-done.3.parts_ref, f32[16,256]{1,0:T(8,128)S(1)} %reshape.42.weight_ref), custom_call_target="tpu_custom_call" | custom-call | flops 4294967296 | bytes 4194304 | tf_op jit(solution)/shard_map/totals/pallas_call | solution.py:189
  154.8 3.3 %collective-permute-start.8 = (bf16[4,256,256]{2,1,0:T(8,128)(2,1)S(1)}, bf16[4,256,256]{2,1,0:T(8,128)(2,1)S(1)}, u32[]{:S(2)}, u32[]{:S(2)}) collective-permute-start(bf16[4,256,256]{2,1,0:T(8,128)(2,1)S(1)} %dynamic-slice_bitcast_fusion), channel_id=1, source_target_pairs={{0,16},{16,0},{32,48},{48,32},{64,80},{80,64},{96,112},{112,96},{1... | collective-permute-start | bytes 1572872 | tf_op jit(solution)/shard_map/ppermute | solution.py:202
  158.1 0.1 collective-permute-start.9
  158.4 1.3 collective-permute-done.9
  159.7 0.1 fusion
  159.8 0.2 maximum_maximum_fusion
  160.1 2.7 %collective-permute-start.11 = (bf16[272,256]{1,0:T(8,128)(2,1)S(1)}, bf16[272,256]{1,0:T(8,128)(2,1)S(1)}, u32[]{:S(2)}, u32[]{:S(2)}) collective-permute-start(bf16[272,256]{1,0:T(8,128)(2,1)S(1)} %get-tuple-element.23), channel_id=1, source_target_pairs={{0,96},{16,112},{32,0},{48,16},{64,32},{80,48},{96,64},{112,80},{1... | collective-permute-start | bytes 417800 | tf_op jit(solution)/shard_map/ppermute | solution.py:206
  162.8 3.4 %collective-permute-done.10 = bf16[272,256]{1,0:T(8,128)(2,1)S(1)} collective-permute-done((bf16[272,256]{1,0:T(8,128)(2,1)S(1)}, bf16[272,256]{1,0:T(8,128)(2,1)S(1)}, u32[]{:S(2)}, u32[]{:S(2)}) %collective-permute-start.10) | collective-permute-done | bytes 139296 | tf_op jit(solution)/shard_map/ppermute | solution.py:206
  166.2 2.0 %collective-permute-done.11 = bf16[272,256]{1,0:T(8,128)(2,1)S(1)} collective-permute-done((bf16[272,256]{1,0:T(8,128)(2,1)S(1)}, bf16[272,256]{1,0:T(8,128)(2,1)S(1)}, u32[]{:S(2)}, u32[]{:S(2)}) %collective-permute-start.11) | collective-permute-done | bytes 139296 | tf_op jit(solution)/shard_map/ppermute | solution.py:206
  168.1 0.4 collective-permute-done.12
  168.6 1.1 multiply_reduce_fusion
  169.8 0.1 bitcast_dynamic-update-slice_fusion.5
  169.9 1.3 collective-permute-start.13
  171.2 2.1 %collective-permute-start.14 = (bf16[256,256]{1,0:T(8,128)(2,1)S(1)}, bf16[256,256]{1,0:T(8,128)(2,1)S(1)}, u32[]{:S(2)}, u32[]{:S(2)}) collective-permute-start(bf16[256,256]{1,0:T(8,128)(2,1)S(1)} %get-tuple-element.18), channel_id=1, source_target_pairs={{0,96},{16,112},{32,0},{48,16},{64,32},{80,48},{96,64},{112,80},{1... | collective-permute-start | bytes 393224 | tf_op jit(solution)/shard_map/ppermute | solution.py:206
  173.3 1.0 collective-permute-start.15
  174.3 1.2 collective-permute-done.13
  175.5 4.8 %collective-permute-done.15 = bf16[256,256]{1,0:T(8,128)(2,1)S(1)} collective-permute-done((bf16[256,256]{1,0:T(8,128)(2,1)S(1)}, bf16[256,256]{1,0:T(8,128)(2,1)S(1)}, u32[]{:S(2)}, u32[]{:S(2)}) %collective-permute-start.15) | collective-permute-done | bytes 131104 | tf_op jit(solution)/shard_map/ppermute | solution.py:206
  180.3 1.8 collective-permute-start.16
  182.2 1.4 collective-permute-done.16
  183.7 1.0 copy-done.6
  (43 shorter events, 0.7 us)
Async XLA Ops:
  1.1 34.9 %copy-start.5 = (bf16[2048,256]{1,0:T(8,128)(2,1)S(1)}, bf16[2048,256]{1,0:T(8,128)(2,1)}, u32[]{:S(2)}) copy-start(bf16[2048,256]{1,0:T(8,128)(2,1)} %cent_ref.1) | copy-start | bytes 3145732
  36.0 25.9 %copy-start.7 = (f32[4096]{0:T(1024)S(1)}, f32[4096]{0:T(1024)}, u32[]{:S(2)}) copy-start(f32[4096]{0:T(1024)} %param.5) | copy-start | bytes 49156
  46.3 11.1 %copy-start = (f32[2048,4096]{1,0:T(8,128)}, f32[2048,4096]{1,0:T(8,128)S(1)}, u32[]{:S(2)}) copy-start(f32[2048,4096]{1,0:T(8,128)S(1)} %get-tuple-element.12.kern_ref) | copy-start | bytes 100663296
  57.4 1.0 copy-start.4
  58.4 10.3 %all-to-all-start.1 = ((bf16[16,16,256]{2,1,0:T(8,128)(2,1)}), bf16[16,16,256]{2,1,0:T(8,128)(2,1)S(1)}, u32[]{:S(2)}, u32[]{:S(2)}) async-start(bf16[16,16,256]{2,1,0:T(8,128)(2,1)} %get-tuple-element.14), calls=%async_computation.1 | async-start | bytes 262144 | tf_op jit(solution)/shard_map/all_to_all | solution.py:215
  68.7 10.5 %copy-start.1 = (f32[2048,4096]{1,0:T(8,128)S(1)}, f32[2048,4096]{1,0:T(8,128)}, u32[]{:S(2)}) copy-start(f32[2048,4096]{1,0:T(8,128)} %copy-done) | copy-start | bytes 100663296
  79.2 15.1 %copy-start.3 = (f32[2048]{0:T(1024)S(1)}, f32[2048]{0:T(1024)}, u32[]{:S(2)}) copy-start(f32[2048]{0:T(1024)} %param.6) | copy-start | bytes 24580
  82.5 4.0 %collective-permute-start = (f32[16,128]{1,0:T(8,128)S(1)}, f32[16,128]{1,0:T(8,128)S(1)}, u32[]{:S(2)}, u32[]{:S(2)}) collective-permute-start(f32[16,128]{1,0:T(8,128)S(1)} %columns.2), channel_id=1, source_target_pairs={{0,16},{16,0},{32,48},{48,32},{64,80},{80,64},{96,112},{112,96},{1... | collective-permute-start | bytes 24584 | tf_op jit(solution)/shard_map/ppermute | solution.py:202
  86.6 5.1 %collective-permute-start.1 = (f32[16,128]{1,0:T(8,128)S(1)}, f32[16,128]{1,0:T(8,128)S(1)}, u32[]{:S(2)}, u32[]{:S(2)}) collective-permute-start(f32[16,128]{1,0:T(8,128)S(1)} %add.150), channel_id=1, source_target_pairs={{0,32},{16,48},{32,64},{48,80},{64,96},{80,112},{96,0},{112,16},{1... | collective-permute-start | bytes 24584 | tf_op jit(solution)/shard_map/ppermute | solution.py:206
  88.2 3.4 %collective-permute-start.2 = (f32[16,128]{1,0:T(8,128)S(1)}, f32[16,128]{1,0:T(8,128)S(1)}, u32[]{:S(2)}, u32[]{:S(2)}) collective-permute-start(f32[16,128]{1,0:T(8,128)S(1)} %add.150), channel_id=1, source_target_pairs={{0,96},{16,112},{32,0},{48,16},{64,32},{80,48},{96,64},{112,80},{1... | collective-permute-start | bytes 24584 | tf_op jit(solution)/shard_map/ppermute | solution.py:206
  90.3 4.0 %collective-permute-start.3 = (f32[16,128]{1,0:T(8,128)S(1)}, f32[16,128]{1,0:T(8,128)S(1)}, u32[]{:S(2)}, u32[]{:S(2)}) collective-permute-start(f32[16,128]{1,0:T(8,128)S(1)} %add.150), channel_id=1, source_target_pairs={{0,64},{16,80},{32,96},{48,112},{64,0},{80,16},{96,32},{112,48},{1... | collective-permute-start | bytes 24584 | tf_op jit(solution)/shard_map/ppermute | solution.py:206
  110.7 4.1 %collective-permute-start.4 = (f32[16,128]{1,0:T(8,128)S(1)}, f32[16,128]{1,0:T(8,128)S(1)}, u32[]{:S(2)}, u32[]{:S(2)}) collective-permute-start(f32[16,128]{1,0:T(8,128)S(1)} %columns.3), channel_id=1, source_target_pairs={{0,16},{16,0},{32,48},{48,32},{64,80},{80,64},{96,112},{112,96},{1... | collective-permute-start | bytes 24584 | tf_op jit(solution)/shard_map/ppermute | solution.py:202
  114.9 3.7 %collective-permute-start.5 = (f32[16,128]{1,0:T(8,128)S(1)}, f32[16,128]{1,0:T(8,128)S(1)}, u32[]{:S(2)}, u32[]{:S(2)}) collective-permute-start(f32[16,128]{1,0:T(8,128)S(1)} %add.154), channel_id=1, source_target_pairs={{0,32},{16,48},{32,64},{48,80},{64,96},{80,112},{96,0},{112,16},{1... | collective-permute-start | bytes 24584 | tf_op jit(solution)/shard_map/ppermute | solution.py:206
  114.9 3.7 %collective-permute-start.6 = (f32[16,128]{1,0:T(8,128)S(1)}, f32[16,128]{1,0:T(8,128)S(1)}, u32[]{:S(2)}, u32[]{:S(2)}) collective-permute-start(f32[16,128]{1,0:T(8,128)S(1)} %add.154), channel_id=1, source_target_pairs={{0,96},{16,112},{32,0},{48,16},{64,32},{80,48},{96,64},{112,80},{1... | collective-permute-start | bytes 24584 | tf_op jit(solution)/shard_map/ppermute | solution.py:206
  117.5 4.0 %collective-permute-start.7 = (f32[16,128]{1,0:T(8,128)S(1)}, f32[16,128]{1,0:T(8,128)S(1)}, u32[]{:S(2)}, u32[]{:S(2)}) collective-permute-start(f32[16,128]{1,0:T(8,128)S(1)} %add.154), channel_id=1, source_target_pairs={{0,64},{16,80},{32,96},{48,112},{64,0},{80,16},{96,32},{112,48},{1... | collective-permute-start | bytes 24584 | tf_op jit(solution)/shard_map/ppermute | solution.py:206
  125.6 10.3 %all-to-all-start.3 = ((bf16[16,16,256]{2,1,0:T(8,128)(2,1)}), bf16[16,16,256]{2,1,0:T(8,128)(2,1)S(1)}, u32[]{:S(2)}, u32[]{:S(2)}) async-start(bf16[16,16,256]{2,1,0:T(8,128)(2,1)} %rows.3), calls=%async_computation.3 | async-start | bytes 262144 | tf_op jit(solution)/shard_map/all_to_all | solution.py:215
  136.0 10.5 %copy-start.2 = (f32[2048,4096]{1,0:T(8,128)S(1)}, f32[2048,4096]{1,0:T(8,128)}, u32[]{:S(2)}) copy-start(f32[2048,4096]{1,0:T(8,128)} %copy-done) | copy-start | bytes 100663296
  154.8 4.9 %collective-permute-start.8 = (bf16[4,256,256]{2,1,0:T(8,128)(2,1)S(1)}, bf16[4,256,256]{2,1,0:T(8,128)(2,1)S(1)}, u32[]{:S(2)}, u32[]{:S(2)}) collective-permute-start(bf16[4,256,256]{2,1,0:T(8,128)(2,1)S(1)} %dynamic-slice_bitcast_fusion), channel_id=1, source_target_pairs={{0,16},{16,0},{32,48},{48,32},{64,80},{80,64},{96,112},{112,96},{1... | collective-permute-start | bytes 1572872 | tf_op jit(solution)/shard_map/ppermute | solution.py:202
  158.1 1.5 collective-permute-start.9
  160.0 6.2 %collective-permute-start.10 = (bf16[272,256]{1,0:T(8,128)(2,1)S(1)}, bf16[272,256]{1,0:T(8,128)(2,1)S(1)}, u32[]{:S(2)}, u32[]{:S(2)}) collective-permute-start(bf16[272,256]{1,0:T(8,128)(2,1)S(1)} %get-tuple-element.21), channel_id=1, source_target_pairs={{0,32},{16,48},{32,64},{48,80},{64,96},{80,112},{96,0},{112,16},{1... | collective-permute-start | bytes 417800 | tf_op jit(solution)/shard_map/ppermute | solution.py:206
  160.1 8.0 %collective-permute-start.11 = (bf16[272,256]{1,0:T(8,128)(2,1)S(1)}, bf16[272,256]{1,0:T(8,128)(2,1)S(1)}, u32[]{:S(2)}, u32[]{:S(2)}) collective-permute-start(bf16[272,256]{1,0:T(8,128)(2,1)S(1)} %get-tuple-element.23), channel_id=1, source_target_pairs={{0,96},{16,112},{32,0},{48,16},{64,32},{80,48},{96,64},{112,80},{1... | collective-permute-start | bytes 417800 | tf_op jit(solution)/shard_map/ppermute | solution.py:206
  162.8 5.7 %collective-permute-start.12 = (bf16[272,256]{1,0:T(8,128)(2,1)S(1)}, bf16[272,256]{1,0:T(8,128)(2,1)S(1)}, u32[]{:S(2)}, u32[]{:S(2)}) collective-permute-start(bf16[272,256]{1,0:T(8,128)(2,1)S(1)} %get-tuple-element.22), channel_id=1, source_target_pairs={{0,64},{16,80},{32,96},{48,112},{64,0},{80,16},{96,32},{112,48},{1... | collective-permute-start | bytes 417800 | tf_op jit(solution)/shard_map/ppermute | solution.py:206
  169.9 5.6 %collective-permute-start.13 = (bf16[256,256]{1,0:T(8,128)(2,1)S(1)}, bf16[256,256]{1,0:T(8,128)(2,1)S(1)}, u32[]{:S(2)}, u32[]{:S(2)}) collective-permute-start(bf16[256,256]{1,0:T(8,128)(2,1)S(1)} %get-tuple-element.18), channel_id=1, source_target_pairs={{0,32},{16,48},{32,64},{48,80},{64,96},{80,112},{96,0},{112,16},{1... | collective-permute-start | bytes 393224 | tf_op jit(solution)/shard_map/ppermute | solution.py:206
  171.2 4.3 %collective-permute-start.14 = (bf16[256,256]{1,0:T(8,128)(2,1)S(1)}, bf16[256,256]{1,0:T(8,128)(2,1)S(1)}, u32[]{:S(2)}, u32[]{:S(2)}) collective-permute-start(bf16[256,256]{1,0:T(8,128)(2,1)S(1)} %get-tuple-element.18), channel_id=1, source_target_pairs={{0,96},{16,112},{32,0},{48,16},{64,32},{80,48},{96,64},{112,80},{1... | collective-permute-start | bytes 393224 | tf_op jit(solution)/shard_map/ppermute | solution.py:206
  173.3 7.0 %collective-permute-start.15 = (bf16[256,256]{1,0:T(8,128)(2,1)S(1)}, bf16[256,256]{1,0:T(8,128)(2,1)S(1)}, u32[]{:S(2)}, u32[]{:S(2)}) collective-permute-start(bf16[256,256]{1,0:T(8,128)(2,1)S(1)} %get-tuple-element.18), channel_id=1, source_target_pairs={{0,64},{16,80},{32,96},{48,112},{64,0},{80,16},{96,32},{112,48},{1... | collective-permute-start | bytes 393224 | tf_op jit(solution)/shard_map/ppermute | solution.py:206
  180.3 3.3 %collective-permute-start.16 = (bf16[4,256,256]{2,1,0:T(8,128)(2,1)S(1)}, bf16[4,256,256]{2,1,0:T(8,128)(2,1)S(1)}, u32[]{:S(2)}, u32[]{:S(2)}) collective-permute-start(bf16[4,256,256]{2,1,0:T(8,128)(2,1)S(1)} %bitcast_dynamic-update-slice_fusion.2), channel_id=1, source_target_pairs={{0,16},{16,0},{32,48},{48,32},{64,80},{80,64},{96,112},{112,96},{1... | collective-permute-start | bytes 1572872 | tf_op jit(solution)/shard_map/ppermute | solution.py:202
  183.6 1.0 copy-start.6

commit v2 on v0

v2 whole, which is shorter than its diff:
```python
import functools
import math

import jax
import jax.numpy as jnp
from jax import lax
from jax.experimental import pallas as pl
from jax.experimental.pallas import tpu as pltpu
from jax.sharding import PartitionSpec as P

E = 256
ITERS = 3
EPS = 1e-06
SHARP = 2.5 * math.sqrt(E) * math.log2(math.e)

ITEM_DEV = 4096
LIST_DEV = 2048
HALF = ITEM_DEV // 2
QUART = ITEM_DEV // 4
N_ITEM = 8
N_LIST = 16

F32 = jnp.float32
BF16 = jnp.bfloat16
VMEM = pltpu.VMEM


def whole(n):
    return [pl.BlockSpec(memory_space=VMEM)] * n


def call(body, args, out, scratch, name, flops=0, limit=4):
    return pl.pallas_call(
        body,
        out_shape=out,
        in_specs=whole(len(args)),
        out_specs=tuple(whole(len(out))) if isinstance(out, tuple) else whole(1)[0],
        scratch_shapes=scratch,
        compiler_params=pltpu.CompilerParams(vmem_limit_bytes=limit << 20),
        cost_estimate=pl.CostEstimate(flops=flops, bytes_accessed=1 << 20, transcendentals=0),
        name=name,
    )(*args)


def unit(values, axis):
    square = jnp.mean(values * values, axis=axis, keepdims=True)
    return values * lax.rsqrt(square + EPS) * E ** (-0.5)


def place():
    item = lax.axis_index("item")
    spot = lax.axis_index("list")
    return item % 2, item // 2, spot // 4, spot % 4


def shift(name, step):
    def along(i):
        if name == "x":
            return i // 4 * 4 + (i + step) % 4
        if name == "y":
            return (i + 4 * step) % N_LIST
        return (i + 2 * step) % N_ITEM

    axis, size = ("item", N_ITEM) if name == "z" else ("list", N_LIST)
    return lambda block: lax.ppermute(block, axis, [(i, along(i)) for i in range(size)])


def swap_core(block):
    return lax.ppermute(block, "item", [(i, i ^ 1) for i in range(N_ITEM)])


ORDER = (0, -1, 1, 2)


def gather_small(block, axis):
    return [block, shift(axis, 1)(block), shift(axis, 3)(block), shift(axis, 2)(block)]


def gather_large(block, axis):
    left, right = shift(axis, 1)(block), shift(axis, 3)(block)
    n = block.shape[0] // 2
    return [block, left, right, shift(axis, 1)(left[:n]), shift(axis, 3)(right[n:])]


def prep_body(cent_ref, weight_ref, cap_ref, list_ref, weight_out_ref, cap_out_ref):
    weight_out_ref[...] = weight_ref[...]
    cap_out_ref[...] = cap_ref[...]
    for m in range(LIST_DEV // 256):
        at = slice(256 * m, 256 * (m + 1))
        list_ref[at, :] = unit(cent_ref[at, :].astype(F32), 1).astype(BF16)


def prep(cent, weight, cap):
    out = (VMEM((LIST_DEV, E), BF16), VMEM((16, 256), F32), VMEM((16, 128), F32))
    return call(prep_body, (cent, weight, cap), out, [], "lists")


def put_rows(total, out_ref):
    for k in range(16):
        row = total[:, 256 * k : 256 * (k + 1)].astype(BF16)
        out_ref[:, k : k + 1, :] = jnp.broadcast_to(row[None], (N_LIST, 1, 256))


TILE_M = 512


def gen_body(last, list_ref, own_ref, left_ref, right_ref, low_ref, high_ref, *refs):
    if last:
        before_ref, *kern_refs, item_ref, rows_ref, feat_ref, total_ref = refs
    else:
        *kern_refs, item_ref, total_ref, feat_ref = refs
    _, _, y, x = place()
    for i, outer in enumerate(ORDER):
        for j, inner in enumerate(ORDER):
            if i < 3:
                block = (own_ref, left_ref, right_ref)[i][16 * j : 16 * (j + 1), :]
            else:
                block = (low_ref, high_ref)[j // 2][16 * (j % 2) : 16 * (j % 2 + 1), :]
            if last:
                spot = (y + inner + 4) % 4 * 4 + (x + outer + 4) % 4
            else:
                spot = (y + outer + 4) % 4 * 4 + (x + inner + 4) % 4
            feat_ref[pl.ds(pl.multiple_of(spot * 16, 16), 16), :] = block

    for n, kern_ref in enumerate(kern_refs):
        at = slice(QUART * n, QUART * (n + 1))
        block = unit(feat_ref[:, at].astype(F32), 0)
        item_ref[at, :] = block.T.astype(BF16)
        block = block.astype(BF16)

        def step(m, total):
            rows = pl.ds(pl.multiple_of(m * TILE_M, TILE_M), TILE_M)
            score = jnp.dot(list_ref[rows, :], block, preferred_element_type=F32)
            value = jnp.exp2(score * SHARP)
            kern_ref[rows, :] = value
            return total + value.reshape(TILE_M // 8, 8, QUART).sum(0)

        total = lax.fori_loop(0, LIST_DEV // TILE_M, step, jnp.zeros((8, QUART), F32))
        total_ref[:, at] = total.sum(0, keepdims=True)

    if last:
        put_rows(jnp.concatenate([before_ref[...], total_ref[...]], 1), rows_ref)


def gen(last, lists, pieces, before=()):
    out = (VMEM((LIST_DEV, QUART), F32),) * 2 + (VMEM((HALF, E), BF16),)
    scratch = [VMEM((E, HALF), BF16)]
    if last:
        out += (VMEM((N_LIST, 16, 256), BF16),)
        scratch += [VMEM((1, HALF), F32)]
    else:
        out += (VMEM((1, HALF), F32),)
    return call(
        functools.partial(gen_body, last), (lists, *pieces, *before), out, scratch, "generate",
        2 * LIST_DEV * HALF * E, 8,
    )


def spread_rows(parts_ref, weight_ref, scale_ref):
    scale = weight_ref[...] / parts_ref[...].astype(F32).sum(0)
    for k in range(16):
        scale_ref[:, 256 * k : 256 * (k + 1)] = jnp.broadcast_to(scale[k : k + 1, :], (8, 256))


def lanes_of(partial):
    m = partial.shape[0] // 128
    return jnp.concatenate([partial[128 * k : 128 * (k + 1)].T.sum(0, keepdims=True) for k in range(m)], 0)


def col_body(*refs):
    *kern_refs, parts_ref, weight_ref, out_ref, scale_ref, partial_ref = refs
    spread_rows(parts_ref, weight_ref, scale_ref)

    @pl.loop(0, LIST_DEV // 64)
    def _(m):
        at = pl.ds(pl.multiple_of(m * 64, 64), 64)
        total = jnp.zeros((8, 8, 128), F32)
        for h, ref in enumerate(kern_refs):
            for n in range(QUART // 128):
                by = scale_ref[:, QUART * h + 128 * n : QUART * h + 128 * (n + 1)]
                total = total + ref[at, 128 * n : 128 * (n + 1)].reshape(8, 8, 128) * by[None]
        partial_ref[at, :] = total.reshape(64, 128)

    out_ref[...] = jnp.broadcast_to(lanes_of(partial_ref[...])[None], (N_ITEM, 16, 128))


def col_pass(kern, parts, weight):
    return call(
        col_body, (*kern, parts, weight), VMEM((N_ITEM, 16, 128), F32),
        [VMEM((8, ITEM_DEV), F32), VMEM((LIST_DEV, 128), F32)], "columns", 2 * LIST_DEV * ITEM_DEV,
    )


def row_body(*refs):
    *kern_refs, cols_ref, cap_ref, out_ref, scale_ref, total_ref = refs
    scale = cap_ref[...] / cols_ref[...].sum(0)
    for k in range(16):
        scale_ref[128 * k : 128 * (k + 1), :] = jnp.broadcast_to(scale[k : k + 1, :], (128, 128)).T

    for h, ref in enumerate(kern_refs):

        def step(m, total):
            at = pl.ds(pl.multiple_of(m * 64, 64), 64)
            by = scale_ref[at, :].reshape(8, 8, 128)
            block = ref[at, :].reshape(8, 8, QUART)
            total = list(total)
            for j in range(8):
                for k in range(8):
                    total[k] = total[k] + block[j, :, 128 * k : 128 * (k + 1)] * by[j]
            return tuple(total)

        total = lax.fori_loop(0, LIST_DEV // 64, step, (jnp.zeros((8, 128), F32),) * 8)
        for k in range(8):
            first = QUART * h + 128 * k
            total_ref[:, first : first + 128] = total[k].sum(0, keepdims=True)

    put_rows(total_ref[...], out_ref)


def row_pass(kern, cols, cap):
    return call(
        row_body, (*kern, cols, cap), VMEM((N_LIST, 16, 256), BF16),
        [VMEM((LIST_DEV, 128), F32), VMEM((1, ITEM_DEV), F32)], "rows", 2 * LIST_DEV * ITEM_DEV,
    )


TILE_L = 256


def last_body(other, *refs):
    *kern_refs, item_one_ref, item_two_ref, parts_ref, weight_ref, out_ref, scale_ref, partial_ref = refs
    core, _, _, _ = place()
    base = (1 - core if other else core) * 1024
    spread_rows(parts_ref, weight_ref, scale_ref)

    @pl.loop(0, 1024 // TILE_L)
    def _(m):
        at = pl.ds(pl.multiple_of(base + m * TILE_L, TILE_L), TILE_L)
        to = pl.ds(pl.multiple_of(m * TILE_L, TILE_L), TILE_L)
        total = jnp.zeros((TILE_L // 8, 8, 128), F32)
        mixed = jnp.zeros((TILE_L, E), F32)
        for h, ref in enumerate(kern_refs):
            item_ref = (item_one_ref, item_two_ref)[h // 2]
            for n in range(QUART // 256):
                lanes = slice(256 * n, 256 * (n + 1))
                first = QUART * (h % 2) + 256 * n
                by = scale_ref[:, QUART * h + 256 * n : QUART * h + 256 * (n + 1)]
                block = ref[at, lanes].reshape(TILE_L // 8, 8, 256) * by[None]
                total = total + block[:, :, :128] + block[:, :, 128:]
                block = block.reshape(TILE_L, 256).astype(BF16)
                mixed = mixed + jnp.dot(block, item_ref[first : first + 256, :], preferred_element_type=F32)
        partial_ref[to, :] = total.reshape(TILE_L, 128)
        out_ref[to, :] = mixed.astype(BF16)

    cols = lanes_of(partial_ref[...])
    high = cols.astype(BF16).astype(F32)
    both = jnp.concatenate([high, cols - high], 1)
    for q in range(4):
        block = jnp.concatenate([both[2 * q : 2 * q + 2], jnp.zeros((14, E), F32)], 0)
        out_ref[1024 + 16 * q : 1024 + 16 * (q + 1), :] = block.astype(BF16)


def last_pass(other, kern, item, parts, weight):
    return call(
        functools.partial(last_body, other), (*kern, *item, parts, weight), VMEM((1088, E), BF16),
        [VMEM((8, ITEM_DEV), F32), VMEM((1024, 128), F32)], "totals", LIST_DEV * ITEM_DEV * E, 4,
    )


AWAY = (0, 1, 3, 2)


def fold_body(stay_ref, came_ref, *out_refs):
    _, z, _, _ = place()
    for d, out_ref in zip(AWAY, out_refs):
        q = (z + d) % 4
        rows = pl.ds(pl.multiple_of(q * 256, 256), 256)
        tail = pl.ds(pl.multiple_of(1024 + q * 16, 16), 16)
        out_ref[:256, :] = (stay_ref[rows, :].astype(F32) + came_ref[rows, :].astype(F32)).astype(out_ref.dtype)
        cols = stay_ref[tail, :].astype(F32) + came_ref[tail, :].astype(F32)
        cols = cols[:, :128] + cols[:, 128:]
        high = cols.astype(BF16).astype(F32)
        out_ref[256:, :] = jnp.concatenate([high, cols - high], 1).astype(out_ref.dtype)


def fold(stay, came):
    out = (VMEM((272, E), F32),) + (VMEM((272, E), BF16),) * 3
    return call(fold_body, (stay, came), out, [], "fold")


def finish_body(mine_ref, a_ref, b_ref, c_ref, list_ref, out_ref):
    core, z, _, _ = place()
    first = pl.multiple_of(core * 1024 + z * 256, 256)
    totals = mine_ref[...] + a_ref[...].astype(F32) + b_ref[...].astype(F32) + c_ref[...].astype(F32)
    cols = totals[256:, :128] + totals[256:, 128:]
    for t in range(2):
        col = jnp.broadcast_to(cols[t : t + 1], (128, 128)).T
        col = jnp.concatenate([col, col], 1)
        own = list_ref[pl.ds(first + 128 * t, 128), :].astype(F32)
        mixed = 0.1 * own + totals[128 * t : 128 * (t + 1)] / col
        out_ref[128 * t : 128 * (t + 1), :] = unit(mixed, 1).astype(BF16)


def finish(pieces, lists):
    return call(finish_body, (*pieces, lists), VMEM((256, E), BF16), [], "finish")


FROM = (0, -1, 1, 2)


def lay_body(*refs):
    blocks, out_ref, sems = refs[:8], refs[8], refs[9]
    core, z, _, _ = place()
    copies = []
    for i, ref in enumerate(blocks):
        half = core if i < 4 else 1 - core
        row = pl.multiple_of(half * 1024 + (z + FROM[i % 4] + 4) % 4 * 256, 256)
        copies.append(pltpu.make_async_copy(ref, out_ref.at[pl.ds(row, 256), :], sems.at[i]))
    for copy in copies:
        copy.start()
    for copy in copies:
        copy.wait()


def lay(blocks):
    return pl.pallas_call(
        lay_body,
        out_shape=jax.ShapeDtypeStruct((LIST_DEV, E), BF16),
        in_specs=whole(8),
        out_specs=pl.BlockSpec(memory_space=pl.ANY),
        scratch_shapes=[pltpu.SemaphoreType.DMA((8,))],
        compiler_params=pltpu.CompilerParams(vmem_limit_bytes=12 << 20),
        name="lay",
    )(*blocks)


def local(items, item_weight, list_capacity, centroids):
    feat = items.T
    weight = item_weight.reshape(16, 256)
    cap = list_capacity.reshape(16, 128)

    one = jnp.concatenate(gather_small(feat[:, :HALF], "x"), 0)
    two = jnp.concatenate(gather_small(feat[:, HALF:], "y"), 0)
    one = gather_large(one, "y")
    two = gather_large(two, "x")

    lists, weight, cap = prep(centroids, weight, cap)
    *kern_one, item_one, before = gen(False, lists, one)
    *kern_two, item_two, parts = gen(True, lists, two, (before,))
    kern, item = kern_one + kern_two, (item_one, item_two)

    for step in range(ITERS - 1):
        parts = lax.all_to_all(parts, "list", 0, 0)
        cols = lax.all_to_all(col_pass(kern, parts, weight), "item", 0, 0)
        parts = row_pass(kern, cols, cap)
    parts = lax.all_to_all(parts, "list", 0, 0)

    came = swap_core(last_pass(True, kern, item, parts, weight))
    stay = last_pass(False, kern, item, parts, weight)
    pieces = fold(stay, came)
    pieces = pieces[:1] + tuple(shift("z", d)(p) for d, p in zip(AWAY[1:], pieces[1:]))
    done = finish(pieces, lists)
    done = [done] + [shift("z", d)(done) for d in AWAY[1:]]
    return lay(done + [swap_core(d) for d in done])


def solution(mesh):
    placed = (P("item", "list"), P("item"), P("list"), P("list", None))
    return jax.shard_map(
        local, mesh=mesh, in_specs=placed, out_specs=P("list", None), check_vma=False
    )
```

time: 568 us -> 139 us (0.24); the launches traced: 559 us -> 139 us
  blocking collectives: 251 us -> 56.5 us
  matrix products: 184 us -> 0 us
  waiting for transfers between devices: 103 us -> 10.8 us
  starting transfers between devices: 0.04 us -> 34.4 us
  Pallas kernels: 0 us -> 33 us
  between operations: 13.8 us -> 0.34 us
  other arithmetic: 7.2 us -> 0.04 us
    psum x6 -> x0, blocking collectives: 251 us -> none  [the longest x3 171 us: local(): lax.psum(jnp.dot(tile, col_scale, precision=lax.Precision.HIGHEST), 'list')]
    dot_general x8 -> x0, matrix products: 184 us -> none  [the longest x3 95.1 us: local(): jnp.dot(tile, col_scale, precision=lax.Precision.HIGHEST)]
    all_to_all x0 -> x5, blocking collectives: none -> 56.5 us  [the longest x3 31.7 us: local(): parts = lax.all_to_all(parts, 'list', 0, 0)]
    psum x1 -> x0, waiting for transfers between devices: 54.2 us -> none  [local(): totals = lax.psum(term.astype(jnp.bfloat16), 'item').astype(jnp.float32)]
    all_gather x1 -> x0, waiting for transfers between devices: 47.8 us -> none  [local(): whole = lax.all_gather(items, 'list', axis=1, tiled=True)]
    ppermute x0 -> x25, starting transfers between devices: none -> 34.4 us  [the longest x20 24.7 us: shift(): lax.ppermute(block, axis, [(i, along(i)) for i in range(size)])]
    pallas_call x0 -> x12, Pallas kernels: none -> 33 us  [the longest x11 32 us: call(): pl.pallas_call(body, out_shape=out, in_specs=whole(len(args)), out_specs=...]
    ppermute x0 -> x25, waiting for transfers between devices: none -> 10.8 us  [the longest x20 9.86 us: shift(): lax.ppermute(block, axis, [(i, along(i)) for i in range(size)])]
  transfers between devices with their start and end apart: 2 -> 25, of which waited for: 2 -> 10; matrix products, arithmetic and copies ran while one was open for 0% -> 1% of each run, Pallas kernels for 0% -> 6%
where the time goes in v2:
time: 139 us
  blocking collectives  56.5 us (41%)
  starting transfers between devices  34.4 us (25%)
  Pallas kernels  33 us (24%)
  waiting for transfers between devices  10.8 us (8%)
  local copies, waits for them, and re-layouts  3.56 us (3%)
    pallas_call x11, Pallas kernels, call(): pl.pallas_call(body, out_shape=out, in_specs=whole(len(args)), out_specs=...  32 us
    all_to_all x3, blocking collectives, local(): parts = lax.all_to_all(parts, 'list', 0, 0)  31.7 us
    all_to_all x2, blocking collectives, local(): cols = lax.all_to_all(col_pass(kern, parts, weight), 'item', 0, 0)  24.8 us
    ppermute x20, starting transfers between devices, shift(): lax.ppermute(block, axis, [(i, along(i)) for i in range(size)])  24.7 us
    ppermute x20, waiting for transfers between devices, shift(): lax.ppermute(block, axis, [(i, along(i)) for i in range(size)])  9.86 us
    ppermute x5, starting transfers between devices, swap_core(): return lax.ppermute(block, 'item', [(i, i ^ 1) for i in range(N_ITEM)])  9.72 us
  transfers between devices with their start and end apart: 25, of which 10 were waited for; matrix products, arithmetic and copies ran while one was open for 1% of the time, Pallas kernels for 6%

profile of v2, /device:TPU:1, one launch (start us, length us, event | category | flops | bytes accessed | tf_op | source)
XLA Modules:
  0.0 138.7 jit_solution(14346272484364964618)
XLA Ops:
  0.0 0.9 fusion
  0.9 3.7 %collective-permute-start.2 = (bf16[16,2048]{1,0:T(8,128)(2,1)S(1)}, bf16[16,2048]{1,0:T(8,128)(2,1)S(1)}, u32[]{:S(2)}, u32[]{:S(2)}) collective-permute-start(bf16[16,2048]{1,0:T(8,128)(2,1)S(1)} %get-tuple-element.36), channel_id=1, source_target_pairs={{0,2},{1,3},{2,0},{3,1},{4,6},{5,7},{6,4},{7,5},{8,10},{9,11},{10,... | collective-permute-start | bytes 196616 | tf_op jit(solution)/shard_map/ppermute | solution.py:65
  4.5 0.9 collective-permute-start.1
  5.4 0.6 collective-permute-start
  6.0 2.9 %collective-permute-start.9 = (bf16[16,2048]{1,0:T(8,128)(2,1)S(1)}, bf16[16,2048]{1,0:T(8,128)(2,1)S(1)}, u32[]{:S(2)}, u32[]{:S(2)}) collective-permute-start(bf16[16,2048]{1,0:T(8,128)(2,1)S(1)} %get-tuple-element.35), channel_id=1, source_target_pairs={{0,8},{1,9},{2,10},{3,11},{4,12},{5,13},{6,14},{7,15},{8,0},{9,1},... | collective-permute-start | bytes 196616 | tf_op jit(solution)/shard_map/ppermute | solution.py:65
  8.9 0.8 collective-permute-start.8
  9.7 0.7 collective-permute-start.7
  10.4 2.1 %collective-permute-start.4 = (bf16[64,2048]{1,0:T(8,128)(2,1)S(1)}, bf16[64,2048]{1,0:T(8,128)(2,1)S(1)}, u32[]{:S(2)}, u32[]{:S(2)}) collective-permute-start(bf16[64,2048]{1,0:T(8,128)(2,1)S(1)} %pad_maximum_fusion.own_ref), channel_id=1, source_target_pairs={{0,12},{1,13},{2,14},{3,15},{4,0},{5,1},{6,2},{7,3},{8,4},{9,5},{1... | collective-permute-start | bytes 786440 | tf_op jit(solution)/shard_map/ppermute | solution.py:65
  12.6 1.5 %collective-permute-done.7 = bf16[16,2048]{1,0:T(8,128)(2,1)S(1)} collective-permute-done((bf16[16,2048]{1,0:T(8,128)(2,1)S(1)}, bf16[16,2048]{1,0:T(8,128)(2,1)S(1)}, u32[]{:S(2)}, u32[]{:S(2)}) %collective-permute-start.7) | collective-permute-done | bytes 65568 | tf_op jit(solution)/shard_map/ppermute | solution.py:65
  14.0 2.1 %collective-permute-start.11 = (bf16[64,2048]{1,0:T(8,128)(2,1)S(1)}, bf16[64,2048]{1,0:T(8,128)(2,1)S(1)}, u32[]{:S(2)}, u32[]{:S(2)}) collective-permute-start(bf16[64,2048]{1,0:T(8,128)(2,1)S(1)} %pad_maximum_fusion.1.own_ref), channel_id=1, source_target_pairs={{0,3},{1,0},{2,1},{3,2},{4,7},{5,4},{6,5},{7,6},{8,11},{9,8},{10,9... | collective-permute-start | bytes 786440 | tf_op jit(solution)/shard_map/ppermute | solution.py:65
  16.2 1.2 collective-permute-done.4.right_ref
  17.4 1.7 %collective-permute-start.6 = (bf16[32,2048]{1,0:T(8,128)(2,1)S(1)}, bf16[32,2048]{1,0:T(8,128)(2,1)S(1)}, u32[]{:S(2)}, u32[]{:S(2)}) collective-permute-start(bf16[32,2048]{1,0:T(8,128)(2,1)S(1)} %slice.26), channel_id=1, source_target_pairs={{0,12},{1,13},{2,14},{3,15},{4,0},{5,1},{6,2},{7,3},{8,4},{9,5},{1... | collective-permute-start | bytes 393224 | tf_op jit(solution)/shard_map/ppermute | solution.py:65
  19.2 0.2 collective-permute-done.3.left_ref
  19.5 0.7 reshape.6.weight_ref
  20.2 1.2 copy-done
  21.4 0.7 copy-done.1
  22.1 0.5 lists.1
  22.6 2.5 %collective-permute-start.13 = (bf16[32,2048]{1,0:T(8,128)(2,1)S(1)}, bf16[32,2048]{1,0:T(8,128)(2,1)S(1)}, u32[]{:S(2)}, u32[]{:S(2)}) collective-permute-start(bf16[32,2048]{1,0:T(8,128)(2,1)S(1)} %slice.29), channel_id=1, source_target_pairs={{0,3},{1,0},{2,1},{3,2},{4,7},{5,4},{6,5},{7,6},{8,11},{9,8},{10,9... | collective-permute-start | bytes 393224 | tf_op jit(solution)/shard_map/ppermute | solution.py:65
  25.3 4.3 %generate.2 = (f32[2048,1024]{1,0:T(8,128)S(1)}, f32[2048,1024]{1,0:T(8,128)S(1)}, bf16[2048,256]{1,0:T(8,128)(2,1)S(1)}, f32[1,2048]{1,0:T(1,128)S(1)}) custom-call(bf16[2048,256]{1,0:T(8,128)(2,1)S(1)} %get-tuple-element.20.list_ref, bf16[64,2048]{1,0:T(8,128)(2,1)S(1)} %pad_maximum_fusion.own_ref, bf16[64,2048]{1,0:T(8,128)(2,1)S(1)} %collective-permute-done.3.left_ref, ...), custom_call_target="tpu_custom_call" | custom-call | flops 2147483648 | bytes 1048576 | tf_op jit(solution)/shard_map/generate/pallas_call | solution.py:33
  29.6 0.7 collective-permute-done.12.low_ref
  30.3 4.4 %generate.3 = (f32[2048,1024]{1,0:T(8,128)S(1)}, f32[2048,1024]{1,0:T(8,128)S(1)}, bf16[2048,256]{1,0:T(8,128)(2,1)S(1)}, bf16[16,16,256]{2,1,0:T(8,128)(2,1)S(1)}) custom-call(bf16[2048,256]{1,0:T(8,128)(2,1)S(1)} %get-tuple-element.20.list_ref, bf16[64,2048]{1,0:T(8,128)(2,1)S(1)} %pad_maximum_fusion.1.own_ref, ...), custom_call_target="tpu_custom_call" | custom-call | flops 2147483648 | bytes 1048576 | tf_op jit(solution)/shard_map/generate/pallas_call | solution.py:33
  34.7 12.4 %all_to_all.25.refs_4_ = bf16[16,16,256]{2,1,0:T(8,128)(2,1)S(1)} all-to-all(bf16[16,16,256]{2,1,0:T(8,128)(2,1)S(1)} %get-tuple-element.28), channel_id=1, replica_groups=mesh['item'=8,'list'=16] {'list'}, dimensions={0} | all-to-all | bytes 262144 | tf_op jit(solution)/shard_map/all_to_all | solution.py:353
  47.0 3.8 %columns.2 = f32[8,16,128]{2,1,0:T(8,128)S(1)} custom-call(f32[2048,1024]{1,0:T(8,128)S(1)} %get-tuple-element.21.refs_0_, f32[2048,1024]{1,0:T(8,128)S(1)} %get-tuple-element.22.refs_1_, f32[2048,1024]{1,0:T(8,128)S(1)} %get-tuple-element.24.refs_2_, f32[2048,1024]{1,0:T(8,128)S(1)} %get-tuple-element.25.refs_3_, ...), custom_call_target="tpu_custom_call" | custom-call | flops 16777216 | bytes 1048576 | tf_op jit(solution)/shard_map/columns/pallas_call | solution.py:33
  50.8 15.4 %all_to_all.26.refs_4_ = f32[8,16,128]{2,1,0:T(8,128)S(1)} all-to-all(f32[8,16,128]{2,1,0:T(8,128)S(1)} %columns.2), channel_id=1, replica_groups=mesh['item'=8,'list'=16] {'item'}, dimensions={0} | all-to-all | bytes 131072 | tf_op jit(solution)/shard_map/all_to_all | solution.py:354
  66.2 3.3 %rows.2 = bf16[16,16,256]{2,1,0:T(8,128)(2,1)S(1)} custom-call(f32[2048,1024]{1,0:T(8,128)S(1)} %get-tuple-element.21.refs_0_, f32[2048,1024]{1,0:T(8,128)S(1)} %get-tuple-element.22.refs_1_, f32[2048,1024]{1,0:T(8,128)S(1)} %get-tuple-element.24.refs_2_, f32[2048,1024]{1,0:T(8,128)S(1)} %get-tuple-element.25.refs_3_, f32[8,16,128]{2,1,0:T(8,128)S(1)} %all_to_all.26.refs_4_, ...), custom_call_target="tpu_custom_call" | custom-call | flops 16777216 | bytes 1048576 | tf_op jit(solution)/shard_map/rows/pallas_call | solution.py:33
  69.5 9.7 %all_to_all.27.refs_4_ = bf16[16,16,256]{2,1,0:T(8,128)(2,1)S(1)} all-to-all(bf16[16,16,256]{2,1,0:T(8,128)(2,1)S(1)} %rows.2), channel_id=1, replica_groups=mesh['item'=8,'list'=16] {'list'}, dimensions={0} | all-to-all | bytes 262144 | tf_op jit(solution)/shard_map/all_to_all | solution.py:353
  79.2 3.8 %columns.3 = f32[8,16,128]{2,1,0:T(8,128)S(1)} custom-call(f32[2048,1024]{1,0:T(8,128)S(1)} %get-tuple-element.21.refs_0_, f32[2048,1024]{1,0:T(8,128)S(1)} %get-tuple-element.22.refs_1_, f32[2048,1024]{1,0:T(8,128)S(1)} %get-tuple-element.24.refs_2_, f32[2048,1024]{1,0:T(8,128)S(1)} %get-tuple-element.25.refs_3_, ...), custom_call_target="tpu_custom_call" | custom-call | flops 16777216 | bytes 1048576 | tf_op jit(solution)/shard_map/columns/pallas_call | solution.py:33
  83.0 9.4 %all_to_all.28.refs_4_ = f32[8,16,128]{2,1,0:T(8,128)S(1)} all-to-all(f32[8,16,128]{2,1,0:T(8,128)S(1)} %columns.3), channel_id=1, replica_groups=mesh['item'=8,'list'=16] {'item'}, dimensions={0} | all-to-all | bytes 131072 | tf_op jit(solution)/shard_map/all_to_all | solution.py:354
  92.4 3.3 %rows.3 = bf16[16,16,256]{2,1,0:T(8,128)(2,1)S(1)} custom-call(f32[2048,1024]{1,0:T(8,128)S(1)} %get-tuple-element.21.refs_0_, f32[2048,1024]{1,0:T(8,128)S(1)} %get-tuple-element.22.refs_1_, f32[2048,1024]{1,0:T(8,128)S(1)} %get-tuple-element.24.refs_2_, f32[2048,1024]{1,0:T(8,128)S(1)} %get-tuple-element.25.refs_3_, f32[8,16,128]{2,1,0:T(8,128)S(1)} %all_to_all.28.refs_4_, ...), custom_call_target="tpu_custom_call" | custom-call | flops 16777216 | bytes 1048576 | tf_op jit(solution)/shard_map/rows/pallas_call | solution.py:33
  95.7 9.7 %all_to_all.29.refs_6_ = bf16[16,16,256]{2,1,0:T(8,128)(2,1)S(1)} all-to-all(bf16[16,16,256]{2,1,0:T(8,128)(2,1)S(1)} %rows.3), channel_id=1, replica_groups=mesh['item'=8,'list'=16] {'list'}, dimensions={0} | all-to-all | bytes 262144 | tf_op jit(solution)/shard_map/all_to_all | solution.py:356
  105.4 4.1 %totals.3 = bf16[1088,256]{1,0:T(8,128)(2,1)S(1)} custom-call(f32[2048,1024]{1,0:T(8,128)S(1)} %get-tuple-element.21.refs_0_, f32[2048,1024]{1,0:T(8,128)S(1)} %get-tuple-element.22.refs_1_, f32[2048,1024]{1,0:T(8,128)S(1)} %get-tuple-element.24.refs_2_, f32[2048,1024]{1,0:T(8,128)S(1)} %get-tuple-element.25.refs_3_, ...), custom_call_target="tpu_custom_call" | custom-call | flops 2147483648 | bytes 1048576 | tf_op jit(solution)/shard_map/totals/pallas_call | solution.py:33
  109.5 2.2 %collective-permute-start.14 = (bf16[1088,256]{1,0:T(8,128)(2,1)S(1)}, bf16[1088,256]{1,0:T(8,128)(2,1)S(1)}, u32[]{:S(2)}, u32[]{:S(2)}) collective-permute-start(bf16[1088,256]{1,0:T(8,128)(2,1)S(1)} %totals.3), channel_id=1, source_target_pairs={{0,16},{16,0},{32,48},{48,32},{64,80},{80,64},{96,112},{112,96},{1... | collective-permute-start | bytes 1671176 | tf_op jit(solution)/shard_map/ppermute | solution.py:69
  111.8 4.1 %totals.2.stay_ref = bf16[1088,256]{1,0:T(8,128)(2,1)S(1)} custom-call(f32[2048,1024]{1,0:T(8,128)S(1)} %get-tuple-element.21.refs_0_, f32[2048,1024]{1,0:T(8,128)S(1)} %get-tuple-element.22.refs_1_, f32[2048,1024]{1,0:T(8,128)S(1)} %get-tuple-element.24.refs_2_, f32[2048,1024]{1,0:T(8,128)S(1)} %get-tuple-element.25.refs_3_, ...), custom_call_target="tpu_custom_call" | custom-call | flops 2147483648 | bytes 1048576 | tf_op jit(solution)/shard_map/totals/pallas_call | solution.py:33
  116.1 0.4 collective-permute-start.15
  116.4 2.4 %collective-permute-start.16 = (bf16[272,256]{1,0:T(8,128)(2,1)S(1)}, bf16[272,256]{1,0:T(8,128)(2,1)S(1)}, u32[]{:S(2)}, u32[]{:S(2)}) collective-permute-start(bf16[272,256]{1,0:T(8,128)(2,1)S(1)} %get-tuple-element.33), channel_id=1, source_target_pairs={{0,96},{16,112},{32,0},{48,16},{64,32},{80,48},{96,64},{112,80},{1... | collective-permute-start | bytes 417800 | tf_op jit(solution)/shard_map/ppermute | solution.py:65
  118.8 3.8 %collective-permute-done.15.a_ref = bf16[272,256]{1,0:T(8,128)(2,1)S(1)} collective-permute-done((bf16[272,256]{1,0:T(8,128)(2,1)S(1)}, bf16[272,256]{1,0:T(8,128)(2,1)S(1)}, u32[]{:S(2)}, u32[]{:S(2)}) %collective-permute-start.15) | collective-permute-done | bytes 139296 | tf_op jit(solution)/shard_map/ppermute | solution.py:65
  122.6 1.8 %collective-permute-done.16.b_ref = bf16[272,256]{1,0:T(8,128)(2,1)S(1)} collective-permute-done((bf16[272,256]{1,0:T(8,128)(2,1)S(1)}, bf16[272,256]{1,0:T(8,128)(2,1)S(1)}, u32[]{:S(2)}, u32[]{:S(2)}) %collective-permute-start.16) | collective-permute-done | bytes 139296 | tf_op jit(solution)/shard_map/ppermute | solution.py:65
  124.4 0.5 collective-permute-done.17.c_ref
  125.0 0.2 finish.1.refs_0_
  125.2 1.3 collective-permute-start.20
  126.5 2.4 %collective-permute-start.19 = (bf16[256,256]{1,0:T(8,128)(2,1)S(1)}, bf16[256,256]{1,0:T(8,128)(2,1)S(1)}, u32[]{:S(2)}, u32[]{:S(2)}) collective-permute-start(bf16[256,256]{1,0:T(8,128)(2,1)S(1)} %finish.1.refs_0_), channel_id=1, source_target_pairs={{0,96},{16,112},{32,0},{48,16},{64,32},{80,48},{96,64},{112,80},{1... | collective-permute-start | bytes 393224 | tf_op jit(solution)/shard_map/ppermute | solution.py:65
  128.9 1.6 %collective-permute-start.21 = (bf16[256,256]{1,0:T(8,128)(2,1)S(1)}, bf16[256,256]{1,0:T(8,128)(2,1)S(1)}, u32[]{:S(2)}, u32[]{:S(2)}) collective-permute-start(bf16[256,256]{1,0:T(8,128)(2,1)S(1)} %finish.1.refs_0_), channel_id=1, source_target_pairs={{0,16},{16,0},{32,48},{48,32},{64,80},{80,64},{96,112},{112,96},{1... | collective-permute-start | bytes 393224 | tf_op jit(solution)/shard_map/ppermute | solution.py:69
  130.6 3.6 %collective-permute-start.24 = (bf16[256,256]{1,0:T(8,128)(2,1)S(1)}, bf16[256,256]{1,0:T(8,128)(2,1)S(1)}, u32[]{:S(2)}, u32[]{:S(2)}) collective-permute-start(bf16[256,256]{1,0:T(8,128)(2,1)S(1)} %collective-permute-done.20.refs_3_), channel_id=1, source_target_pairs={{0,16},{16,0},{32,48},{48,32},{64,80},{80,64},{96,112},{112,96},{1... | collective-permute-start | bytes 393224 | tf_op jit(solution)/shard_map/ppermute | solution.py:69
  134.2 1.9 %collective-permute-start.23 = (bf16[256,256]{1,0:T(8,128)(2,1)S(1)}, bf16[256,256]{1,0:T(8,128)(2,1)S(1)}, u32[]{:S(2)}, u32[]{:S(2)}) collective-permute-start(bf16[256,256]{1,0:T(8,128)(2,1)S(1)} %collective-permute-done.19.refs_2_), channel_id=1, source_target_pairs={{0,16},{16,0},{32,48},{48,32},{64,80},{80,64},{96,112},{112,96},{1... | collective-permute-start | bytes 393224 | tf_op jit(solution)/shard_map/ppermute | solution.py:69
  136.1 0.4 collective-permute-start.22
  136.5 0.6 collective-permute-done.23.refs_6_
  137.1 0.4 collective-permute-done.22.refs_5_
  137.5 1.0 lay.1
  (31 shorter events, 0.5 us)
Async XLA Ops:
  0.9 8.8 %collective-permute-start.2 = (bf16[16,2048]{1,0:T(8,128)(2,1)S(1)}, bf16[16,2048]{1,0:T(8,128)(2,1)S(1)}, u32[]{:S(2)}, u32[]{:S(2)}) collective-permute-start(bf16[16,2048]{1,0:T(8,128)(2,1)S(1)} %get-tuple-element.36), channel_id=1, source_target_pairs={{0,2},{1,3},{2,0},{3,1},{4,6},{5,7},{6,4},{7,5},{8,10},{9,11},{10,... | collective-permute-start | bytes 196616 | tf_op jit(solution)/shard_map/ppermute | solution.py:65
  4.5 5.9 %collective-permute-start.1 = (bf16[16,2048]{1,0:T(8,128)(2,1)S(1)}, bf16[16,2048]{1,0:T(8,128)(2,1)S(1)}, u32[]{:S(2)}, u32[]{:S(2)}) collective-permute-start(bf16[16,2048]{1,0:T(8,128)(2,1)S(1)} %get-tuple-element.36), channel_id=1, source_target_pairs={{0,3},{1,0},{2,1},{3,2},{4,7},{5,4},{6,5},{7,6},{8,11},{9,8},{10,9... | collective-permute-start | bytes 196616 | tf_op jit(solution)/shard_map/ppermute | solution.py:65
  5.4 5.0 %collective-permute-start = (bf16[16,2048]{1,0:T(8,128)(2,1)S(1)}, bf16[16,2048]{1,0:T(8,128)(2,1)S(1)}, u32[]{:S(2)}, u32[]{:S(2)}) collective-permute-start(bf16[16,2048]{1,0:T(8,128)(2,1)S(1)} %get-tuple-element.36), channel_id=1, source_target_pairs={{0,1},{1,2},{2,3},{3,0},{4,5},{5,6},{6,7},{7,4},{8,9},{9,10},{10,1... | collective-permute-start | bytes 196616 | tf_op jit(solution)/shard_map/ppermute | solution.py:65
  6.0 6.6 %collective-permute-start.9 = (bf16[16,2048]{1,0:T(8,128)(2,1)S(1)}, bf16[16,2048]{1,0:T(8,128)(2,1)S(1)}, u32[]{:S(2)}, u32[]{:S(2)}) collective-permute-start(bf16[16,2048]{1,0:T(8,128)(2,1)S(1)} %get-tuple-element.35), channel_id=1, source_target_pairs={{0,8},{1,9},{2,10},{3,11},{4,12},{5,13},{6,14},{7,15},{8,0},{9,1},... | collective-permute-start | bytes 196616 | tf_op jit(solution)/shard_map/ppermute | solution.py:65
  8.9 3.6 %collective-permute-start.8 = (bf16[16,2048]{1,0:T(8,128)(2,1)S(1)}, bf16[16,2048]{1,0:T(8,128)(2,1)S(1)}, u32[]{:S(2)}, u32[]{:S(2)}) collective-permute-start(bf16[16,2048]{1,0:T(8,128)(2,1)S(1)} %get-tuple-element.35), channel_id=1, source_target_pairs={{0,12},{1,13},{2,14},{3,15},{4,0},{5,1},{6,2},{7,3},{8,4},{9,5},{1... | collective-permute-start | bytes 196616 | tf_op jit(solution)/shard_map/ppermute | solution.py:65
  9.7 4.3 %collective-permute-start.7 = (bf16[16,2048]{1,0:T(8,128)(2,1)S(1)}, bf16[16,2048]{1,0:T(8,128)(2,1)S(1)}, u32[]{:S(2)}, u32[]{:S(2)}) collective-permute-start(bf16[16,2048]{1,0:T(8,128)(2,1)S(1)} %get-tuple-element.35), channel_id=1, source_target_pairs={{0,4},{1,5},{2,6},{3,7},{4,8},{5,9},{6,10},{7,11},{8,12},{9,13},{1... | collective-permute-start | bytes 196616 | tf_op jit(solution)/shard_map/ppermute | solution.py:65
  10.4 7.0 %collective-permute-start.4 = (bf16[64,2048]{1,0:T(8,128)(2,1)S(1)}, bf16[64,2048]{1,0:T(8,128)(2,1)S(1)}, u32[]{:S(2)}, u32[]{:S(2)}) collective-permute-start(bf16[64,2048]{1,0:T(8,128)(2,1)S(1)} %pad_maximum_fusion.own_ref), channel_id=1, source_target_pairs={{0,12},{1,13},{2,14},{3,15},{4,0},{5,1},{6,2},{7,3},{8,4},{9,5},{1... | collective-permute-start | bytes 786440 | tf_op jit(solution)/shard_map/ppermute | solution.py:65
  12.6 6.8 %collective-permute-start.3 = (bf16[64,2048]{1,0:T(8,128)(2,1)S(1)}, bf16[64,2048]{1,0:T(8,128)(2,1)S(1)}, u32[]{:S(2)}, u32[]{:S(2)}) collective-permute-start(bf16[64,2048]{1,0:T(8,128)(2,1)S(1)} %pad_maximum_fusion.own_ref), channel_id=1, source_target_pairs={{0,4},{1,5},{2,6},{3,7},{4,8},{5,9},{6,10},{7,11},{8,12},{9,13},{1... | collective-permute-start | bytes 786440 | tf_op jit(solution)/shard_map/ppermute | solution.py:65
  14.0 8.5 %collective-permute-start.11 = (bf16[64,2048]{1,0:T(8,128)(2,1)S(1)}, bf16[64,2048]{1,0:T(8,128)(2,1)S(1)}, u32[]{:S(2)}, u32[]{:S(2)}) collective-permute-start(bf16[64,2048]{1,0:T(8,128)(2,1)S(1)} %pad_maximum_fusion.1.own_ref), channel_id=1, source_target_pairs={{0,3},{1,0},{2,1},{3,2},{4,7},{5,4},{6,5},{7,6},{8,11},{9,8},{10,9... | collective-permute-start | bytes 786440 | tf_op jit(solution)/shard_map/ppermute | solution.py:65
  16.2 9.0 %collective-permute-start.10 = (bf16[64,2048]{1,0:T(8,128)(2,1)S(1)}, bf16[64,2048]{1,0:T(8,128)(2,1)S(1)}, u32[]{:S(2)}, u32[]{:S(2)}) collective-permute-start(bf16[64,2048]{1,0:T(8,128)(2,1)S(1)} %pad_maximum_fusion.1.own_ref), channel_id=1, source_target_pairs={{0,1},{1,2},{2,3},{3,0},{4,5},{5,6},{6,7},{7,4},{8,9},{9,10},{10,1... | collective-permute-start | bytes 786440 | tf_op jit(solution)/shard_map/ppermute | solution.py:65
  17.4 7.8 %collective-permute-start.6 = (bf16[32,2048]{1,0:T(8,128)(2,1)S(1)}, bf16[32,2048]{1,0:T(8,128)(2,1)S(1)}, u32[]{:S(2)}, u32[]{:S(2)}) collective-permute-start(bf16[32,2048]{1,0:T(8,128)(2,1)S(1)} %slice.26), channel_id=1, source_target_pairs={{0,12},{1,13},{2,14},{3,15},{4,0},{5,1},{6,2},{7,3},{8,4},{9,5},{1... | collective-permute-start | bytes 393224 | tf_op jit(solution)/shard_map/ppermute | solution.py:65
  19.4 5.9 %collective-permute-start.5 = (bf16[32,2048]{1,0:T(8,128)(2,1)S(1)}, bf16[32,2048]{1,0:T(8,128)(2,1)S(1)}, u32[]{:S(2)}, u32[]{:S(2)}) collective-permute-start(bf16[32,2048]{1,0:T(8,128)(2,1)S(1)} %slice.25), channel_id=1, source_target_pairs={{0,4},{1,5},{2,6},{3,7},{4,8},{5,9},{6,10},{7,11},{8,12},{9,13},{1... | collective-permute-start | bytes 393224 | tf_op jit(solution)/shard_map/ppermute | solution.py:65
  20.2 1.2 copy-start
  21.4 0.7 copy-start.1
  22.6 7.0 %collective-permute-start.13 = (bf16[32,2048]{1,0:T(8,128)(2,1)S(1)}, bf16[32,2048]{1,0:T(8,128)(2,1)S(1)}, u32[]{:S(2)}, u32[]{:S(2)}) collective-permute-start(bf16[32,2048]{1,0:T(8,128)(2,1)S(1)} %slice.29), channel_id=1, source_target_pairs={{0,3},{1,0},{2,1},{3,2},{4,7},{5,4},{6,5},{7,6},{8,11},{9,8},{10,9... | collective-permute-start | bytes 393224 | tf_op jit(solution)/shard_map/ppermute | solution.py:65
  25.2 5.1 %collective-permute-start.12 = (bf16[32,2048]{1,0:T(8,128)(2,1)S(1)}, bf16[32,2048]{1,0:T(8,128)(2,1)S(1)}, u32[]{:S(2)}, u32[]{:S(2)}) collective-permute-start(bf16[32,2048]{1,0:T(8,128)(2,1)S(1)} %slice.28), channel_id=1, source_target_pairs={{0,1},{1,2},{2,3},{3,0},{4,5},{5,6},{6,7},{7,4},{8,9},{9,10},{10,1... | collective-permute-start | bytes 393224 | tf_op jit(solution)/shard_map/ppermute | solution.py:65
  109.5 6.4 %collective-permute-start.14 = (bf16[1088,256]{1,0:T(8,128)(2,1)S(1)}, bf16[1088,256]{1,0:T(8,128)(2,1)S(1)}, u32[]{:S(2)}, u32[]{:S(2)}) collective-permute-start(bf16[1088,256]{1,0:T(8,128)(2,1)S(1)} %totals.3), channel_id=1, source_target_pairs={{0,16},{16,0},{32,48},{48,32},{64,80},{80,64},{96,112},{112,96},{1... | collective-permute-start | bytes 1671176 | tf_op jit(solution)/shard_map/ppermute | solution.py:69
  116.1 6.6 %collective-permute-start.15 = (bf16[272,256]{1,0:T(8,128)(2,1)S(1)}, bf16[272,256]{1,0:T(8,128)(2,1)S(1)}, u32[]{:S(2)}, u32[]{:S(2)}) collective-permute-start(bf16[272,256]{1,0:T(8,128)(2,1)S(1)} %get-tuple-element.32), channel_id=1, source_target_pairs={{0,32},{16,48},{32,64},{48,80},{64,96},{80,112},{96,0},{112,16},{1... | collective-permute-start | bytes 417800 | tf_op jit(solution)/shard_map/ppermute | solution.py:65
  116.4 8.0 %collective-permute-start.16 = (bf16[272,256]{1,0:T(8,128)(2,1)S(1)}, bf16[272,256]{1,0:T(8,128)(2,1)S(1)}, u32[]{:S(2)}, u32[]{:S(2)}) collective-permute-start(bf16[272,256]{1,0:T(8,128)(2,1)S(1)} %get-tuple-element.33), channel_id=1, source_target_pairs={{0,96},{16,112},{32,0},{48,16},{64,32},{80,48},{96,64},{112,80},{1... | collective-permute-start | bytes 417800 | tf_op jit(solution)/shard_map/ppermute | solution.py:65
  118.8 6.2 %collective-permute-start.17 = (bf16[272,256]{1,0:T(8,128)(2,1)S(1)}, bf16[272,256]{1,0:T(8,128)(2,1)S(1)}, u32[]{:S(2)}, u32[]{:S(2)}) collective-permute-start(bf16[272,256]{1,0:T(8,128)(2,1)S(1)} %get-tuple-element.34), channel_id=1, source_target_pairs={{0,64},{16,80},{32,96},{48,112},{64,0},{80,16},{96,32},{112,48},{1... | collective-permute-start | bytes 417800 | tf_op jit(solution)/shard_map/ppermute | solution.py:65
  125.2 5.4 %collective-permute-start.20 = (bf16[256,256]{1,0:T(8,128)(2,1)S(1)}, bf16[256,256]{1,0:T(8,128)(2,1)S(1)}, u32[]{:S(2)}, u32[]{:S(2)}) collective-permute-start(bf16[256,256]{1,0:T(8,128)(2,1)S(1)} %finish.1.refs_0_), channel_id=1, source_target_pairs={{0,64},{16,80},{32,96},{48,112},{64,0},{80,16},{96,32},{112,48},{1... | collective-permute-start | bytes 393224 | tf_op jit(solution)/shard_map/ppermute | solution.py:65
  126.5 7.7 %collective-permute-start.19 = (bf16[256,256]{1,0:T(8,128)(2,1)S(1)}, bf16[256,256]{1,0:T(8,128)(2,1)S(1)}, u32[]{:S(2)}, u32[]{:S(2)}) collective-permute-start(bf16[256,256]{1,0:T(8,128)(2,1)S(1)} %finish.1.refs_0_), channel_id=1, source_target_pairs={{0,96},{16,112},{32,0},{48,16},{64,32},{80,48},{96,64},{112,80},{1... | collective-permute-start | bytes 393224 | tf_op jit(solution)/shard_map/ppermute | solution.py:65
  128.9 7.2 %collective-permute-start.18 = (bf16[256,256]{1,0:T(8,128)(2,1)S(1)}, bf16[256,256]{1,0:T(8,128)(2,1)S(1)}, u32[]{:S(2)}, u32[]{:S(2)}) collective-permute-start(bf16[256,256]{1,0:T(8,128)(2,1)S(1)} %finish.1.refs_0_), channel_id=1, source_target_pairs={{0,32},{16,48},{32,64},{48,80},{64,96},{80,112},{96,0},{112,16},{1... | collective-permute-start | bytes 393224 | tf_op jit(solution)/shard_map/ppermute | solution.py:65
  128.9 7.6 %collective-permute-start.21 = (bf16[256,256]{1,0:T(8,128)(2,1)S(1)}, bf16[256,256]{1,0:T(8,128)(2,1)S(1)}, u32[]{:S(2)}, u32[]{:S(2)}) collective-permute-start(bf16[256,256]{1,0:T(8,128)(2,1)S(1)} %finish.1.refs_0_), channel_id=1, source_target_pairs={{0,16},{16,0},{32,48},{48,32},{64,80},{80,64},{96,112},{112,96},{1... | collective-permute-start | bytes 393224 | tf_op jit(solution)/shard_map/ppermute | solution.py:69
  130.6 5.9 %collective-permute-start.24 = (bf16[256,256]{1,0:T(8,128)(2,1)S(1)}, bf16[256,256]{1,0:T(8,128)(2,1)S(1)}, u32[]{:S(2)}, u32[]{:S(2)}) collective-permute-start(bf16[256,256]{1,0:T(8,128)(2,1)S(1)} %collective-permute-done.20.refs_3_), channel_id=1, source_target_pairs={{0,16},{16,0},{32,48},{48,32},{64,80},{80,64},{96,112},{112,96},{1... | collective-permute-start | bytes 393224 | tf_op jit(solution)/shard_map/ppermute | solution.py:69
  134.2 2.9 %collective-permute-start.23 = (bf16[256,256]{1,0:T(8,128)(2,1)S(1)}, bf16[256,256]{1,0:T(8,128)(2,1)S(1)}, u32[]{:S(2)}, u32[]{:S(2)}) collective-permute-start(bf16[256,256]{1,0:T(8,128)(2,1)S(1)} %collective-permute-done.19.refs_2_), channel_id=1, source_target_pairs={{0,16},{16,0},{32,48},{48,32},{64,80},{80,64},{96,112},{112,96},{1... | collective-permute-start | bytes 393224 | tf_op jit(solution)/shard_map/ppermute | solution.py:69
  136.1 1.4 collective-permute-start.22

commit v3 on v2

v3 whole, which is shorter than its diff:
```python
import functools
import math

import jax
import jax.numpy as jnp
from jax import lax
from jax.experimental import pallas as pl
from jax.experimental.pallas import tpu as pltpu
from jax.sharding import PartitionSpec as P

E = 256
ITERS = 3
EPS = 1e-06
SHARP = 2.5 * math.sqrt(E) * math.log2(math.e)

ITEM_DEV = 4096
LIST_DEV = 2048
QUART = ITEM_DEV // 4
N_ITEM = 8
N_LIST = 16

F32 = jnp.float32
BF16 = jnp.bfloat16
VMEM = pltpu.VMEM


def whole(n):
    return [pl.BlockSpec(memory_space=VMEM)] * n


def call(body, args, out, scratch, name, flops=0, limit=4):
    return pl.pallas_call(
        body,
        out_shape=out,
        in_specs=whole(len(args)),
        out_specs=tuple(whole(len(out))) if isinstance(out, tuple) else whole(1)[0],
        scratch_shapes=scratch,
        compiler_params=pltpu.CompilerParams(vmem_limit_bytes=limit << 20),
        cost_estimate=pl.CostEstimate(flops=flops, bytes_accessed=1 << 20, transcendentals=0),
        name=name,
    )(*args)


def unit(values, axis):
    square = jnp.mean(values * values, axis=axis, keepdims=True)
    return values * lax.rsqrt(square + EPS) * E ** (-0.5)


def place():
    item = lax.axis_index("item")
    spot = lax.axis_index("list")
    return item % 2, item // 2, spot // 4, spot % 4


def shift_z(block, step):
    return lax.ppermute(block, "item", [(i, (i + 2 * step) % N_ITEM) for i in range(N_ITEM)])


def swap_core(block):
    return lax.ppermute(block, "item", [(i, i ^ 1) for i in range(N_ITEM)])


def shift_plane(block, first, step):
    pairs = []
    for i in range(N_ITEM):
        for spot in range(N_LIST):
            if (i % 2 == 0) == first:
                to = spot // 4 * 4 + (spot + step) % 4
            else:
                to = (spot + 4 * step) % N_LIST
            pairs.append((i * N_LIST + spot, i * N_LIST + to))
    return lax.ppermute(block, ("item", "list"), pairs)


ORDER = (0, -1, 1, 2)


def gather(feat):
    block = jnp.concatenate([feat] + [shift_plane(feat, True, d) for d in (1, 3, 2)], 0)
    left, right = shift_plane(block, False, 1), shift_plane(block, False, 3)
    n = block.shape[0] // 2
    return [block, left, right, shift_plane(left[:n], False, 1), shift_plane(right[n:], False, 3)]


def prep_body(cent_ref, list_ref, raw_ref, sems):
    parts = [pl.ds(512 * m, 512) for m in range(4)]
    copies = [pltpu.make_async_copy(cent_ref.at[p, :], raw_ref.at[p, :], sems.at[m]) for m, p in enumerate(parts)]
    for copy in copies:
        copy.start()
    for copy, p in zip(copies, parts):
        copy.wait()
        list_ref[p, :] = unit(raw_ref[p, :].astype(F32), 1).astype(BF16)


def prep(cent):
    return pl.pallas_call(
        prep_body,
        out_shape=VMEM((LIST_DEV, E), BF16),
        in_specs=[pl.BlockSpec(memory_space=pl.ANY)],
        out_specs=whole(1)[0],
        scratch_shapes=[VMEM((LIST_DEV, E), BF16), pltpu.SemaphoreType.DMA((4,))],
        compiler_params=pltpu.CompilerParams(vmem_limit_bytes=4 << 20),
        name="lists",
    )(cent)


def put_rows(total, out_ref):
    rows = jnp.concatenate([total[:, 128 * k : 128 * (k + 1)] for k in range(32)], 0)
    out_ref[...] = jnp.broadcast_to(rows.astype(BF16)[None], (N_LIST, 32, 128))


TILE_M = 256


def gen_body(list_ref, own_ref, left_ref, right_ref, low_ref, high_ref, *refs):
    *kern_refs, item_ref, rows_ref, feat_ref = refs
    core, _, y, x = place()
    for i, outer in enumerate(ORDER):
        for j, inner in enumerate(ORDER):
            if i < 3:
                block = (own_ref, left_ref, right_ref)[i][16 * j : 16 * (j + 1), :]
            else:
                block = (low_ref, high_ref)[j // 2][16 * (j % 2) : 16 * (j % 2 + 1), :]
            from_y = (y + jnp.where(core == 0, outer, inner) + 4) % 4
            from_x = (x + jnp.where(core == 0, inner, outer) + 4) % 4
            spot = from_y * 4 + from_x
            feat_ref[pl.ds(pl.multiple_of(spot * 16, 16), 16), :] = block

    totals = []
    for n, kern_ref in enumerate(kern_refs):
        at = slice(QUART * n, QUART * (n + 1))
        block = feat_ref[:, at]
        wide = block.astype(F32)
        norm = lax.rsqrt(jnp.mean(wide * wide, axis=0, keepdims=True) + EPS) * E ** (-0.5)
        item_ref[at, :] = (wide * norm).T.astype(BF16)
        norm = norm * SHARP
        total = jnp.zeros((8, QUART), F32)
        for m in range(LIST_DEV // TILE_M):
            rows = slice(TILE_M * m, TILE_M * (m + 1))
            score = jnp.dot(list_ref[rows, :], block, preferred_element_type=F32)
            value = jnp.exp2(score * norm)
            kern_ref[rows, :] = value
            total = total + value.reshape(TILE_M // 8, 8, QUART).sum(0)
        totals.append(total.sum(0, keepdims=True))
    put_rows(jnp.concatenate(totals, 1), rows_ref)


def gen(lists, pieces):
    out = (VMEM((LIST_DEV, QUART), F32),) * 4 + (VMEM((ITEM_DEV, E), BF16), VMEM((N_LIST, 32, 128), BF16))
    return call(gen_body, (lists, *pieces), out, [VMEM((E, ITEM_DEV), BF16)], "generate", 2 * LIST_DEV * ITEM_DEV * E, 8)


def spread_rows(parts_ref, weight_ref, scale_ref):
    scale = weight_ref[...] / parts_ref[...].astype(F32).sum(0)
    for k in range(32):
        scale_ref[:, 128 * k : 128 * (k + 1)] = jnp.broadcast_to(scale[k : k + 1, :], (8, 128))


def lane(partial):
    return partial.T.sum(0, keepdims=True)


def col_body(*refs):
    *kern_refs, parts_ref, weight_ref, out_ref, scale_ref = refs
    spread_rows(parts_ref, weight_ref, scale_ref)
    cols = []
    for m in range(LIST_DEV // 128):
        at = slice(128 * m, 128 * (m + 1))
        total = jnp.zeros((16, 8, 128), F32)
        for h, ref in enumerate(kern_refs):
            for n in range(QUART // 128):
                by = scale_ref[:, QUART * h + 128 * n : QUART * h + 128 * (n + 1)]
                total = total + ref[at, 128 * n : 128 * (n + 1)].reshape(16, 8, 128) * by[None]
        cols.append(lane(total.reshape(128, 128)))
    out_ref[...] = jnp.broadcast_to(jnp.concatenate(cols, 0)[None], (N_ITEM, 16, 128))


def col_pass(kern, parts, weight):
    return call(
        col_body, (*kern, parts, weight), VMEM((N_ITEM, 16, 128), F32), [VMEM((8, ITEM_DEV), F32)],
        "columns", 2 * LIST_DEV * ITEM_DEV,
    )


def row_body(*refs):
    *kern_refs, cols_ref, cap_ref, out_ref, scale_ref, total_ref = refs
    scale = cap_ref[...] / cols_ref[...].sum(0)
    for k in range(16):
        scale_ref[128 * k : 128 * (k + 1), :] = jnp.broadcast_to(scale[k : k + 1, :], (128, 128)).T

    for h, ref in enumerate(kern_refs):

        def step(m, total):
            at = pl.ds(pl.multiple_of(m * 128, 128), 128)
            by = scale_ref[at, :].reshape(16, 8, 128)
            block = ref[at, :].reshape(16, 8, QUART)
            total = list(total)
            for j in range(16):
                for k in range(8):
                    total[k] = total[k] + block[j, :, 128 * k : 128 * (k + 1)] * by[j]
            return tuple(total)

        total = lax.fori_loop(0, LIST_DEV // 128, step, (jnp.zeros((8, 128), F32),) * 8)
        for k in range(8):
            first = QUART * h + 128 * k
            total_ref[:, first : first + 128] = total[k].sum(0, keepdims=True)

    put_rows(total_ref[...], out_ref)


def row_pass(kern, cols, cap):
    return call(
        row_body, (*kern, cols, cap), VMEM((N_LIST, 32, 128), BF16),
        [VMEM((LIST_DEV, 128), F32), VMEM((1, ITEM_DEV), F32)], "rows", 2 * LIST_DEV * ITEM_DEV,
    )


TILE_L = 256


def last_body(other, *refs):
    *kern_refs, item_ref, parts_ref, weight_ref, out_ref, scale_ref = refs
    core, _, _, _ = place()
    base = (1 - core if other else core) * 1024
    spread_rows(parts_ref, weight_ref, scale_ref)
    cols = []
    for m in range(1024 // TILE_L):
        at = pl.ds(pl.multiple_of(base + m * TILE_L, TILE_L), TILE_L)
        total = jnp.zeros((TILE_L // 8, 8, 128), F32)
        mixed = jnp.zeros((TILE_L, E), F32)
        for h, ref in enumerate(kern_refs):
            for n in range(QUART // 256):
                first = QUART * h + 256 * n
                block = ref[at, 256 * n : 256 * (n + 1)].reshape(TILE_L // 8, 8, 256)
                block = block * scale_ref[:, first : first + 256][None]
                total = total + block[:, :, :128] + block[:, :, 128:]
                block = block.reshape(TILE_L, 256).astype(BF16)
                mixed = mixed + jnp.dot(block, item_ref[first : first + 256, :], preferred_element_type=F32)
        out_ref[TILE_L * m : TILE_L * (m + 1), :] = mixed.astype(BF16)
        total = total.reshape(TILE_L, 128)
        cols += [lane(total[128 * t : 128 * (t + 1)]) for t in range(TILE_L // 128)]

    for q in range(4):
        col = jnp.concatenate(cols[2 * q : 2 * q + 2], 0)
        high = col.astype(BF16).astype(F32)
        block = jnp.concatenate([jnp.concatenate([high, col - high], 1), jnp.zeros((14, E), F32)], 0)
        out_ref[1024 + 16 * q : 1024 + 16 * (q + 1), :] = block.astype(BF16)


def last_pass(other, kern, item, parts, weight):
    return call(
        functools.partial(last_body, other), (*kern, item, parts, weight), VMEM((1088, E), BF16),
        [VMEM((8, ITEM_DEV), F32)], "totals", LIST_DEV * ITEM_DEV * E, 4,
    )


AWAY = (0, 1, 3, 2)


def fold_body(stay_ref, came_ref, *out_refs):
    _, z, _, _ = place()
    for d, out_ref in zip(AWAY, out_refs):
        q = (z + d) % 4
        rows = pl.ds(pl.multiple_of(q * 256, 256), 256)
        tail = pl.ds(pl.multiple_of(1024 + q * 16, 16), 16)
        out_ref[:256, :] = (stay_ref[rows, :].astype(F32) + came_ref[rows, :].astype(F32)).astype(out_ref.dtype)
        cols = stay_ref[tail, :].astype(F32) + came_ref[tail, :].astype(F32)
        cols = cols[:, :128] + cols[:, 128:]
        high = cols.astype(BF16).astype(F32)
        out_ref[256:, :] = jnp.concatenate([high, cols - high], 1).astype(out_ref.dtype)


def fold(stay, came):
    out = (VMEM((272, E), F32),) + (VMEM((272, E), BF16),) * 3
    return call(fold_body, (stay, came), out, [], "fold")


def finish_body(mine_ref, a_ref, b_ref, c_ref, list_ref, out_ref):
    core, z, _, _ = place()
    first = pl.multiple_of(core * 1024 + z * 256, 256)
    totals = mine_ref[...] + a_ref[...].astype(F32) + b_ref[...].astype(F32) + c_ref[...].astype(F32)
    cols = totals[256:, :128] + totals[256:, 128:]
    for t in range(2):
        col = jnp.broadcast_to(cols[t : t + 1], (128, 128)).T
        col = jnp.concatenate([col, col], 1)
        own = list_ref[pl.ds(first + 128 * t, 128), :].astype(F32)
        mixed = 0.1 * own + totals[128 * t : 128 * (t + 1)] / col
        out_ref[128 * t : 128 * (t + 1), :] = unit(mixed, 1).astype(BF16)


def finish(pieces, lists):
    return call(finish_body, (*pieces, lists), VMEM((256, E), BF16), [], "finish")


FROM = (0, -1, 1, 2)


def lay_body(*refs):
    blocks, out_ref, sems = refs[:8], refs[8], refs[9]
    core, z, _, _ = place()
    copies = []
    for i, ref in enumerate(blocks):
        half = core if i < 4 else 1 - core
        row = pl.multiple_of(half * 1024 + (z + FROM[i % 4] + 4) % 4 * 256, 256)
        copies.append(pltpu.make_async_copy(ref, out_ref.at[pl.ds(row, 256), :], sems.at[i]))
    for copy in copies:
        copy.start()
    for copy in copies:
        copy.wait()


def lay(blocks):
    return pl.pallas_call(
        lay_body,
        out_shape=jax.ShapeDtypeStruct((LIST_DEV, E), BF16),
        in_specs=whole(8),
        out_specs=pl.BlockSpec(memory_space=pl.ANY),
        scratch_shapes=[pltpu.SemaphoreType.DMA((8,))],
        compiler_params=pltpu.CompilerParams(vmem_limit_bytes=12 << 20),
        name="lay",
    )(*blocks)


def local(items, item_weight, list_capacity, centroids):
    weight = item_weight.reshape(32, 128)
    cap = list_capacity.reshape(16, 128)
    lists = prep(centroids)
    *kern, item, parts = gen(lists, gather(items.T))

    for step in range(ITERS - 1):
        parts = lax.all_to_all(parts, "list", 0, 0)
        cols = lax.all_to_all(col_pass(kern, parts, weight), "item", 0, 0)
        parts = row_pass(kern, cols, cap)
    parts = lax.all_to_all(parts, "list", 0, 0)

    came = swap_core(last_pass(True, kern, item, parts, weight))
    stay = last_pass(False, kern, item, parts, weight)
    pieces = fold(stay, came)
    pieces = pieces[:1] + tuple(shift_z(p, d) for d, p in zip(AWAY[1:], pieces[1:]))
    done = finish(pieces, lists)
    done = [done] + [shift_z(done, d) for d in AWAY[1:]]
    return lay(done + [swap_core(d) for d in done])


def solution(mesh):
    placed = (P("item", "list"), P("item"), P("list"), P("list", None))
    return jax.shard_map(
        local, mesh=mesh, in_specs=placed, out_specs=P("list", None), check_vma=False
    )
```

time: 139 us -> 130 us (0.935)
  waiting for transfers between devices: 10.8 us -> 22.4 us
  Pallas kernels: 33 us -> 22.9 us
  starting transfers between devices: 34.4 us -> 27.5 us
  blocking collectives: 56.5 us -> 54.1 us
  local copies, waits for them, and re-layouts: 3.56 us -> 1.27 us
    ppermute x20 -> x13, waiting for transfers between devices: 9.86 us -> 21.4 us  [the longest x7 15.1 us: shift_plane(): return lax.ppermute(block, ('item', 'list'), pairs)]
    pallas_call x11 -> x9, Pallas kernels: 32 us -> 21.1 us  [call(): pl.pallas_call(body, out_shape=out, in_specs=whole(len(args)), out_specs=...]
    ppermute x20 -> x13, starting transfers between devices: 24.7 us -> 17.8 us  [the longest x7 11.3 us: shift_plane(): return lax.ppermute(block, ('item', 'list'), pairs)]
    all_to_all x3, blocking collectives: 31.7 us -> 28.8 us  [local(): parts = lax.all_to_all(parts, 'list', 0, 0)]
  transfers between devices with their start and end apart: 25 -> 18, of which waited for: 10 -> 13; matrix products, arithmetic and copies ran while one was open for 1% -> 0% of each run, Pallas kernels for 6% -> 2%
where the time goes in v3:
time: 130 us; the launch traced here: 129 us
  blocking collectives  54.1 us (42%)
  starting transfers between devices  27.5 us (21%)
  Pallas kernels  22.9 us (18%)
  waiting for transfers between devices  22.4 us (17%)
    all_to_all x3, blocking collectives, local(): parts = lax.all_to_all(parts, 'list', 0, 0)  28.8 us
    all_to_all x2, blocking collectives, local(): cols = lax.all_to_all(col_pass(kern, parts, weight), 'item', 0, 0)  25.3 us
    pallas_call x9, Pallas kernels, call(): pl.pallas_call(body, out_shape=out, in_specs=whole(len(args)), out_specs=...  21.1 us
    ppermute x7, waiting for transfers between devices, shift_plane(): return lax.ppermute(block, ('item', 'list'), pairs)  15.1 us
    ppermute x7, starting transfers between devices, shift_plane(): return lax.ppermute(block, ('item', 'list'), pairs)  11.3 us
    ppermute x5, starting transfers between devices, swap_core(): return lax.ppermute(block, 'item', [(i, i ^ 1) for i in range(N_ITEM)])  9.71 us
    ppermute x6, starting transfers between devices, shift_z(): lax.ppermute(block, 'item', [(i, (i + 2 * step) % N_ITEM) for i in range(...  6.45 us
    ppermute x6, waiting for transfers between devices, shift_z(): lax.ppermute(block, 'item', [(i, (i + 2 * step) % N_ITEM) for i in range(...  6.28 us
  transfers between devices with their start and end apart: 18, of which 13 were waited for; matrix products, arithmetic and copies ran while one was open for 0% of the time, Pallas kernels for 2%

profile of v3, /device:TPU:1, one launch (start us, length us, event | category | flops | bytes accessed | tf_op | source)
XLA Modules:
  0.0 129.3 jit_solution(7858143312601752084)
XLA Ops:
  0.0 3.7 %collective-permute-start.2 = (bf16[16,4096]{1,0:T(8,128)(2,1)}, bf16[16,4096]{1,0:T(8,128)(2,1)S(1)}, u32[]{:S(2)}, u32[]{:S(2)}) collective-permute-start(bf16[16,4096]{1,0:T(8,128)(2,1)} %bitcast.9), channel_id=1, source_target_pairs={{0,2},{1,3},{2,0},{3,1},{4,6},{5,7},{6,4},{7,5},{8,10},{9,11},{10,... | collective-permute-start | bytes 393224 | tf_op jit(solution)/shard_map/ppermute | solution.py:72
  3.7 0.8 collective-permute-start.1
  4.5 0.7 collective-permute-start
  5.2 1.4 %collective-permute-done.2 = bf16[16,4096]{1,0:T(8,128)(2,1)S(1)} collective-permute-done((bf16[16,4096]{1,0:T(8,128)(2,1)}, bf16[16,4096]{1,0:T(8,128)(2,1)S(1)}, u32[]{:S(2)}, u32[]{:S(2)}) %collective-permute-start.2) | collective-permute-done | bytes 131104 | tf_op jit(solution)/shard_map/ppermute | solution.py:72
  6.6 1.8 %collective-permute-done.1 = bf16[16,4096]{1,0:T(8,128)(2,1)S(1)} collective-permute-done((bf16[16,4096]{1,0:T(8,128)(2,1)}, bf16[16,4096]{1,0:T(8,128)(2,1)S(1)}, u32[]{:S(2)}, u32[]{:S(2)}) %collective-permute-start.1) | collective-permute-done | bytes 131104 | tf_op jit(solution)/shard_map/ppermute | solution.py:72
  8.4 1.4 %collective-permute-done = bf16[16,4096]{1,0:T(8,128)(2,1)S(1)} collective-permute-done((bf16[16,4096]{1,0:T(8,128)(2,1)}, bf16[16,4096]{1,0:T(8,128)(2,1)S(1)}, u32[]{:S(2)}, u32[]{:S(2)}) %collective-permute-start) | collective-permute-done | bytes 131104 | tf_op jit(solution)/shard_map/ppermute | solution.py:72
  9.8 0.9 pad_maximum_fusion.own_ref
  10.7 2.5 %collective-permute-start.4 = (bf16[64,4096]{1,0:T(8,128)(2,1)S(1)}, bf16[64,4096]{1,0:T(8,128)(2,1)S(1)}, u32[]{:S(2)}, u32[]{:S(2)}) collective-permute-start(bf16[64,4096]{1,0:T(8,128)(2,1)S(1)} %pad_maximum_fusion.own_ref), channel_id=1, source_target_pairs={{0,12},{1,13},{2,14},{3,15},{4,0},{5,1},{6,2},{7,3},{8,4},{9,5},{1... | collective-permute-start | bytes 1572872 | tf_op jit(solution)/shard_map/ppermute | solution.py:72
  13.3 6.1 %collective-permute-done.4.right_ref = bf16[64,4096]{1,0:T(8,128)(2,1)S(1)} collective-permute-done((bf16[64,4096]{1,0:T(8,128)(2,1)S(1)}, bf16[64,4096]{1,0:T(8,128)(2,1)S(1)}, u32[]{:S(2)}, u32[]{:S(2)}) %collective-permute-start.4) | collective-permute-done | bytes 524320 | tf_op jit(solution)/shard_map/ppermute | solution.py:72
  19.4 3.5 %collective-permute-start.6 = (bf16[32,4096]{1,0:T(8,128)(2,1)S(1)}, bf16[32,4096]{1,0:T(8,128)(2,1)S(1)}, u32[]{:S(2)}, u32[]{:S(2)}) collective-permute-start(bf16[32,4096]{1,0:T(8,128)(2,1)S(1)} %slice.9), channel_id=1, source_target_pairs={{0,12},{1,13},{2,14},{3,15},{4,0},{5,1},{6,2},{7,3},{8,4},{9,5},{1... | collective-permute-start | bytes 786440 | tf_op jit(solution)/shard_map/ppermute | solution.py:72
  22.9 0.1 collective-permute-start.5
  23.0 0.0 copy-start
  23.0 1.2 copy-done
  24.2 0.8 lists.1.list_ref
  25.0 0.0 copy-start.1
  25.0 1.2 collective-permute-done.6.high_ref
  26.2 3.2 %collective-permute-done.5.low_ref = bf16[32,4096]{1,0:T(8,128)(2,1)S(1)} collective-permute-done((bf16[32,4096]{1,0:T(8,128)(2,1)S(1)}, bf16[32,4096]{1,0:T(8,128)(2,1)S(1)}, u32[]{:S(2)}, u32[]{:S(2)}) %collective-permute-start.5) | collective-permute-done | bytes 262176 | tf_op jit(solution)/shard_map/ppermute | solution.py:72
  29.4 5.6 %generate.1 = (f32[2048,1024]{1,0:T(8,128)S(1)}, f32[2048,1024]{1,0:T(8,128)S(1)}, f32[2048,1024]{1,0:T(8,128)S(1)}, f32[2048,1024]{1,0:T(8,128)S(1)}, bf16[4096...) custom-call(bf16[2048,256]{1,0:T(8,128)(2,1)S(1)} %lists.1.list_ref, ...), custom_call_target="tpu_custom_call" | custom-call | flops 4294967296 | bytes 1048576 | tf_op jit(solution)/shard_map/generate/pallas_call | solution.py:32
  35.0 9.4 %all_to_all.25.refs_4_ = bf16[16,32,128]{2,1,0:T(8,128)(2,1)S(1)} all-to-all(bf16[16,32,128]{2,1,0:T(8,128)(2,1)S(1)} %get-tuple-element.20), channel_id=1, replica_groups=mesh['item'=8,'list'=16] {'list'}, dimensions={0} | all-to-all | bytes 262144 | tf_op jit(solution)/shard_map/all_to_all | solution.py:331
  44.4 2.3 %columns.2 = f32[8,16,128]{2,1,0:T(8,128)S(1)} custom-call(f32[2048,1024]{1,0:T(8,128)S(1)} %get-tuple-element.15.refs_0_, f32[2048,1024]{1,0:T(8,128)S(1)} %get-tuple-element.16.refs_1_, f32[2048,1024]{1,0:T(8,128)S(1)} %get-tuple-element.17.refs_2_, f32[2048,1024]{1,0:T(8,128)S(1)} %get-tuple-element.18.refs_3_, ...), custom_call_target="tpu_custom_call" | custom-call | flops 16777216 | bytes 1048576 | tf_op jit(solution)/shard_map/columns/pallas_call | solution.py:32
  46.7 16.0 %all_to_all.26.refs_4_ = f32[8,16,128]{2,1,0:T(8,128)S(1)} all-to-all(f32[8,16,128]{2,1,0:T(8,128)S(1)} %columns.2), channel_id=1, replica_groups=mesh['item'=8,'list'=16] {'item'}, dimensions={0} | all-to-all | bytes 131072 | tf_op jit(solution)/shard_map/all_to_all | solution.py:332
  62.7 2.9 %rows.2 = bf16[16,32,128]{2,1,0:T(8,128)(2,1)S(1)} custom-call(f32[2048,1024]{1,0:T(8,128)S(1)} %get-tuple-element.15.refs_0_, f32[2048,1024]{1,0:T(8,128)S(1)} %get-tuple-element.16.refs_1_, f32[2048,1024]{1,0:T(8,128)S(1)} %get-tuple-element.17.refs_2_, f32[2048,1024]{1,0:T(8,128)S(1)} %get-tuple-element.18.refs_3_, f32[8,16,128]{2,1,0:T(8,128)S(1)} %all_to_all.26.refs_4_, ...), custom_call_target="tpu_custom_call" | custom-call | flops 16777216 | bytes 1048576 | tf_op jit(solution)/shard_map/rows/pallas_call | solution.py:32
  65.6 9.7 %all_to_all.27.refs_4_ = bf16[16,32,128]{2,1,0:T(8,128)(2,1)S(1)} all-to-all(bf16[16,32,128]{2,1,0:T(8,128)(2,1)S(1)} %rows.2), channel_id=1, replica_groups=mesh['item'=8,'list'=16] {'list'}, dimensions={0} | all-to-all | bytes 262144 | tf_op jit(solution)/shard_map/all_to_all | solution.py:331
  75.3 2.3 %columns.3 = f32[8,16,128]{2,1,0:T(8,128)S(1)} custom-call(f32[2048,1024]{1,0:T(8,128)S(1)} %get-tuple-element.15.refs_0_, f32[2048,1024]{1,0:T(8,128)S(1)} %get-tuple-element.16.refs_1_, f32[2048,1024]{1,0:T(8,128)S(1)} %get-tuple-element.17.refs_2_, f32[2048,1024]{1,0:T(8,128)S(1)} %get-tuple-element.18.refs_3_, ...), custom_call_target="tpu_custom_call" | custom-call | flops 16777216 | bytes 1048576 | tf_op jit(solution)/shard_map/columns/pallas_call | solution.py:32
  77.5 9.4 %all_to_all.28.refs_4_ = f32[8,16,128]{2,1,0:T(8,128)S(1)} all-to-all(f32[8,16,128]{2,1,0:T(8,128)S(1)} %columns.3), channel_id=1, replica_groups=mesh['item'=8,'list'=16] {'item'}, dimensions={0} | all-to-all | bytes 131072 | tf_op jit(solution)/shard_map/all_to_all | solution.py:332
  86.9 2.9 %rows.3 = bf16[16,32,128]{2,1,0:T(8,128)(2,1)S(1)} custom-call(f32[2048,1024]{1,0:T(8,128)S(1)} %get-tuple-element.15.refs_0_, f32[2048,1024]{1,0:T(8,128)S(1)} %get-tuple-element.16.refs_1_, f32[2048,1024]{1,0:T(8,128)S(1)} %get-tuple-element.17.refs_2_, f32[2048,1024]{1,0:T(8,128)S(1)} %get-tuple-element.18.refs_3_, f32[8,16,128]{2,1,0:T(8,128)S(1)} %all_to_all.28.refs_4_, ...), custom_call_target="tpu_custom_call" | custom-call | flops 16777216 | bytes 1048576 | tf_op jit(solution)/shard_map/rows/pallas_call | solution.py:32
  89.8 9.7 %all_to_all.29.refs_5_ = bf16[16,32,128]{2,1,0:T(8,128)(2,1)S(1)} all-to-all(bf16[16,32,128]{2,1,0:T(8,128)(2,1)S(1)} %rows.3), channel_id=1, replica_groups=mesh['item'=8,'list'=16] {'list'}, dimensions={0} | all-to-all | bytes 262144 | tf_op jit(solution)/shard_map/all_to_all | solution.py:334
  99.5 2.4 %totals.3 = bf16[1088,256]{1,0:T(8,128)(2,1)S(1)} custom-call(f32[2048,1024]{1,0:T(8,128)S(1)} %get-tuple-element.15.refs_0_, f32[2048,1024]{1,0:T(8,128)S(1)} %get-tuple-element.16.refs_1_, f32[2048,1024]{1,0:T(8,128)S(1)} %get-tuple-element.17.refs_2_, f32[2048,1024]{1,0:T(8,128)S(1)} %get-tuple-element.18.refs_3_, ...), custom_call_target="tpu_custom_call" | custom-call | flops 2147483648 | bytes 1048576 | tf_op jit(solution)/shard_map/totals/pallas_call | solution.py:32
  101.9 2.2 %collective-permute-start.7 = (bf16[1088,256]{1,0:T(8,128)(2,1)S(1)}, bf16[1088,256]{1,0:T(8,128)(2,1)S(1)}, u32[]{:S(2)}, u32[]{:S(2)}) collective-permute-start(bf16[1088,256]{1,0:T(8,128)(2,1)S(1)} %totals.3), channel_id=1, source_target_pairs={{0,16},{16,0},{32,48},{48,32},{64,80},{80,64},{96,112},{112,96},{1... | collective-permute-start | bytes 1671176 | tf_op jit(solution)/shard_map/ppermute | solution.py:60
  104.2 2.4 %totals.2.stay_ref = bf16[1088,256]{1,0:T(8,128)(2,1)S(1)} custom-call(f32[2048,1024]{1,0:T(8,128)S(1)} %get-tuple-element.15.refs_0_, f32[2048,1024]{1,0:T(8,128)S(1)} %get-tuple-element.16.refs_1_, f32[2048,1024]{1,0:T(8,128)S(1)} %get-tuple-element.17.refs_2_, f32[2048,1024]{1,0:T(8,128)S(1)} %get-tuple-element.18.refs_3_, ...), custom_call_target="tpu_custom_call" | custom-call | flops 2147483648 | bytes 1048576 | tf_op jit(solution)/shard_map/totals/pallas_call | solution.py:32
  106.6 0.2 fold.1
  106.7 0.4 collective-permute-start.8
  107.1 2.4 %collective-permute-start.9 = (bf16[272,256]{1,0:T(8,128)(2,1)S(1)}, bf16[272,256]{1,0:T(8,128)(2,1)S(1)}, u32[]{:S(2)}, u32[]{:S(2)}) collective-permute-start(bf16[272,256]{1,0:T(8,128)(2,1)S(1)} %get-tuple-element.23), channel_id=1, source_target_pairs={{0,96},{16,112},{32,0},{48,16},{64,32},{80,48},{96,64},{112,80},{1... | collective-permute-start | bytes 417800 | tf_op jit(solution)/shard_map/ppermute | solution.py:56
  109.5 3.8 %collective-permute-done.8.a_ref = bf16[272,256]{1,0:T(8,128)(2,1)S(1)} collective-permute-done((bf16[272,256]{1,0:T(8,128)(2,1)S(1)}, bf16[272,256]{1,0:T(8,128)(2,1)S(1)}, u32[]{:S(2)}, u32[]{:S(2)}) %collective-permute-start.8) | collective-permute-done | bytes 139296 | tf_op jit(solution)/shard_map/ppermute | solution.py:56
  113.3 1.8 %collective-permute-done.9.b_ref = bf16[272,256]{1,0:T(8,128)(2,1)S(1)} collective-permute-done((bf16[272,256]{1,0:T(8,128)(2,1)S(1)}, bf16[272,256]{1,0:T(8,128)(2,1)S(1)}, u32[]{:S(2)}, u32[]{:S(2)}) %collective-permute-start.9) | collective-permute-done | bytes 139296 | tf_op jit(solution)/shard_map/ppermute | solution.py:56
  115.1 0.5 collective-permute-done.10.c_ref
  115.7 0.2 finish.1.refs_0_
  115.9 1.3 %collective-permute-start.13 = (bf16[256,256]{1,0:T(8,128)(2,1)S(1)}, bf16[256,256]{1,0:T(8,128)(2,1)S(1)}, u32[]{:S(2)}, u32[]{:S(2)}) collective-permute-start(bf16[256,256]{1,0:T(8,128)(2,1)S(1)} %finish.1.refs_0_), channel_id=1, source_target_pairs={{0,64},{16,80},{32,96},{48,112},{64,0},{80,16},{96,32},{112,48},{1... | collective-permute-start | bytes 393224 | tf_op jit(solution)/shard_map/ppermute | solution.py:56
  117.2 2.4 %collective-permute-start.12 = (bf16[256,256]{1,0:T(8,128)(2,1)S(1)}, bf16[256,256]{1,0:T(8,128)(2,1)S(1)}, u32[]{:S(2)}, u32[]{:S(2)}) collective-permute-start(bf16[256,256]{1,0:T(8,128)(2,1)S(1)} %finish.1.refs_0_), channel_id=1, source_target_pairs={{0,96},{16,112},{32,0},{48,16},{64,32},{80,48},{96,64},{112,80},{1... | collective-permute-start | bytes 393224 | tf_op jit(solution)/shard_map/ppermute | solution.py:56
  119.6 1.6 %collective-permute-start.14 = (bf16[256,256]{1,0:T(8,128)(2,1)S(1)}, bf16[256,256]{1,0:T(8,128)(2,1)S(1)}, u32[]{:S(2)}, u32[]{:S(2)}) collective-permute-start(bf16[256,256]{1,0:T(8,128)(2,1)S(1)} %finish.1.refs_0_), channel_id=1, source_target_pairs={{0,16},{16,0},{32,48},{48,32},{64,80},{80,64},{96,112},{112,96},{1... | collective-permute-start | bytes 393224 | tf_op jit(solution)/shard_map/ppermute | solution.py:60
  121.2 0.1 collective-permute-done.13.refs_3_
  121.3 3.6 %collective-permute-start.17 = (bf16[256,256]{1,0:T(8,128)(2,1)S(1)}, bf16[256,256]{1,0:T(8,128)(2,1)S(1)}, u32[]{:S(2)}, u32[]{:S(2)}) collective-permute-start(bf16[256,256]{1,0:T(8,128)(2,1)S(1)} %collective-permute-done.13.refs_3_), channel_id=1, source_target_pairs={{0,16},{16,0},{32,48},{48,32},{64,80},{80,64},{96,112},{112,96},{1... | collective-permute-start | bytes 393224 | tf_op jit(solution)/shard_map/ppermute | solution.py:60
  124.8 0.1 collective-permute-done.12.refs_2_
  124.9 1.9 %collective-permute-start.16 = (bf16[256,256]{1,0:T(8,128)(2,1)S(1)}, bf16[256,256]{1,0:T(8,128)(2,1)S(1)}, u32[]{:S(2)}, u32[]{:S(2)}) collective-permute-start(bf16[256,256]{1,0:T(8,128)(2,1)S(1)} %collective-permute-done.12.refs_2_), channel_id=1, source_target_pairs={{0,16},{16,0},{32,48},{48,32},{64,80},{80,64},{96,112},{112,96},{1... | collective-permute-start | bytes 393224 | tf_op jit(solution)/shard_map/ppermute | solution.py:60
  126.8 0.4 collective-permute-start.15
  127.2 0.6 collective-permute-done.16.refs_6_
  127.8 0.4 collective-permute-done.15.refs_5_
  128.2 1.0 lay.1
  (13 shorter events, 0.1 us)
Async XLA Ops:
  0.0 6.6 %collective-permute-start.2 = (bf16[16,4096]{1,0:T(8,128)(2,1)}, bf16[16,4096]{1,0:T(8,128)(2,1)S(1)}, u32[]{:S(2)}, u32[]{:S(2)}) collective-permute-start(bf16[16,4096]{1,0:T(8,128)(2,1)} %bitcast.9), channel_id=1, source_target_pairs={{0,2},{1,3},{2,0},{3,1},{4,6},{5,7},{6,4},{7,5},{8,10},{9,11},{10,... | collective-permute-start | bytes 393224 | tf_op jit(solution)/shard_map/ppermute | solution.py:72
  3.7 4.7 %collective-permute-start.1 = (bf16[16,4096]{1,0:T(8,128)(2,1)}, bf16[16,4096]{1,0:T(8,128)(2,1)S(1)}, u32[]{:S(2)}, u32[]{:S(2)}) collective-permute-start(bf16[16,4096]{1,0:T(8,128)(2,1)} %bitcast.10), channel_id=1, source_target_pairs={{0,3},{1,0},{2,1},{3,2},{4,7},{5,4},{6,5},{7,6},{8,11},{9,8},{10,9... | collective-permute-start | bytes 393224 | tf_op jit(solution)/shard_map/ppermute | solution.py:72
  4.5 5.2 %collective-permute-start = (bf16[16,4096]{1,0:T(8,128)(2,1)}, bf16[16,4096]{1,0:T(8,128)(2,1)S(1)}, u32[]{:S(2)}, u32[]{:S(2)}) collective-permute-start(bf16[16,4096]{1,0:T(8,128)(2,1)} %bitcast.11), channel_id=1, source_target_pairs={{0,1},{1,2},{2,3},{3,0},{4,5},{5,6},{6,7},{7,4},{8,9},{9,10},{10,1... | collective-permute-start | bytes 393224 | tf_op jit(solution)/shard_map/ppermute | solution.py:72
  10.7 8.7 %collective-permute-start.4 = (bf16[64,4096]{1,0:T(8,128)(2,1)S(1)}, bf16[64,4096]{1,0:T(8,128)(2,1)S(1)}, u32[]{:S(2)}, u32[]{:S(2)}) collective-permute-start(bf16[64,4096]{1,0:T(8,128)(2,1)S(1)} %pad_maximum_fusion.own_ref), channel_id=1, source_target_pairs={{0,12},{1,13},{2,14},{3,15},{4,0},{5,1},{6,2},{7,3},{8,4},{9,5},{1... | collective-permute-start | bytes 1572872 | tf_op jit(solution)/shard_map/ppermute | solution.py:72
  13.2 9.6 %collective-permute-start.3 = (bf16[64,4096]{1,0:T(8,128)(2,1)S(1)}, bf16[64,4096]{1,0:T(8,128)(2,1)S(1)}, u32[]{:S(2)}, u32[]{:S(2)}) collective-permute-start(bf16[64,4096]{1,0:T(8,128)(2,1)S(1)} %pad_maximum_fusion.own_ref), channel_id=1, source_target_pairs={{0,4},{1,5},{2,6},{3,7},{4,8},{5,9},{6,10},{7,11},{8,12},{9,13},{1... | collective-permute-start | bytes 1572872 | tf_op jit(solution)/shard_map/ppermute | solution.py:72
  19.4 6.8 %collective-permute-start.6 = (bf16[32,4096]{1,0:T(8,128)(2,1)S(1)}, bf16[32,4096]{1,0:T(8,128)(2,1)S(1)}, u32[]{:S(2)}, u32[]{:S(2)}) collective-permute-start(bf16[32,4096]{1,0:T(8,128)(2,1)S(1)} %slice.9), channel_id=1, source_target_pairs={{0,12},{1,13},{2,14},{3,15},{4,0},{5,1},{6,2},{7,3},{8,4},{9,5},{1... | collective-permute-start | bytes 786440 | tf_op jit(solution)/shard_map/ppermute | solution.py:72
  22.9 6.5 %collective-permute-start.5 = (bf16[32,4096]{1,0:T(8,128)(2,1)S(1)}, bf16[32,4096]{1,0:T(8,128)(2,1)S(1)}, u32[]{:S(2)}, u32[]{:S(2)}) collective-permute-start(bf16[32,4096]{1,0:T(8,128)(2,1)S(1)} %slice.8), channel_id=1, source_target_pairs={{0,4},{1,5},{2,6},{3,7},{4,8},{5,9},{6,10},{7,11},{8,12},{9,13},{1... | collective-permute-start | bytes 786440 | tf_op jit(solution)/shard_map/ppermute | solution.py:72
  23.0 1.2 copy-start
  25.0 19.4 %copy-start.1 = (f32[4096]{0:T(1024)S(1)}, f32[4096]{0:T(1024)}, u32[]{:S(2)}) copy-start(f32[4096]{0:T(1024)} %param.5) | copy-start | bytes 49156
  44.4 18.2 %copy-start.2 = (f32[2048]{0:T(1024)S(1)}, f32[2048]{0:T(1024)}, u32[]{:S(2)}) copy-start(f32[2048]{0:T(1024)} %param.6) | copy-start | bytes 24580
  101.9 4.7 %collective-permute-start.7 = (bf16[1088,256]{1,0:T(8,128)(2,1)S(1)}, bf16[1088,256]{1,0:T(8,128)(2,1)S(1)}, u32[]{:S(2)}, u32[]{:S(2)}) collective-permute-start(bf16[1088,256]{1,0:T(8,128)(2,1)S(1)} %totals.3), channel_id=1, source_target_pairs={{0,16},{16,0},{32,48},{48,32},{64,80},{80,64},{96,112},{112,96},{1... | collective-permute-start | bytes 1671176 | tf_op jit(solution)/shard_map/ppermute | solution.py:60
  106.7 6.6 %collective-permute-start.8 = (bf16[272,256]{1,0:T(8,128)(2,1)S(1)}, bf16[272,256]{1,0:T(8,128)(2,1)S(1)}, u32[]{:S(2)}, u32[]{:S(2)}) collective-permute-start(bf16[272,256]{1,0:T(8,128)(2,1)S(1)} %get-tuple-element.22), channel_id=1, source_target_pairs={{0,32},{16,48},{32,64},{48,80},{64,96},{80,112},{96,0},{112,16},{1... | collective-permute-start | bytes 417800 | tf_op jit(solution)/shard_map/ppermute | solution.py:56
  107.1 8.0 %collective-permute-start.9 = (bf16[272,256]{1,0:T(8,128)(2,1)S(1)}, bf16[272,256]{1,0:T(8,128)(2,1)S(1)}, u32[]{:S(2)}, u32[]{:S(2)}) collective-permute-start(bf16[272,256]{1,0:T(8,128)(2,1)S(1)} %get-tuple-element.23), channel_id=1, source_target_pairs={{0,96},{16,112},{32,0},{48,16},{64,32},{80,48},{96,64},{112,80},{1... | collective-permute-start | bytes 417800 | tf_op jit(solution)/shard_map/ppermute | solution.py:56
  109.5 6.2 %collective-permute-start.10 = (bf16[272,256]{1,0:T(8,128)(2,1)S(1)}, bf16[272,256]{1,0:T(8,128)(2,1)S(1)}, u32[]{:S(2)}, u32[]{:S(2)}) collective-permute-start(bf16[272,256]{1,0:T(8,128)(2,1)S(1)} %get-tuple-element.24), channel_id=1, source_target_pairs={{0,64},{16,80},{32,96},{48,112},{64,0},{80,16},{96,32},{112,48},{1... | collective-permute-start | bytes 417800 | tf_op jit(solution)/shard_map/ppermute | solution.py:56
  115.9 5.4 %collective-permute-start.13 = (bf16[256,256]{1,0:T(8,128)(2,1)S(1)}, bf16[256,256]{1,0:T(8,128)(2,1)S(1)}, u32[]{:S(2)}, u32[]{:S(2)}) collective-permute-start(bf16[256,256]{1,0:T(8,128)(2,1)S(1)} %finish.1.refs_0_), channel_id=1, source_target_pairs={{0,64},{16,80},{32,96},{48,112},{64,0},{80,16},{96,32},{112,48},{1... | collective-permute-start | bytes 393224 | tf_op jit(solution)/shard_map/ppermute | solution.py:56
  117.2 7.7 %collective-permute-start.12 = (bf16[256,256]{1,0:T(8,128)(2,1)S(1)}, bf16[256,256]{1,0:T(8,128)(2,1)S(1)}, u32[]{:S(2)}, u32[]{:S(2)}) collective-permute-start(bf16[256,256]{1,0:T(8,128)(2,1)S(1)} %finish.1.refs_0_), channel_id=1, source_target_pairs={{0,96},{16,112},{32,0},{48,16},{64,32},{80,48},{96,64},{112,80},{1... | collective-permute-start | bytes 393224 | tf_op jit(solution)/shard_map/ppermute | solution.py:56
  119.6 7.2 %collective-permute-start.11 = (bf16[256,256]{1,0:T(8,128)(2,1)S(1)}, bf16[256,256]{1,0:T(8,128)(2,1)S(1)}, u32[]{:S(2)}, u32[]{:S(2)}) collective-permute-start(bf16[256,256]{1,0:T(8,128)(2,1)S(1)} %finish.1.refs_0_), channel_id=1, source_target_pairs={{0,32},{16,48},{32,64},{48,80},{64,96},{80,112},{96,0},{112,16},{1... | collective-permute-start | bytes 393224 | tf_op jit(solution)/shard_map/ppermute | solution.py:56
  119.6 7.6 %collective-permute-start.14 = (bf16[256,256]{1,0:T(8,128)(2,1)S(1)}, bf16[256,256]{1,0:T(8,128)(2,1)S(1)}, u32[]{:S(2)}, u32[]{:S(2)}) collective-permute-start(bf16[256,256]{1,0:T(8,128)(2,1)S(1)} %finish.1.refs_0_), channel_id=1, source_target_pairs={{0,16},{16,0},{32,48},{48,32},{64,80},{80,64},{96,112},{112,96},{1... | collective-permute-start | bytes 393224 | tf_op jit(solution)/shard_map/ppermute | solution.py:60
  121.3 5.9 %collective-permute-start.17 = (bf16[256,256]{1,0:T(8,128)(2,1)S(1)}, bf16[256,256]{1,0:T(8,128)(2,1)S(1)}, u32[]{:S(2)}, u32[]{:S(2)}) collective-permute-start(bf16[256,256]{1,0:T(8,128)(2,1)S(1)} %collective-permute-done.13.refs_3_), channel_id=1, source_target_pairs={{0,16},{16,0},{32,48},{48,32},{64,80},{80,64},{96,112},{112,96},{1... | collective-permute-start | bytes 393224 | tf_op jit(solution)/shard_map/ppermute | solution.py:60
  124.9 2.9 %collective-permute-start.16 = (bf16[256,256]{1,0:T(8,128)(2,1)S(1)}, bf16[256,256]{1,0:T(8,128)(2,1)S(1)}, u32[]{:S(2)}, u32[]{:S(2)}) collective-permute-start(bf16[256,256]{1,0:T(8,128)(2,1)S(1)} %collective-permute-done.12.refs_2_), channel_id=1, source_target_pairs={{0,16},{16,0},{32,48},{48,32},{64,80},{80,64},{96,112},{112,96},{1... | collective-permute-start | bytes 393224 | tf_op jit(solution)/shard_map/ppermute | solution.py:60
  126.8 1.4 %collective-permute-start.15 = (bf16[256,256]{1,0:T(8,128)(2,1)S(1)}, bf16[256,256]{1,0:T(8,128)(2,1)S(1)}, u32[]{:S(2)}, u32[]{:S(2)}) collective-permute-start(bf16[256,256]{1,0:T(8,128)(2,1)S(1)} %collective-permute-done.11.refs_1_), channel_id=1, source_target_pairs={{0,16},{16,0},{32,48},{48,32},{64,80},{80,64},{96,112},{112,96},{1... | collective-permute-start | bytes 393224 | tf_op jit(solution)/shard_map/ppermute | solution.py:60

commit v4 on v3

--- a/solution.py
+++ b/solution.py
@@ -75,33 +75,38 @@
 ORDER = (0, -1, 1, 2)
 
 
-def gather(feat):
-    block = jnp.concatenate([feat] + [shift_plane(feat, True, d) for d in (1, 3, 2)], 0)
-    left, right = shift_plane(block, False, 1), shift_plane(block, False, 3)
-    n = block.shape[0] // 2
-    return [block, left, right, shift_plane(left[:n], False, 1), shift_plane(right[n:], False, 3)]
-
-
-def prep_body(cent_ref, list_ref, raw_ref, sems):
+def gather(feat, own):
+    came = [shift_plane(feat, True, d) for d in (1, 3, 2)]
+    low, high = jnp.concatenate([own, came[0]], 0), jnp.concatenate(came[1:], 0)
+    left_low, right_high = shift_plane(low, False, 1), shift_plane(high, False, 3)
+    left_high, right_low = shift_plane(high, False, 1), shift_plane(low, False, 3)
+    far = [shift_plane(left_low, False, 1), shift_plane(right_high, False, 3)]
+    return [low, high, left_low, left_high, right_low, right_high] + far
+
+
+def prep_body(cent_ref, feat_ref, list_ref, own_ref, raw_ref, sems):
     parts = [pl.ds(512 * m, 512) for m in range(4)]
     copies = [pltpu.make_async_copy(cent_ref.at[p, :], raw_ref.at[p, :], sems.at[m]) for m, p in enumerate(parts)]
+    copies.append(pltpu.make_async_copy(feat_ref, own_ref, sems.at[4]))
     for copy in copies:
         copy.start()
     for copy, p in zip(copies, parts):
         copy.wait()
         list_ref[p, :] = unit(raw_ref[p, :].astype(F32), 1).astype(BF16)
-
-
-def prep(cent):
+    copies[4].wait()
+
+
+def prep(cent, feat):
     return pl.pallas_call(
         prep_body,
-        out_shape=VMEM((LIST_DEV, E), BF16),
-        in_specs=[pl.BlockSpec(memory_space=pl.ANY)],
-        out_specs=whole(1)[0],
-        scratch_shapes=[VMEM((LIST_DEV, E), BF16), pltpu.SemaphoreType.DMA((4,))],
+        out_shape=(VMEM((LIST_DEV, E), BF16), VMEM(feat.shape, BF16)),
+        in_specs=[pl.BlockSpec(memory_space=pltpu.HBM)] * 2,
+        out_specs=tuple(whole(2)),
+        scratch_shapes=[VMEM((LIST_DEV, E), BF16), pltpu.SemaphoreType.DMA((5,))],
         compiler_params=pltpu.CompilerParams(vmem_limit_bytes=4 << 20),
+        cost_estimate=pl.CostEstimate(flops=1 << 20, bytes_accessed=1 << 21, transcendentals=0),
         name="lists",
-    )(cent)
+    )(cent, feat)
 
 
 def put_rows(total, out_ref):
@@ -112,15 +117,12 @@
 TILE_M = 256
 
 
-def gen_body(list_ref, own_ref, left_ref, right_ref, low_ref, high_ref, *refs):
-    *kern_refs, item_ref, rows_ref, feat_ref = refs
+def gen_body(list_ref, *refs):
+    piece_refs, (*kern_refs, item_ref, rows_ref, feat_ref) = refs[:8], refs[8:]
     core, _, y, x = place()
     for i, outer in enumerate(ORDER):
         for j, inner in enumerate(ORDER):
-            if i < 3:
-                block = (own_ref, left_ref, right_ref)[i][16 * j : 16 * (j + 1), :]
-            else:
-                block = (low_ref, high_ref)[j // 2][16 * (j % 2) : 16 * (j % 2 + 1), :]
+            block = piece_refs[2 * i + j // 2][16 * (j % 2) : 16 * (j % 2 + 1), :]
             from_y = (y + jnp.where(core == 0, outer, inner) + 4) % 4
             from_x = (x + jnp.where(core == 0, inner, outer) + 4) % 4
             spot = from_y * 4 + from_x
@@ -324,8 +326,9 @@
 def local(items, item_weight, list_capacity, centroids):
     weight = item_weight.reshape(32, 128)
     cap = list_capacity.reshape(16, 128)
-    lists = prep(centroids)
-    *kern, item, parts = gen(lists, gather(items.T))
+    feat = items.T
+    lists, own = prep(centroids, feat)
+    *kern, item, parts = gen(lists, gather(feat, own))
 
     for step in range(ITERS - 1):
         parts = lax.all_to_all(parts, "list", 0, 0)

time: 130 us -> 125 us (0.962)
  waiting for transfers between devices: 22.4 us -> 14.6 us
  starting transfers between devices: 27.5 us -> 30.1 us
    ppermute x7 -> x9, waiting for transfers between devices: 15.1 us -> 7.39 us  [shift_plane(): return lax.ppermute(block, ('item', 'list'), pairs)]
    ppermute x7 -> x9, starting transfers between devices: 11.3 us -> 13.7 us  [shift_plane(): return lax.ppermute(block, ('item', 'list'), pairs)]
  transfers between devices with their start and end apart: 18 -> 20, of which waited for: 13 -> 11; matrix products, arithmetic and copies ran while one was open for 0% -> 0% of each run, Pallas kernels for 2% -> 3%
where the time goes in v4:
time: 125 us
  blocking collectives  54.4 us (44%)
  starting transfers between devices  30.1 us (24%)
  Pallas kernels  23.1 us (18%)
  waiting for transfers between devices  14.6 us (12%)
  local copies, waits for them, and re-layouts  2.18 us (2%)
    all_to_all x3, blocking collectives, local(): parts = lax.all_to_all(parts, 'list', 0, 0)  30 us
    all_to_all x2, blocking collectives, local(): cols = lax.all_to_all(col_pass(kern, parts, weight), 'item', 0, 0)  24.4 us
    pallas_call x9, Pallas kernels, call(): pl.pallas_call(body, out_shape=out, in_specs=whole(len(args)), out_specs=...  21.1 us
    ppermute x9, starting transfers between devices, shift_plane(): return lax.ppermute(block, ('item', 'list'), pairs)  13.7 us
    ppermute x5, starting transfers between devices, swap_core(): return lax.ppermute(block, 'item', [(i, i ^ 1) for i in range(N_ITEM)])  9.74 us
    ppermute x9, waiting for transfers between devices, shift_plane(): return lax.ppermute(block, ('item', 'list'), pairs)  7.39 us
    ppermute x6, starting transfers between devices, shift_z(): lax.ppermute(block, 'item', [(i, (i + 2 * step) % N_ITEM) for i in range(...  6.68 us
    ppermute x6, waiting for transfers between devices, shift_z(): lax.ppermute(block, 'item', [(i, (i + 2 * step) % N_ITEM) for i in range(...  6.24 us
  transfers between devices with their start and end apart: 20, of which 11 were waited for; matrix products, arithmetic and copies ran while one was open for 0% of the time, Pallas kernels for 3%

profile of v4, /device:TPU:1, one launch (start us, length us, event | category | flops | bytes accessed | tf_op | source)
XLA Modules:
  0.0 124.7 jit_solution(17745898781931732590)
XLA Ops:
  0.0 3.7 %collective-permute-start.2 = (bf16[16,4096]{1,0:T(8,128)(2,1)}, bf16[16,4096]{1,0:T(8,128)(2,1)S(1)}, u32[]{:S(2)}, u32[]{:S(2)}) collective-permute-start(bf16[16,4096]{1,0:T(8,128)(2,1)} %bitcast.7), channel_id=1, source_target_pairs={{0,2},{1,3},{2,0},{3,1},{4,6},{5,7},{6,4},{7,5},{8,10},{9,11},{10,... | collective-permute-start | bytes 393224 | tf_op jit(solution)/shard_map/ppermute | solution.py:72
  3.7 0.8 collective-permute-start.1
  4.5 0.7 collective-permute-start
  5.2 1.2 copy-done
  6.4 0.9 copy-done.2
  7.3 0.9 lists.1
  8.3 0.1 collective-permute-done.1
  8.5 2.5 %collective-permute-start.6 = (bf16[32,4096]{1,0:T(8,128)(2,1)S(1)}, bf16[32,4096]{1,0:T(8,128)(2,1)S(1)}, u32[]{:S(2)}, u32[]{:S(2)}) collective-permute-start(bf16[32,4096]{1,0:T(8,128)(2,1)S(1)} %constant_dynamic-update-slice_fusion.2.refs_1_), channel_id=1, source_target_pairs={{0,12},{1,13},{2,14},{3,15},{4,0},{5,1},{6,2},{7,3},{8,4},{9,5},{1... | collective-permute-start | bytes 786440 | tf_op jit(solution)/shard_map/ppermute | solution.py:72
  11.0 0.1 collective-permute-start.3
  11.1 1.2 collective-permute-start.4
  12.3 1.6 %collective-permute-start.5 = (bf16[32,4096]{1,0:T(8,128)(2,1)S(1)}, bf16[32,4096]{1,0:T(8,128)(2,1)S(1)}, u32[]{:S(2)}, u32[]{:S(2)}) collective-permute-start(bf16[32,4096]{1,0:T(8,128)(2,1)S(1)} %constant_dynamic-update-slice_fusion.refs_0_), channel_id=1, source_target_pairs={{0,12},{1,13},{2,14},{3,15},{4,0},{5,1},{6,2},{7,3},{8,4},{9,5},{1... | collective-permute-start | bytes 786440 | tf_op jit(solution)/shard_map/ppermute | solution.py:72
  13.9 0.5 collective-permute-done.6.refs_5_
  14.3 3.1 %collective-permute-start.8 = (bf16[32,4096]{1,0:T(8,128)(2,1)S(1)}, bf16[32,4096]{1,0:T(8,128)(2,1)S(1)}, u32[]{:S(2)}, u32[]{:S(2)}) collective-permute-start(bf16[32,4096]{1,0:T(8,128)(2,1)S(1)} %collective-permute-done.6.refs_5_), channel_id=1, source_target_pairs={{0,12},{1,13},{2,14},{3,15},{4,0},{5,1},{6,2},{7,3},{8,4},{9,5},{1... | collective-permute-start | bytes 786440 | tf_op jit(solution)/shard_map/ppermute | solution.py:72
  17.4 0.4 collective-permute-done.3.refs_2_
  17.8 2.8 %collective-permute-done.4.refs_3_ = bf16[32,4096]{1,0:T(8,128)(2,1)S(1)} collective-permute-done((bf16[32,4096]{1,0:T(8,128)(2,1)S(1)}, bf16[32,4096]{1,0:T(8,128)(2,1)S(1)}, u32[]{:S(2)}, u32[]{:S(2)}) %collective-permute-start.4) | collective-permute-done | bytes 262176 | tf_op jit(solution)/shard_map/ppermute | solution.py:72
  20.6 0.1 collective-permute-done.8.refs_7_
  20.8 3.5 %collective-permute-done.7.refs_6_ = bf16[32,4096]{1,0:T(8,128)(2,1)S(1)} collective-permute-done((bf16[32,4096]{1,0:T(8,128)(2,1)S(1)}, bf16[32,4096]{1,0:T(8,128)(2,1)S(1)}, u32[]{:S(2)}, u32[]{:S(2)}) %collective-permute-start.7) | collective-permute-done | bytes 262176 | tf_op jit(solution)/shard_map/ppermute | solution.py:72
  24.3 5.6 %generate.1 = (f32[2048,1024]{1,0:T(8,128)S(1)}, f32[2048,1024]{1,0:T(8,128)S(1)}, f32[2048,1024]{1,0:T(8,128)S(1)}, f32[2048,1024]{1,0:T(8,128)S(1)}, bf16[4096...) custom-call(bf16[2048,256]{1,0:T(8,128)(2,1)S(1)} %get-tuple-element.17.list_ref, ...), custom_call_target="tpu_custom_call" | custom-call | flops 4294967296 | bytes 1048576 | tf_op jit(solution)/shard_map/generate/pallas_call | solution.py:32
  29.8 10.6 %all_to_all.25.refs_4_ = bf16[16,32,128]{2,1,0:T(8,128)(2,1)S(1)} all-to-all(bf16[16,32,128]{2,1,0:T(8,128)(2,1)S(1)} %get-tuple-element.24), channel_id=1, replica_groups=mesh['item'=8,'list'=16] {'list'}, dimensions={0} | all-to-all | bytes 262144 | tf_op jit(solution)/shard_map/all_to_all | solution.py:334
  40.5 2.3 %columns.2 = f32[8,16,128]{2,1,0:T(8,128)S(1)} custom-call(f32[2048,1024]{1,0:T(8,128)S(1)} %get-tuple-element.19.refs_0_, f32[2048,1024]{1,0:T(8,128)S(1)} %get-tuple-element.20.refs_1_, f32[2048,1024]{1,0:T(8,128)S(1)} %get-tuple-element.21.refs_2_, f32[2048,1024]{1,0:T(8,128)S(1)} %get-tuple-element.22.refs_3_, ...), custom_call_target="tpu_custom_call" | custom-call | flops 16777216 | bytes 1048576 | tf_op jit(solution)/shard_map/columns/pallas_call | solution.py:32
  42.8 15.0 %all_to_all.26.refs_4_ = f32[8,16,128]{2,1,0:T(8,128)S(1)} all-to-all(f32[8,16,128]{2,1,0:T(8,128)S(1)} %columns.2), channel_id=1, replica_groups=mesh['item'=8,'list'=16] {'item'}, dimensions={0} | all-to-all | bytes 131072 | tf_op jit(solution)/shard_map/all_to_all | solution.py:335
  57.8 2.9 %rows.2 = bf16[16,32,128]{2,1,0:T(8,128)(2,1)S(1)} custom-call(f32[2048,1024]{1,0:T(8,128)S(1)} %get-tuple-element.19.refs_0_, f32[2048,1024]{1,0:T(8,128)S(1)} %get-tuple-element.20.refs_1_, f32[2048,1024]{1,0:T(8,128)S(1)} %get-tuple-element.21.refs_2_, f32[2048,1024]{1,0:T(8,128)S(1)} %get-tuple-element.22.refs_3_, f32[8,16,128]{2,1,0:T(8,128)S(1)} %all_to_all.26.refs_4_, ...), custom_call_target="tpu_custom_call" | custom-call | flops 16777216 | bytes 1048576 | tf_op jit(solution)/shard_map/rows/pallas_call | solution.py:32
  60.7 9.7 %all_to_all.27.refs_4_ = bf16[16,32,128]{2,1,0:T(8,128)(2,1)S(1)} all-to-all(bf16[16,32,128]{2,1,0:T(8,128)(2,1)S(1)} %rows.2), channel_id=1, replica_groups=mesh['item'=8,'list'=16] {'list'}, dimensions={0} | all-to-all | bytes 262144 | tf_op jit(solution)/shard_map/all_to_all | solution.py:334
  70.3 2.3 %columns.3 = f32[8,16,128]{2,1,0:T(8,128)S(1)} custom-call(f32[2048,1024]{1,0:T(8,128)S(1)} %get-tuple-element.19.refs_0_, f32[2048,1024]{1,0:T(8,128)S(1)} %get-tuple-element.20.refs_1_, f32[2048,1024]{1,0:T(8,128)S(1)} %get-tuple-element.21.refs_2_, f32[2048,1024]{1,0:T(8,128)S(1)} %get-tuple-element.22.refs_3_, ...), custom_call_target="tpu_custom_call" | custom-call | flops 16777216 | bytes 1048576 | tf_op jit(solution)/shard_map/columns/pallas_call | solution.py:32
  72.6 9.4 %all_to_all.28.refs_4_ = f32[8,16,128]{2,1,0:T(8,128)S(1)} all-to-all(f32[8,16,128]{2,1,0:T(8,128)S(1)} %columns.3), channel_id=1, replica_groups=mesh['item'=8,'list'=16] {'item'}, dimensions={0} | all-to-all | bytes 131072 | tf_op jit(solution)/shard_map/all_to_all | solution.py:335
  82.0 2.9 %rows.3 = bf16[16,32,128]{2,1,0:T(8,128)(2,1)S(1)} custom-call(f32[2048,1024]{1,0:T(8,128)S(1)} %get-tuple-element.19.refs_0_, f32[2048,1024]{1,0:T(8,128)S(1)} %get-tuple-element.20.refs_1_, f32[2048,1024]{1,0:T(8,128)S(1)} %get-tuple-element.21.refs_2_, f32[2048,1024]{1,0:T(8,128)S(1)} %get-tuple-element.22.refs_3_, f32[8,16,128]{2,1,0:T(8,128)S(1)} %all_to_all.28.refs_4_, ...), custom_call_target="tpu_custom_call" | custom-call | flops 16777216 | bytes 1048576 | tf_op jit(solution)/shard_map/rows/pallas_call | solution.py:32
  84.9 9.7 %all_to_all.29.refs_5_ = bf16[16,32,128]{2,1,0:T(8,128)(2,1)S(1)} all-to-all(bf16[16,32,128]{2,1,0:T(8,128)(2,1)S(1)} %rows.3), channel_id=1, replica_groups=mesh['item'=8,'list'=16] {'list'}, dimensions={0} | all-to-all | bytes 262144 | tf_op jit(solution)/shard_map/all_to_all | solution.py:337
  94.6 2.4 %totals.3 = bf16[1088,256]{1,0:T(8,128)(2,1)S(1)} custom-call(f32[2048,1024]{1,0:T(8,128)S(1)} %get-tuple-element.19.refs_0_, f32[2048,1024]{1,0:T(8,128)S(1)} %get-tuple-element.20.refs_1_, f32[2048,1024]{1,0:T(8,128)S(1)} %get-tuple-element.21.refs_2_, f32[2048,1024]{1,0:T(8,128)S(1)} %get-tuple-element.22.refs_3_, ...), custom_call_target="tpu_custom_call" | custom-call | flops 2147483648 | bytes 1048576 | tf_op jit(solution)/shard_map/totals/pallas_call | solution.py:32
  97.0 2.2 %collective-permute-start.9 = (bf16[1088,256]{1,0:T(8,128)(2,1)S(1)}, bf16[1088,256]{1,0:T(8,128)(2,1)S(1)}, u32[]{:S(2)}, u32[]{:S(2)}) collective-permute-start(bf16[1088,256]{1,0:T(8,128)(2,1)S(1)} %totals.3), channel_id=1, source_target_pairs={{0,16},{16,0},{32,48},{48,32},{64,80},{80,64},{96,112},{112,96},{1... | collective-permute-start | bytes 1671176 | tf_op jit(solution)/shard_map/ppermute | solution.py:60
  99.2 2.4 %totals.2.stay_ref = bf16[1088,256]{1,0:T(8,128)(2,1)S(1)} custom-call(f32[2048,1024]{1,0:T(8,128)S(1)} %get-tuple-element.19.refs_0_, f32[2048,1024]{1,0:T(8,128)S(1)} %get-tuple-element.20.refs_1_, f32[2048,1024]{1,0:T(8,128)S(1)} %get-tuple-element.21.refs_2_, f32[2048,1024]{1,0:T(8,128)S(1)} %get-tuple-element.22.refs_3_, ...), custom_call_target="tpu_custom_call" | custom-call | flops 2147483648 | bytes 1048576 | tf_op jit(solution)/shard_map/totals/pallas_call | solution.py:32
  101.7 0.2 fold.1
  101.8 0.6 collective-permute-start.10
  102.4 2.4 %collective-permute-start.11 = (bf16[272,256]{1,0:T(8,128)(2,1)S(1)}, bf16[272,256]{1,0:T(8,128)(2,1)S(1)}, u32[]{:S(2)}, u32[]{:S(2)}) collective-permute-start(bf16[272,256]{1,0:T(8,128)(2,1)S(1)} %get-tuple-element.27), channel_id=1, source_target_pairs={{0,96},{16,112},{32,0},{48,16},{64,32},{80,48},{96,64},{112,80},{1... | collective-permute-start | bytes 417800 | tf_op jit(solution)/shard_map/ppermute | solution.py:56
  104.8 3.8 %collective-permute-done.10.a_ref = bf16[272,256]{1,0:T(8,128)(2,1)S(1)} collective-permute-done((bf16[272,256]{1,0:T(8,128)(2,1)S(1)}, bf16[272,256]{1,0:T(8,128)(2,1)S(1)}, u32[]{:S(2)}, u32[]{:S(2)}) %collective-permute-start.10) | collective-permute-done | bytes 139296 | tf_op jit(solution)/shard_map/ppermute | solution.py:56
  108.6 1.8 %collective-permute-done.11.b_ref = bf16[272,256]{1,0:T(8,128)(2,1)S(1)} collective-permute-done((bf16[272,256]{1,0:T(8,128)(2,1)S(1)}, bf16[272,256]{1,0:T(8,128)(2,1)S(1)}, u32[]{:S(2)}, u32[]{:S(2)}) %collective-permute-start.11) | collective-permute-done | bytes 139296 | tf_op jit(solution)/shard_map/ppermute | solution.py:56
  110.4 0.5 collective-permute-done.12.c_ref
  111.0 0.2 finish.1.refs_0_
  111.2 1.3 %collective-permute-start.15 = (bf16[256,256]{1,0:T(8,128)(2,1)S(1)}, bf16[256,256]{1,0:T(8,128)(2,1)S(1)}, u32[]{:S(2)}, u32[]{:S(2)}) collective-permute-start(bf16[256,256]{1,0:T(8,128)(2,1)S(1)} %finish.1.refs_0_), channel_id=1, source_target_pairs={{0,64},{16,80},{32,96},{48,112},{64,0},{80,16},{96,32},{112,48},{1... | collective-permute-start | bytes 393224 | tf_op jit(solution)/shard_map/ppermute | solution.py:56
  112.5 2.4 %collective-permute-start.14 = (bf16[256,256]{1,0:T(8,128)(2,1)S(1)}, bf16[256,256]{1,0:T(8,128)(2,1)S(1)}, u32[]{:S(2)}, u32[]{:S(2)}) collective-permute-start(bf16[256,256]{1,0:T(8,128)(2,1)S(1)} %finish.1.refs_0_), channel_id=1, source_target_pairs={{0,96},{16,112},{32,0},{48,16},{64,32},{80,48},{96,64},{112,80},{1... | collective-permute-start | bytes 393224 | tf_op jit(solution)/shard_map/ppermute | solution.py:56
  114.9 1.6 %collective-permute-start.16 = (bf16[256,256]{1,0:T(8,128)(2,1)S(1)}, bf16[256,256]{1,0:T(8,128)(2,1)S(1)}, u32[]{:S(2)}, u32[]{:S(2)}) collective-permute-start(bf16[256,256]{1,0:T(8,128)(2,1)S(1)} %finish.1.refs_0_), channel_id=1, source_target_pairs={{0,16},{16,0},{32,48},{48,32},{64,80},{80,64},{96,112},{112,96},{1... | collective-permute-start | bytes 393224 | tf_op jit(solution)/shard_map/ppermute | solution.py:60
  116.5 0.0 collective-permute-done.15.refs_3_
  116.6 3.6 %collective-permute-start.19 = (bf16[256,256]{1,0:T(8,128)(2,1)S(1)}, bf16[256,256]{1,0:T(8,128)(2,1)S(1)}, u32[]{:S(2)}, u32[]{:S(2)}) collective-permute-start(bf16[256,256]{1,0:T(8,128)(2,1)S(1)} %collective-permute-done.15.refs_3_), channel_id=1, source_target_pairs={{0,16},{16,0},{32,48},{48,32},{64,80},{80,64},{96,112},{112,96},{1... | collective-permute-start | bytes 393224 | tf_op jit(solution)/shard_map/ppermute | solution.py:60
  120.1 0.0 collective-permute-done.14.refs_2_
  120.2 1.9 %collective-permute-start.18 = (bf16[256,256]{1,0:T(8,128)(2,1)S(1)}, bf16[256,256]{1,0:T(8,128)(2,1)S(1)}, u32[]{:S(2)}, u32[]{:S(2)}) collective-permute-start(bf16[256,256]{1,0:T(8,128)(2,1)S(1)} %collective-permute-done.14.refs_2_), channel_id=1, source_target_pairs={{0,16},{16,0},{32,48},{48,32},{64,80},{80,64},{96,112},{112,96},{1... | collective-permute-start | bytes 393224 | tf_op jit(solution)/shard_map/ppermute | solution.py:60
  122.1 0.4 collective-permute-start.17
  122.5 0.6 collective-permute-done.18.refs_6_
  123.1 0.4 collective-permute-done.17.refs_5_
  123.5 1.0 lay.1
  (20 shorter events, 0.1 us)
Async XLA Ops:
  0.0 8.4 %collective-permute-start.2 = (bf16[16,4096]{1,0:T(8,128)(2,1)}, bf16[16,4096]{1,0:T(8,128)(2,1)S(1)}, u32[]{:S(2)}, u32[]{:S(2)}) collective-permute-start(bf16[16,4096]{1,0:T(8,128)(2,1)} %bitcast.7), channel_id=1, source_target_pairs={{0,2},{1,3},{2,0},{3,1},{4,6},{5,7},{6,4},{7,5},{8,10},{9,11},{10,... | collective-permute-start | bytes 393224 | tf_op jit(solution)/shard_map/ppermute | solution.py:72
  3.7 4.7 %collective-permute-start.1 = (bf16[16,4096]{1,0:T(8,128)(2,1)}, bf16[16,4096]{1,0:T(8,128)(2,1)S(1)}, u32[]{:S(2)}, u32[]{:S(2)}) collective-permute-start(bf16[16,4096]{1,0:T(8,128)(2,1)} %bitcast.8), channel_id=1, source_target_pairs={{0,3},{1,0},{2,1},{3,2},{4,7},{5,4},{6,5},{7,6},{8,11},{9,8},{10,9... | collective-permute-start | bytes 393224 | tf_op jit(solution)/shard_map/ppermute | solution.py:72
  4.5 6.5 %collective-permute-start = (bf16[16,4096]{1,0:T(8,128)(2,1)}, bf16[16,4096]{1,0:T(8,128)(2,1)S(1)}, u32[]{:S(2)}, u32[]{:S(2)}) collective-permute-start(bf16[16,4096]{1,0:T(8,128)(2,1)} %bitcast.9), channel_id=1, source_target_pairs={{0,1},{1,2},{2,3},{3,0},{4,5},{5,6},{6,7},{7,4},{8,9},{9,10},{10,1... | collective-permute-start | bytes 393224 | tf_op jit(solution)/shard_map/ppermute | solution.py:72
  5.2 1.2 copy-start
  6.4 0.9 copy-start.2
  8.4 32.1 %copy-start.1 = (f32[4096]{0:T(1024)S(1)}, f32[4096]{0:T(1024)}, u32[]{:S(2)}) copy-start(f32[4096]{0:T(1024)} %param.5) | copy-start | bytes 49156
  8.5 5.9 %collective-permute-start.6 = (bf16[32,4096]{1,0:T(8,128)(2,1)S(1)}, bf16[32,4096]{1,0:T(8,128)(2,1)S(1)}, u32[]{:S(2)}, u32[]{:S(2)}) collective-permute-start(bf16[32,4096]{1,0:T(8,128)(2,1)S(1)} %constant_dynamic-update-slice_fusion.2.refs_1_), channel_id=1, source_target_pairs={{0,12},{1,13},{2,14},{3,15},{4,0},{5,1},{6,2},{7,3},{8,4},{9,5},{1... | collective-permute-start | bytes 786440 | tf_op jit(solution)/shard_map/ppermute | solution.py:72
  11.0 6.8 %collective-permute-start.3 = (bf16[32,4096]{1,0:T(8,128)(2,1)S(1)}, bf16[32,4096]{1,0:T(8,128)(2,1)S(1)}, u32[]{:S(2)}, u32[]{:S(2)}) collective-permute-start(bf16[32,4096]{1,0:T(8,128)(2,1)S(1)} %constant_dynamic-update-slice_fusion.refs_0_), channel_id=1, source_target_pairs={{0,4},{1,5},{2,6},{3,7},{4,8},{5,9},{6,10},{7,11},{8,12},{9,13},{1... | collective-permute-start | bytes 786440 | tf_op jit(solution)/shard_map/ppermute | solution.py:72
  11.1 9.5 %collective-permute-start.4 = (bf16[32,4096]{1,0:T(8,128)(2,1)S(1)}, bf16[32,4096]{1,0:T(8,128)(2,1)S(1)}, u32[]{:S(2)}, u32[]{:S(2)}) collective-permute-start(bf16[32,4096]{1,0:T(8,128)(2,1)S(1)} %constant_dynamic-update-slice_fusion.2.refs_1_), channel_id=1, source_target_pairs={{0,4},{1,5},{2,6},{3,7},{4,8},{5,9},{6,10},{7,11},{8,12},{9,13},{1... | collective-permute-start | bytes 786440 | tf_op jit(solution)/shard_map/ppermute | solution.py:72
  12.3 8.4 %collective-permute-start.5 = (bf16[32,4096]{1,0:T(8,128)(2,1)S(1)}, bf16[32,4096]{1,0:T(8,128)(2,1)S(1)}, u32[]{:S(2)}, u32[]{:S(2)}) collective-permute-start(bf16[32,4096]{1,0:T(8,128)(2,1)S(1)} %constant_dynamic-update-slice_fusion.refs_0_), channel_id=1, source_target_pairs={{0,12},{1,13},{2,14},{3,15},{4,0},{5,1},{6,2},{7,3},{8,4},{9,5},{1... | collective-permute-start | bytes 786440 | tf_op jit(solution)/shard_map/ppermute | solution.py:72
  14.3 6.4 %collective-permute-start.8 = (bf16[32,4096]{1,0:T(8,128)(2,1)S(1)}, bf16[32,4096]{1,0:T(8,128)(2,1)S(1)}, u32[]{:S(2)}, u32[]{:S(2)}) collective-permute-start(bf16[32,4096]{1,0:T(8,128)(2,1)S(1)} %collective-permute-done.6.refs_5_), channel_id=1, source_target_pairs={{0,12},{1,13},{2,14},{3,15},{4,0},{5,1},{6,2},{7,3},{8,4},{9,5},{1... | collective-permute-start | bytes 786440 | tf_op jit(solution)/shard_map/ppermute | solution.py:72
  17.8 6.4 %collective-permute-start.7 = (bf16[32,4096]{1,0:T(8,128)(2,1)S(1)}, bf16[32,4096]{1,0:T(8,128)(2,1)S(1)}, u32[]{:S(2)}, u32[]{:S(2)}) collective-permute-start(bf16[32,4096]{1,0:T(8,128)(2,1)S(1)} %collective-permute-done.3.refs_2_), channel_id=1, source_target_pairs={{0,4},{1,5},{2,6},{3,7},{4,8},{5,9},{6,10},{7,11},{8,12},{9,13},{1... | collective-permute-start | bytes 786440 | tf_op jit(solution)/shard_map/ppermute | solution.py:72
  40.5 17.3 %copy-start.3 = (f32[2048]{0:T(1024)S(1)}, f32[2048]{0:T(1024)}, u32[]{:S(2)}) copy-start(f32[2048]{0:T(1024)} %param.6) | copy-start | bytes 24580
  97.0 4.7 %collective-permute-start.9 = (bf16[1088,256]{1,0:T(8,128)(2,1)S(1)}, bf16[1088,256]{1,0:T(8,128)(2,1)S(1)}, u32[]{:S(2)}, u32[]{:S(2)}) collective-permute-start(bf16[1088,256]{1,0:T(8,128)(2,1)S(1)} %totals.3), channel_id=1, source_target_pairs={{0,16},{16,0},{32,48},{48,32},{64,80},{80,64},{96,112},{112,96},{1... | collective-permute-start | bytes 1671176 | tf_op jit(solution)/shard_map/ppermute | solution.py:60
  101.8 6.8 %collective-permute-start.10 = (bf16[272,256]{1,0:T(8,128)(2,1)S(1)}, bf16[272,256]{1,0:T(8,128)(2,1)S(1)}, u32[]{:S(2)}, u32[]{:S(2)}) collective-permute-start(bf16[272,256]{1,0:T(8,128)(2,1)S(1)} %get-tuple-element.26), channel_id=1, source_target_pairs={{0,32},{16,48},{32,64},{48,80},{64,96},{80,112},{96,0},{112,16},{1... | collective-permute-start | bytes 417800 | tf_op jit(solution)/shard_map/ppermute | solution.py:56
  102.4 8.0 %collective-permute-start.11 = (bf16[272,256]{1,0:T(8,128)(2,1)S(1)}, bf16[272,256]{1,0:T(8,128)(2,1)S(1)}, u32[]{:S(2)}, u32[]{:S(2)}) collective-permute-start(bf16[272,256]{1,0:T(8,128)(2,1)S(1)} %get-tuple-element.27), channel_id=1, source_target_pairs={{0,96},{16,112},{32,0},{48,16},{64,32},{80,48},{96,64},{112,80},{1... | collective-permute-start | bytes 417800 | tf_op jit(solution)/shard_map/ppermute | solution.py:56
  104.8 6.1 %collective-permute-start.12 = (bf16[272,256]{1,0:T(8,128)(2,1)S(1)}, bf16[272,256]{1,0:T(8,128)(2,1)S(1)}, u32[]{:S(2)}, u32[]{:S(2)}) collective-permute-start(bf16[272,256]{1,0:T(8,128)(2,1)S(1)} %get-tuple-element.28), channel_id=1, source_target_pairs={{0,64},{16,80},{32,96},{48,112},{64,0},{80,16},{96,32},{112,48},{1... | collective-permute-start | bytes 417800 | tf_op jit(solution)/shard_map/ppermute | solution.py:56
  111.2 5.4 %collective-permute-start.15 = (bf16[256,256]{1,0:T(8,128)(2,1)S(1)}, bf16[256,256]{1,0:T(8,128)(2,1)S(1)}, u32[]{:S(2)}, u32[]{:S(2)}) collective-permute-start(bf16[256,256]{1,0:T(8,128)(2,1)S(1)} %finish.1.refs_0_), channel_id=1, source_target_pairs={{0,64},{16,80},{32,96},{48,112},{64,0},{80,16},{96,32},{112,48},{1... | collective-permute-start | bytes 393224 | tf_op jit(solution)/shard_map/ppermute | solution.py:56
  112.5 7.7 %collective-permute-start.14 = (bf16[256,256]{1,0:T(8,128)(2,1)S(1)}, bf16[256,256]{1,0:T(8,128)(2,1)S(1)}, u32[]{:S(2)}, u32[]{:S(2)}) collective-permute-start(bf16[256,256]{1,0:T(8,128)(2,1)S(1)} %finish.1.refs_0_), channel_id=1, source_target_pairs={{0,96},{16,112},{32,0},{48,16},{64,32},{80,48},{96,64},{112,80},{1... | collective-permute-start | bytes 393224 | tf_op jit(solution)/shard_map/ppermute | solution.py:56
  114.9 7.2 %collective-permute-start.13 = (bf16[256,256]{1,0:T(8,128)(2,1)S(1)}, bf16[256,256]{1,0:T(8,128)(2,1)S(1)}, u32[]{:S(2)}, u32[]{:S(2)}) collective-permute-start(bf16[256,256]{1,0:T(8,128)(2,1)S(1)} %finish.1.refs_0_), channel_id=1, source_target_pairs={{0,32},{16,48},{32,64},{48,80},{64,96},{80,112},{96,0},{112,16},{1... | collective-permute-start | bytes 393224 | tf_op jit(solution)/shard_map/ppermute | solution.py:56
  114.9 7.6 %collective-permute-start.16 = (bf16[256,256]{1,0:T(8,128)(2,1)S(1)}, bf16[256,256]{1,0:T(8,128)(2,1)S(1)}, u32[]{:S(2)}, u32[]{:S(2)}) collective-permute-start(bf16[256,256]{1,0:T(8,128)(2,1)S(1)} %finish.1.refs_0_), channel_id=1, source_target_pairs={{0,16},{16,0},{32,48},{48,32},{64,80},{80,64},{96,112},{112,96},{1... | collective-permute-start | bytes 393224 | tf_op jit(solution)/shard_map/ppermute | solution.py:60
  116.6 5.9 %collective-permute-start.19 = (bf16[256,256]{1,0:T(8,128)(2,1)S(1)}, bf16[256,256]{1,0:T(8,128)(2,1)S(1)}, u32[]{:S(2)}, u32[]{:S(2)}) collective-permute-start(bf16[256,256]{1,0:T(8,128)(2,1)S(1)} %collective-permute-done.15.refs_3_), channel_id=1, source_target_pairs={{0,16},{16,0},{32,48},{48,32},{64,80},{80,64},{96,112},{112,96},{1... | collective-permute-start | bytes 393224 | tf_op jit(solution)/shard_map/ppermute | solution.py:60
  120.2 2.9 %collective-permute-start.18 = (bf16[256,256]{1,0:T(8,128)(2,1)S(1)}, bf16[256,256]{1,0:T(8,128)(2,1)S(1)}, u32[]{:S(2)}, u32[]{:S(2)}) collective-permute-start(bf16[256,256]{1,0:T(8,128)(2,1)S(1)} %collective-permute-done.14.refs_2_), channel_id=1, source_target_pairs={{0,16},{16,0},{32,48},{48,32},{64,80},{80,64},{96,112},{112,96},{1... | collective-permute-start | bytes 393224 | tf_op jit(solution)/shard_map/ppermute | solution.py:60
  122.1 1.4 %collective-permute-start.17 = (bf16[256,256]{1,0:T(8,128)(2,1)S(1)}, bf16[256,256]{1,0:T(8,128)(2,1)S(1)}, u32[]{:S(2)}, u32[]{:S(2)}) collective-permute-start(bf16[256,256]{1,0:T(8,128)(2,1)S(1)} %collective-permute-done.13.refs_1_), channel_id=1, source_target_pairs={{0,16},{16,0},{32,48},{48,32},{64,80},{80,64},{96,112},{112,96},{1... | collective-permute-start | bytes 393224 | tf_op jit(solution)/shard_map/ppermute | solution.py:60

commit v5 on v4

--- a/solution.py
+++ b/solution.py
@@ -50,10 +50,6 @@
     item = lax.axis_index("item")
     spot = lax.axis_index("list")
     return item % 2, item // 2, spot // 4, spot % 4
-
-
-def shift_z(block, step):
-    return lax.ppermute(block, "item", [(i, (i + 2 * step) % N_ITEM) for i in range(N_ITEM)])
 
 
 def swap_core(block):
@@ -217,71 +213,73 @@
     )
 
 
-TILE_L = 256
-
-
-def last_body(other, *refs):
-    *kern_refs, item_ref, parts_ref, weight_ref, out_ref, scale_ref = refs
-    core, _, _, _ = place()
-    base = (1 - core if other else core) * 1024
-    spread_rows(parts_ref, weight_ref, scale_ref)
-    cols = []
-    for m in range(1024 // TILE_L):
-        at = pl.ds(pl.multiple_of(base + m * TILE_L, TILE_L), TILE_L)
-        total = jnp.zeros((TILE_L // 8, 8, 128), F32)
-        mixed = jnp.zeros((TILE_L, E), F32)
-        for h, ref in enumerate(kern_refs):
-            for n in range(QUART // 256):
-                first = QUART * h + 256 * n
-                block = ref[at, 256 * n : 256 * (n + 1)].reshape(TILE_L // 8, 8, 256)
-                block = block * scale_ref[:, first : first + 256][None]
-                total = total + block[:, :, :128] + block[:, :, 128:]
-                block = block.reshape(TILE_L, 256).astype(BF16)
-                mixed = mixed + jnp.dot(block, item_ref[first : first + 256, :], preferred_element_type=F32)
-        out_ref[TILE_L * m : TILE_L * (m + 1), :] = mixed.astype(BF16)
-        total = total.reshape(TILE_L, 128)
-        cols += [lane(total[128 * t : 128 * (t + 1)]) for t in range(TILE_L // 128)]
-
-    for q in range(4):
-        col = jnp.concatenate(cols[2 * q : 2 * q + 2], 0)
-        high = col.astype(BF16).astype(F32)
-        block = jnp.concatenate([jnp.concatenate([high, col - high], 1), jnp.zeros((14, E), F32)], 0)
-        out_ref[1024 + 16 * q : 1024 + 16 * (q + 1), :] = block.astype(BF16)
-
-
-def last_pass(other, kern, item, parts, weight):
-    return call(
-        functools.partial(last_body, other), (*kern, item, parts, weight), VMEM((1088, E), BF16),
-        [VMEM((8, ITEM_DEV), F32)], "totals", LIST_DEV * ITEM_DEV * E, 4,
-    )
-
-
-AWAY = (0, 1, 3, 2)
-
-
-def fold_body(stay_ref, came_ref, *out_refs):
-    _, z, _, _ = place()
-    for d, out_ref in zip(AWAY, out_refs):
-        q = (z + d) % 4
-        rows = pl.ds(pl.multiple_of(q * 256, 256), 256)
-        tail = pl.ds(pl.multiple_of(1024 + q * 16, 16), 16)
-        out_ref[:256, :] = (stay_ref[rows, :].astype(F32) + came_ref[rows, :].astype(F32)).astype(out_ref.dtype)
-        cols = stay_ref[tail, :].astype(F32) + came_ref[tail, :].astype(F32)
-        cols = cols[:, :128] + cols[:, 128:]
-        high = cols.astype(BF16).astype(F32)
-        out_ref[256:, :] = jnp.concatenate([high, cols - high], 1).astype(out_ref.dtype)
-
-
-def fold(stay, came):
-    out = (VMEM((272, E), F32),) + (VMEM((272, E), BF16),) * 3
-    return call(fold_body, (stay, came), out, [], "fold")
+QROWS = 272
+
+
+def pack(mixed, col, dtype):
+    high = col.astype(BF16).astype(F32)
+    tail = jnp.concatenate([jnp.concatenate([high, col - high], 1), jnp.zeros((14, E), F32)], 0)
+    return jnp.concatenate([mixed, tail], 0).astype(dtype)
+
+
+def unpack(ref, first=0):
+    block = ref[first : first + QROWS, :].astype(F32)
+    return block[:256], block[256:258, :128] + block[256:258, 128:]
+
+
+def quarter(kern_refs, item_ref, scale_ref, half, number):
+    at = pl.ds(pl.multiple_of(half * 1024 + number * 256, 256), 256)
+    total = jnp.zeros((32, 8, 128), F32)
+    mixed = jnp.zeros((256, E), F32)
+    for h, ref in enumerate(kern_refs):
+        for n in range(QUART // 256):
+            first = QUART * h + 256 * n
+            block = ref[at, 256 * n : 256 * (n + 1)].reshape(32, 8, 256)
+            block = block * scale_ref[:, first : first + 256][None]
+            total = total + block[:, :, :128] + block[:, :, 128:]
+            block = block.reshape(256, 256).astype(BF16)
+            mixed = mixed + jnp.dot(block, item_ref[first : first + 256, :], preferred_element_type=F32)
+    total = total.reshape(256, 128)
+    return mixed, jnp.concatenate([lane(total[:128]), lane(total[128:])], 0)
+
+
+def go_body(fars, new, *refs):
+    if new:
+        *kern_refs, item_ref, parts_ref, weight_ref, out_ref, scale_ref = refs
+        spread_rows(parts_ref, weight_ref, scale_ref)
+    else:
+        *kern_refs, item_ref, scale_ref, _, out_ref = refs
+    core, z, _, _ = place()
+    for i, far in enumerate(fars):
+        mixed, col = quarter(kern_refs, item_ref, scale_ref, 1 - core, (z + far) % 4)
+        out_ref[QROWS * i : QROWS * (i + 1), :] = pack(mixed, col, BF16)
+
+
+def go(fars, new, kern, item, *more):
+    out = VMEM((QROWS * len(fars), E), BF16)
+    if new:
+        out = (out, VMEM((8, ITEM_DEV), F32))
+    body = functools.partial(go_body, fars, new)
+    return call(body, (*kern, item, *more), out, [], "totals", LIST_DEV * ITEM_DEV * E)
+
+
+def stay_body(far, first, *refs):
+    *kern_refs, item_ref, scale_ref, came_ref, _, out_ref = refs
+    core, z, _, _ = place()
+    mixed, col = quarter(kern_refs, item_ref, scale_ref, core, (z + far) % 4)
+    came_mixed, came_col = unpack(came_ref, first)
+    out_ref[...] = pack(mixed + came_mixed, col + came_col, out_ref.dtype)
+
+
+def stay(far, first, dtype, kern, item, scale, came, after):
+    body = functools.partial(stay_body, far, first)
+    return call(body, (*kern, item, scale, came, after), VMEM((QROWS, E), dtype), [], "stay", LIST_DEV * ITEM_DEV * E)
 
 
 def finish_body(mine_ref, a_ref, b_ref, c_ref, list_ref, out_ref):
     core, z, _, _ = place()
     first = pl.multiple_of(core * 1024 + z * 256, 256)
-    totals = mine_ref[...] + a_ref[...].astype(F32) + b_ref[...].astype(F32) + c_ref[...].astype(F32)
-    cols = totals[256:, :128] + totals[256:, 128:]
+    totals, cols = (sum(parts) for parts in zip(*(unpack(ref) for ref in (mine_ref, a_ref, b_ref, c_ref))))
     for t in range(2):
         col = jnp.broadcast_to(cols[t : t + 1], (128, 128)).T
         col = jnp.concatenate([col, col], 1)
@@ -290,20 +288,21 @@
         out_ref[128 * t : 128 * (t + 1), :] = unit(mixed, 1).astype(BF16)
 
 
-def finish(pieces, lists):
-    return call(finish_body, (*pieces, lists), VMEM((256, E), BF16), [], "finish")
-
-
-FROM = (0, -1, 1, 2)
-
-
-def lay_body(*refs):
-    blocks, out_ref, sems = refs[:8], refs[8], refs[9]
+def finish(mine, came, lists):
+    return call(finish_body, (mine, *came, lists), VMEM((256, E), BF16), [], "finish")
+
+
+def shift_z(block, step):
+    return lax.ppermute(block, "item", [(i, (i + 2 * step) % N_ITEM) for i in range(N_ITEM)])
+
+
+def lay_body(spots, more, *refs):
+    blocks, (out_ref, sems) = refs[more:-2], refs[-2:]
     core, z, _, _ = place()
     copies = []
-    for i, ref in enumerate(blocks):
-        half = core if i < 4 else 1 - core
-        row = pl.multiple_of(half * 1024 + (z + FROM[i % 4] + 4) % 4 * 256, 256)
+    for i, ((back, other), ref) in enumerate(zip(spots, blocks)):
+        half = 1 - core if other else core
+        row = pl.multiple_of(half * 1024 + (z - back + 4) % 4 * 256, 256)
         copies.append(pltpu.make_async_copy(ref, out_ref.at[pl.ds(row, 256), :], sems.at[i]))
     for copy in copies:
         copy.start()
@@ -311,16 +310,20 @@
         copy.wait()
 
 
-def lay(blocks):
+def lay(spots, blocks, out=None):
+    n = len(spots)
+    more = int(out is not None)
+    place_any = pl.BlockSpec(memory_space=pl.ANY)
     return pl.pallas_call(
-        lay_body,
+        functools.partial(lay_body, spots, more),
         out_shape=jax.ShapeDtypeStruct((LIST_DEV, E), BF16),
-        in_specs=whole(8),
-        out_specs=pl.BlockSpec(memory_space=pl.ANY),
-        scratch_shapes=[pltpu.SemaphoreType.DMA((8,))],
-        compiler_params=pltpu.CompilerParams(vmem_limit_bytes=12 << 20),
+        in_specs=[place_any] * more + whole(n),
+        out_specs=place_any,
+        input_output_aliases={0: 0} if more else {},
+        scratch_shapes=[pltpu.SemaphoreType.DMA((n,))],
+        compiler_params=pltpu.CompilerParams(vmem_limit_bytes=4 << 20),
         name="lay",
-    )(*blocks)
+    )(*([out] if more else []), *blocks)
 
 
 def local(items, item_weight, list_capacity, centroids):
@@ -336,13 +339,20 @@
         parts = row_pass(kern, cols, cap)
     parts = lax.all_to_all(parts, "list", 0, 0)
 
-    came = swap_core(last_pass(True, kern, item, parts, weight))
-    stay = last_pass(False, kern, item, parts, weight)
-    pieces = fold(stay, came)
-    pieces = pieces[:1] + tuple(shift_z(p, d) for d, p in zip(AWAY[1:], pieces[1:]))
-    done = finish(pieces, lists)
-    done = [done] + [shift_z(done, d) for d in AWAY[1:]]
-    return lay(done + [swap_core(d) for d in done])
+    early, scale = go((2, 1), True, kern, item, parts, weight)
+    came_early = swap_core(early)
+    late = go((3, 0), False, kern, item, scale, early)
+    came_late = swap_core(late)
+    held = (kern, item, scale)
+    two = stay(2, 0, BF16, *held, came_early, late)
+    one = stay(1, QROWS, BF16, *held, came_early, two)
+    three = stay(3, 0, BF16, *held, came_late, one)
+    mine = stay(0, QROWS, F32, *held, came_late, three)
+    done = finish(mine, [shift_z(block, d) for block, d in ((two, 2), (one, 1), (three, 3))], lists)
+
+    two, one, three = (shift_z(done, d) for d in (2, 1, 3))
+    out = lay(((0, 0), (2, 0), (1, 0), (0, 1), (2, 1)), (done, two, one, swap_core(done), swap_core(two)))
+    return lay(((3, 0), (1, 1), (3, 1)), (three, swap_core(one), swap_core(three)), out)
 
 
 def solution(mesh):

time: 125 us -> 123 us (0.984)
  waiting for transfers between devices: 14.6 us -> 12 us
  Pallas kernels: 23.1 us -> 25.1 us
    ppermute x6, waiting for transfers between devices: 6.24 us -> 4.51 us  [shift_z(): lax.ppermute(block, 'item', [(i, (i + 2 * step) % N_ITEM) for i in range(...]
    pallas_call x9 -> x12, Pallas kernels: 21.1 us -> 22.5 us  [call(): pl.pallas_call(body, out_shape=out, in_specs=whole(len(args)), out_specs=...]
    ppermute x5 -> x6, starting transfers between devices: 9.74 us -> 9.43 us  [swap_core(): return lax.ppermute(block, 'item', [(i, i ^ 1) for i in range(N_ITEM)])]
  transfers between devices with their start and end apart: 20 -> 21, of which waited for: 11 -> 10; matrix products, arithmetic and copies ran while one was open for 0% -> 0% of each run, Pallas kernels for 3% -> 5%
where the time goes in v5:
time: 123 us
  blocking collectives  54.4 us (44%)
  starting transfers between devices  29 us (24%)
  Pallas kernels  25.1 us (20%)
  waiting for transfers between devices  12 us (10%)
  local copies, waits for them, and re-layouts  2.18 us (2%)
    all_to_all x3, blocking collectives, local(): parts = lax.all_to_all(parts, 'list', 0, 0)  30 us
    all_to_all x2, blocking collectives, local(): cols = lax.all_to_all(col_pass(kern, parts, weight), 'item', 0, 0)  24.4 us
    pallas_call x12, Pallas kernels, call(): pl.pallas_call(body, out_shape=out, in_specs=whole(len(args)), out_specs=...  22.5 us
    ppermute x9, starting transfers between devices, shift_plane(): return lax.ppermute(block, ('item', 'list'), pairs)  13.7 us
    ppermute x6, starting transfers between devices, swap_core(): return lax.ppermute(block, 'item', [(i, i ^ 1) for i in range(N_ITEM)])  9.43 us
    ppermute x9, waiting for transfers between devices, shift_plane(): return lax.ppermute(block, ('item', 'list'), pairs)  7.39 us
    ppermute x6, starting transfers between devices, shift_z(): lax.ppermute(block, 'item', [(i, (i + 2 * step) % N_ITEM) for i in range(...  5.92 us
    ppermute x6, waiting for transfers between devices, shift_z(): lax.ppermute(block, 'item', [(i, (i + 2 * step) % N_ITEM) for i in range(...  4.51 us
  transfers between devices with their start and end apart: 21, of which 10 were waited for; matrix products, arithmetic and copies ran while one was open for 0% of the time, Pallas kernels for 5%

profile of v5, /device:TPU:1, one launch (start us, length us, event | category | flops | bytes accessed | tf_op | source)
XLA Modules:
  0.0 123.0 jit_solution(17290256742158278153)
XLA Ops:
  0.0 3.7 %collective-permute-start.2 = (bf16[16,4096]{1,0:T(8,128)(2,1)}, bf16[16,4096]{1,0:T(8,128)(2,1)S(1)}, u32[]{:S(2)}, u32[]{:S(2)}) collective-permute-start(bf16[16,4096]{1,0:T(8,128)(2,1)} %bitcast.6), channel_id=1, source_target_pairs={{0,2},{1,3},{2,0},{3,1},{4,6},{5,7},{6,4},{7,5},{8,10},{9,11},{10,... | collective-permute-start | bytes 393224 | tf_op jit(solution)/shard_map/ppermute | solution.py:68
  3.7 0.8 collective-permute-start.1
  4.5 0.7 collective-permute-start
  5.2 1.2 copy-done
  6.4 0.9 copy-done.2
  7.3 0.9 lists.1
  8.3 0.1 collective-permute-done.1
  8.5 2.5 %collective-permute-start.6 = (bf16[32,4096]{1,0:T(8,128)(2,1)S(1)}, bf16[32,4096]{1,0:T(8,128)(2,1)S(1)}, u32[]{:S(2)}, u32[]{:S(2)}) collective-permute-start(bf16[32,4096]{1,0:T(8,128)(2,1)S(1)} %constant_dynamic-update-slice_fusion.2.refs_1_), channel_id=1, source_target_pairs={{0,12},{1,13},{2,14},{3,15},{4,0},{5,1},{6,2},{7,3},{8,4},{9,5},{1... | collective-permute-start | bytes 786440 | tf_op jit(solution)/shard_map/ppermute | solution.py:68
  11.1 1.2 collective-permute-start.4
  12.3 1.6 %collective-permute-start.5 = (bf16[32,4096]{1,0:T(8,128)(2,1)S(1)}, bf16[32,4096]{1,0:T(8,128)(2,1)S(1)}, u32[]{:S(2)}, u32[]{:S(2)}) collective-permute-start(bf16[32,4096]{1,0:T(8,128)(2,1)S(1)} %constant_dynamic-update-slice_fusion.refs_0_), channel_id=1, source_target_pairs={{0,12},{1,13},{2,14},{3,15},{4,0},{5,1},{6,2},{7,3},{8,4},{9,5},{1... | collective-permute-start | bytes 786440 | tf_op jit(solution)/shard_map/ppermute | solution.py:68
  13.9 0.5 collective-permute-done.6.refs_5_
  14.3 3.1 %collective-permute-start.8 = (bf16[32,4096]{1,0:T(8,128)(2,1)S(1)}, bf16[32,4096]{1,0:T(8,128)(2,1)S(1)}, u32[]{:S(2)}, u32[]{:S(2)}) collective-permute-start(bf16[32,4096]{1,0:T(8,128)(2,1)S(1)} %collective-permute-done.6.refs_5_), channel_id=1, source_target_pairs={{0,12},{1,13},{2,14},{3,15},{4,0},{5,1},{6,2},{7,3},{8,4},{9,5},{1... | collective-permute-start | bytes 786440 | tf_op jit(solution)/shard_map/ppermute | solution.py:68
  17.4 0.4 collective-permute-done.3.refs_2_
  17.8 2.8 %collective-permute-done.4.refs_3_ = bf16[32,4096]{1,0:T(8,128)(2,1)S(1)} collective-permute-done((bf16[32,4096]{1,0:T(8,128)(2,1)S(1)}, bf16[32,4096]{1,0:T(8,128)(2,1)S(1)}, u32[]{:S(2)}, u32[]{:S(2)}) %collective-permute-start.4) | collective-permute-done | bytes 262176 | tf_op jit(solution)/shard_map/ppermute | solution.py:68
  20.6 0.1 collective-permute-done.8.refs_7_
  20.8 3.5 %collective-permute-done.7.refs_6_ = bf16[32,4096]{1,0:T(8,128)(2,1)S(1)} collective-permute-done((bf16[32,4096]{1,0:T(8,128)(2,1)S(1)}, bf16[32,4096]{1,0:T(8,128)(2,1)S(1)}, u32[]{:S(2)}, u32[]{:S(2)}) %collective-permute-start.7) | collective-permute-done | bytes 262176 | tf_op jit(solution)/shard_map/ppermute | solution.py:68
  24.3 5.6 %generate.1 = (f32[2048,1024]{1,0:T(8,128)S(1)}, f32[2048,1024]{1,0:T(8,128)S(1)}, f32[2048,1024]{1,0:T(8,128)S(1)}, f32[2048,1024]{1,0:T(8,128)S(1)}, bf16[4096...) custom-call(bf16[2048,256]{1,0:T(8,128)(2,1)S(1)} %get-tuple-element.15.list_ref, ...), custom_call_target="tpu_custom_call" | custom-call | flops 4294967296 | bytes 1048576 | tf_op jit(solution)/shard_map/generate/pallas_call | solution.py:32
  29.8 10.6 %all_to_all.25.refs_4_ = bf16[16,32,128]{2,1,0:T(8,128)(2,1)S(1)} all-to-all(bf16[16,32,128]{2,1,0:T(8,128)(2,1)S(1)} %get-tuple-element.22), channel_id=1, replica_groups=mesh['item'=8,'list'=16] {'list'}, dimensions={0} | all-to-all | bytes 262144 | tf_op jit(solution)/shard_map/all_to_all | solution.py:337
  40.5 2.3 %columns.2 = f32[8,16,128]{2,1,0:T(8,128)S(1)} custom-call(f32[2048,1024]{1,0:T(8,128)S(1)} %get-tuple-element.17.refs_0_, f32[2048,1024]{1,0:T(8,128)S(1)} %get-tuple-element.18.refs_1_, f32[2048,1024]{1,0:T(8,128)S(1)} %get-tuple-element.19.refs_2_, f32[2048,1024]{1,0:T(8,128)S(1)} %get-tuple-element.20.refs_3_, ...), custom_call_target="tpu_custom_call" | custom-call | flops 16777216 | bytes 1048576 | tf_op jit(solution)/shard_map/columns/pallas_call | solution.py:32
  42.8 15.0 %all_to_all.26.refs_4_ = f32[8,16,128]{2,1,0:T(8,128)S(1)} all-to-all(f32[8,16,128]{2,1,0:T(8,128)S(1)} %columns.2), channel_id=1, replica_groups=mesh['item'=8,'list'=16] {'item'}, dimensions={0} | all-to-all | bytes 131072 | tf_op jit(solution)/shard_map/all_to_all | solution.py:338
  57.8 2.9 %rows.2 = bf16[16,32,128]{2,1,0:T(8,128)(2,1)S(1)} custom-call(f32[2048,1024]{1,0:T(8,128)S(1)} %get-tuple-element.17.refs_0_, f32[2048,1024]{1,0:T(8,128)S(1)} %get-tuple-element.18.refs_1_, f32[2048,1024]{1,0:T(8,128)S(1)} %get-tuple-element.19.refs_2_, f32[2048,1024]{1,0:T(8,128)S(1)} %get-tuple-element.20.refs_3_, f32[8,16,128]{2,1,0:T(8,128)S(1)} %all_to_all.26.refs_4_, ...), custom_call_target="tpu_custom_call" | custom-call | flops 16777216 | bytes 1048576 | tf_op jit(solution)/shard_map/rows/pallas_call | solution.py:32
  60.7 9.7 %all_to_all.27.refs_4_ = bf16[16,32,128]{2,1,0:T(8,128)(2,1)S(1)} all-to-all(bf16[16,32,128]{2,1,0:T(8,128)(2,1)S(1)} %rows.2), channel_id=1, replica_groups=mesh['item'=8,'list'=16] {'list'}, dimensions={0} | all-to-all | bytes 262144 | tf_op jit(solution)/shard_map/all_to_all | solution.py:337
  70.3 2.3 %columns.3 = f32[8,16,128]{2,1,0:T(8,128)S(1)} custom-call(f32[2048,1024]{1,0:T(8,128)S(1)} %get-tuple-element.17.refs_0_, f32[2048,1024]{1,0:T(8,128)S(1)} %get-tuple-element.18.refs_1_, f32[2048,1024]{1,0:T(8,128)S(1)} %get-tuple-element.19.refs_2_, f32[2048,1024]{1,0:T(8,128)S(1)} %get-tuple-element.20.refs_3_, ...), custom_call_target="tpu_custom_call" | custom-call | flops 16777216 | bytes 1048576 | tf_op jit(solution)/shard_map/columns/pallas_call | solution.py:32
  72.6 9.4 %all_to_all.28.refs_4_ = f32[8,16,128]{2,1,0:T(8,128)S(1)} all-to-all(f32[8,16,128]{2,1,0:T(8,128)S(1)} %columns.3), channel_id=1, replica_groups=mesh['item'=8,'list'=16] {'item'}, dimensions={0} | all-to-all | bytes 131072 | tf_op jit(solution)/shard_map/all_to_all | solution.py:338
  82.0 2.9 %rows.3 = bf16[16,32,128]{2,1,0:T(8,128)(2,1)S(1)} custom-call(f32[2048,1024]{1,0:T(8,128)S(1)} %get-tuple-element.17.refs_0_, f32[2048,1024]{1,0:T(8,128)S(1)} %get-tuple-element.18.refs_1_, f32[2048,1024]{1,0:T(8,128)S(1)} %get-tuple-element.19.refs_2_, f32[2048,1024]{1,0:T(8,128)S(1)} %get-tuple-element.20.refs_3_, f32[8,16,128]{2,1,0:T(8,128)S(1)} %all_to_all.28.refs_4_, ...), custom_call_target="tpu_custom_call" | custom-call | flops 16777216 | bytes 1048576 | tf_op jit(solution)/shard_map/rows/pallas_call | solution.py:32
  84.9 9.7 %all_to_all.29.refs_5_ = bf16[16,32,128]{2,1,0:T(8,128)(2,1)S(1)} all-to-all(bf16[16,32,128]{2,1,0:T(8,128)(2,1)S(1)} %rows.3), channel_id=1, replica_groups=mesh['item'=8,'list'=16] {'list'}, dimensions={0} | all-to-all | bytes 262144 | tf_op jit(solution)/shard_map/all_to_all | solution.py:340
  94.6 1.4 %totals.2 = (bf16[544,256]{1,0:T(8,128)(2,1)S(1)}, f32[8,4096]{1,0:T(8,128)S(1)}) custom-call(f32[2048,1024]{1,0:T(8,128)S(1)} %get-tuple-element.17.refs_0_, f32[2048,1024]{1,0:T(8,128)S(1)} %get-tuple-element.18.refs_1_, f32[2048,1024]{1,0:T(8,128)S(1)} %get-tuple-element.19.refs_2_, f32[2048,1024]{1,0:T(8,128)S(1)} %get-tuple-element.20.refs_3_, ...), custom_call_target="tpu_custom_call" | custom-call | flops 2147483648 | bytes 1048576 | tf_op jit(solution)/shard_map/totals/pallas_call | solution.py:32
  96.0 2.2 %collective-permute-start.10 = (bf16[544,256]{1,0:T(8,128)(2,1)S(1)}, bf16[544,256]{1,0:T(8,128)(2,1)S(1)}, u32[]{:S(2)}, u32[]{:S(2)}) collective-permute-start(bf16[544,256]{1,0:T(8,128)(2,1)S(1)} %get-tuple-element.24.refs_6_), channel_id=1, source_target_pairs={{0,16},{16,0},{32,48},{48,32},{64,80},{80,64},{96,112},{112,96},{1... | collective-permute-start | bytes 835592 | tf_op jit(solution)/shard_map/ppermute | solution.py:56
  98.3 1.5 %totals.3.refs_7_ = bf16[544,256]{1,0:T(8,128)(2,1)S(1)} custom-call(f32[2048,1024]{1,0:T(8,128)S(1)} %get-tuple-element.17.refs_0_, f32[2048,1024]{1,0:T(8,128)S(1)} %get-tuple-element.18.refs_1_, f32[2048,1024]{1,0:T(8,128)S(1)} %get-tuple-element.19.refs_2_, f32[2048,1024]{1,0:T(8,128)S(1)} %get-tuple-element.20.refs_3_, ...), custom_call_target="tpu_custom_call" | custom-call | flops 2147483648 | bytes 1048576 | tf_op jit(solution)/shard_map/totals/pallas_call | solution.py:32
  99.8 0.9 stay.4.refs_7_
  100.7 0.8 collective-permute-start.11
  101.5 0.9 stay.5.refs_7_
  102.4 1.0 collective-permute-start.12
  103.4 0.9 stay.6.refs_7_
  104.3 2.0 %collective-permute-start.13 = (bf16[272,256]{1,0:T(8,128)(2,1)S(1)}, bf16[272,256]{1,0:T(8,128)(2,1)S(1)}, u32[]{:S(2)}, u32[]{:S(2)}) collective-permute-start(bf16[272,256]{1,0:T(8,128)(2,1)S(1)} %stay.6.refs_7_), channel_id=1, source_target_pairs={{0,96},{16,112},{32,0},{48,16},{64,32},{80,48},{96,64},{112,80},{1... | collective-permute-start | bytes 417800 | tf_op jit(solution)/shard_map/ppermute | solution.py:296
  106.3 0.9 stay.7.mine_ref
  107.2 1.4 %collective-permute-done.13.c_ref = bf16[272,256]{1,0:T(8,128)(2,1)S(1)} collective-permute-done((bf16[272,256]{1,0:T(8,128)(2,1)S(1)}, bf16[272,256]{1,0:T(8,128)(2,1)S(1)}, u32[]{:S(2)}, u32[]{:S(2)}) %collective-permute-start.13) | collective-permute-done | bytes 139296 | tf_op jit(solution)/shard_map/ppermute | solution.py:296
  108.6 2.0 %collective-permute-done.12.b_ref = bf16[272,256]{1,0:T(8,128)(2,1)S(1)} collective-permute-done((bf16[272,256]{1,0:T(8,128)(2,1)S(1)}, bf16[272,256]{1,0:T(8,128)(2,1)S(1)}, u32[]{:S(2)}, u32[]{:S(2)}) %collective-permute-start.12) | collective-permute-done | bytes 139296 | tf_op jit(solution)/shard_map/ppermute | solution.py:296
  110.6 0.2 finish.1.refs_0_
  110.8 0.6 collective-permute-start.14
  111.4 1.0 collective-permute-start.18
  112.5 0.4 collective-permute-start.15
  112.9 2.6 %collective-permute-start.16 = (bf16[256,256]{1,0:T(8,128)(2,1)S(1)}, bf16[256,256]{1,0:T(8,128)(2,1)S(1)}, u32[]{:S(2)}, u32[]{:S(2)}) collective-permute-start(bf16[256,256]{1,0:T(8,128)(2,1)S(1)} %finish.1.refs_0_), channel_id=1, source_target_pairs={{0,16},{16,0},{32,48},{48,32},{64,80},{80,64},{96,112},{112,96},{1... | collective-permute-start | bytes 393224 | tf_op jit(solution)/shard_map/ppermute | solution.py:56
  115.5 1.1 collective-permute-done.14.refs_1_
  116.6 3.0 %collective-permute-start.17 = (bf16[256,256]{1,0:T(8,128)(2,1)S(1)}, bf16[256,256]{1,0:T(8,128)(2,1)S(1)}, u32[]{:S(2)}, u32[]{:S(2)}) collective-permute-start(bf16[256,256]{1,0:T(8,128)(2,1)S(1)} %collective-permute-done.14.refs_1_), channel_id=1, source_target_pairs={{0,16},{16,0},{32,48},{48,32},{64,80},{80,64},{96,112},{112,96},{1... | collective-permute-start | bytes 393224 | tf_op jit(solution)/shard_map/ppermute | solution.py:56
  119.6 1.5 %collective-permute-start.19 = (bf16[256,256]{1,0:T(8,128)(2,1)S(1)}, bf16[256,256]{1,0:T(8,128)(2,1)S(1)}, u32[]{:S(2)}, u32[]{:S(2)}) collective-permute-start(bf16[256,256]{1,0:T(8,128)(2,1)S(1)} %collective-permute-done.15.refs_2_), channel_id=1, source_target_pairs={{0,16},{16,0},{32,48},{48,32},{64,80},{80,64},{96,112},{112,96},{1... | collective-permute-start | bytes 393224 | tf_op jit(solution)/shard_map/ppermute | solution.py:56
  121.1 0.9 lay.2.refs_0_
  122.1 0.8 lay.3
  (26 shorter events, 0.3 us)
Async XLA Ops:
  0.0 8.4 %collective-permute-start.2 = (bf16[16,4096]{1,0:T(8,128)(2,1)}, bf16[16,4096]{1,0:T(8,128)(2,1)S(1)}, u32[]{:S(2)}, u32[]{:S(2)}) collective-permute-start(bf16[16,4096]{1,0:T(8,128)(2,1)} %bitcast.6), channel_id=1, source_target_pairs={{0,2},{1,3},{2,0},{3,1},{4,6},{5,7},{6,4},{7,5},{8,10},{9,11},{10,... | collective-permute-start | bytes 393224 | tf_op jit(solution)/shard_map/ppermute | solution.py:68
  3.7 4.7 %collective-permute-start.1 = (bf16[16,4096]{1,0:T(8,128)(2,1)}, bf16[16,4096]{1,0:T(8,128)(2,1)S(1)}, u32[]{:S(2)}, u32[]{:S(2)}) collective-permute-start(bf16[16,4096]{1,0:T(8,128)(2,1)} %bitcast.7), channel_id=1, source_target_pairs={{0,3},{1,0},{2,1},{3,2},{4,7},{5,4},{6,5},{7,6},{8,11},{9,8},{10,9... | collective-permute-start | bytes 393224 | tf_op jit(solution)/shard_map/ppermute | solution.py:68
  4.5 6.5 %collective-permute-start = (bf16[16,4096]{1,0:T(8,128)(2,1)}, bf16[16,4096]{1,0:T(8,128)(2,1)S(1)}, u32[]{:S(2)}, u32[]{:S(2)}) collective-permute-start(bf16[16,4096]{1,0:T(8,128)(2,1)} %bitcast.8), channel_id=1, source_target_pairs={{0,1},{1,2},{2,3},{3,0},{4,5},{5,6},{6,7},{7,4},{8,9},{9,10},{10,1... | collective-permute-start | bytes 393224 | tf_op jit(solution)/shard_map/ppermute | solution.py:68
  5.2 1.2 copy-start
  6.4 0.9 copy-start.2
  8.4 32.1 %copy-start.1 = (f32[4096]{0:T(1024)S(1)}, f32[4096]{0:T(1024)}, u32[]{:S(2)}) copy-start(f32[4096]{0:T(1024)} %param.5) | copy-start | bytes 49156
  8.5 5.9 %collective-permute-start.6 = (bf16[32,4096]{1,0:T(8,128)(2,1)S(1)}, bf16[32,4096]{1,0:T(8,128)(2,1)S(1)}, u32[]{:S(2)}, u32[]{:S(2)}) collective-permute-start(bf16[32,4096]{1,0:T(8,128)(2,1)S(1)} %constant_dynamic-update-slice_fusion.2.refs_1_), channel_id=1, source_target_pairs={{0,12},{1,13},{2,14},{3,15},{4,0},{5,1},{6,2},{7,3},{8,4},{9,5},{1... | collective-permute-start | bytes 786440 | tf_op jit(solution)/shard_map/ppermute | solution.py:68
  11.0 6.8 %collective-permute-start.3 = (bf16[32,4096]{1,0:T(8,128)(2,1)S(1)}, bf16[32,4096]{1,0:T(8,128)(2,1)S(1)}, u32[]{:S(2)}, u32[]{:S(2)}) collective-permute-start(bf16[32,4096]{1,0:T(8,128)(2,1)S(1)} %constant_dynamic-update-slice_fusion.refs_0_), channel_id=1, source_target_pairs={{0,4},{1,5},{2,6},{3,7},{4,8},{5,9},{6,10},{7,11},{8,12},{9,13},{1... | collective-permute-start | bytes 786440 | tf_op jit(solution)/shard_map/ppermute | solution.py:68
  11.1 9.5 %collective-permute-start.4 = (bf16[32,4096]{1,0:T(8,128)(2,1)S(1)}, bf16[32,4096]{1,0:T(8,128)(2,1)S(1)}, u32[]{:S(2)}, u32[]{:S(2)}) collective-permute-start(bf16[32,4096]{1,0:T(8,128)(2,1)S(1)} %constant_dynamic-update-slice_fusion.2.refs_1_), channel_id=1, source_target_pairs={{0,4},{1,5},{2,6},{3,7},{4,8},{5,9},{6,10},{7,11},{8,12},{9,13},{1... | collective-permute-start | bytes 786440 | tf_op jit(solution)/shard_map/ppermute | solution.py:68
  12.3 8.4 %collective-permute-start.5 = (bf16[32,4096]{1,0:T(8,128)(2,1)S(1)}, bf16[32,4096]{1,0:T(8,128)(2,1)S(1)}, u32[]{:S(2)}, u32[]{:S(2)}) collective-permute-start(bf16[32,4096]{1,0:T(8,128)(2,1)S(1)} %constant_dynamic-update-slice_fusion.refs_0_), channel_id=1, source_target_pairs={{0,12},{1,13},{2,14},{3,15},{4,0},{5,1},{6,2},{7,3},{8,4},{9,5},{1... | collective-permute-start | bytes 786440 | tf_op jit(solution)/shard_map/ppermute | solution.py:68
  14.3 6.4 %collective-permute-start.8 = (bf16[32,4096]{1,0:T(8,128)(2,1)S(1)}, bf16[32,4096]{1,0:T(8,128)(2,1)S(1)}, u32[]{:S(2)}, u32[]{:S(2)}) collective-permute-start(bf16[32,4096]{1,0:T(8,128)(2,1)S(1)} %collective-permute-done.6.refs_5_), channel_id=1, source_target_pairs={{0,12},{1,13},{2,14},{3,15},{4,0},{5,1},{6,2},{7,3},{8,4},{9,5},{1... | collective-permute-start | bytes 786440 | tf_op jit(solution)/shard_map/ppermute | solution.py:68
  17.8 6.4 %collective-permute-start.7 = (bf16[32,4096]{1,0:T(8,128)(2,1)S(1)}, bf16[32,4096]{1,0:T(8,128)(2,1)S(1)}, u32[]{:S(2)}, u32[]{:S(2)}) collective-permute-start(bf16[32,4096]{1,0:T(8,128)(2,1)S(1)} %collective-permute-done.3.refs_2_), channel_id=1, source_target_pairs={{0,4},{1,5},{2,6},{3,7},{4,8},{5,9},{6,10},{7,11},{8,12},{9,13},{1... | collective-permute-start | bytes 786440 | tf_op jit(solution)/shard_map/ppermute | solution.py:68
  40.5 17.3 %copy-start.3 = (f32[2048]{0:T(1024)S(1)}, f32[2048]{0:T(1024)}, u32[]{:S(2)}) copy-start(f32[2048]{0:T(1024)} %param.6) | copy-start | bytes 24580
  96.0 3.8 %collective-permute-start.10 = (bf16[544,256]{1,0:T(8,128)(2,1)S(1)}, bf16[544,256]{1,0:T(8,128)(2,1)S(1)}, u32[]{:S(2)}, u32[]{:S(2)}) collective-permute-start(bf16[544,256]{1,0:T(8,128)(2,1)S(1)} %get-tuple-element.24.refs_6_), channel_id=1, source_target_pairs={{0,16},{16,0},{32,48},{48,32},{64,80},{80,64},{96,112},{112,96},{1... | collective-permute-start | bytes 835592 | tf_op jit(solution)/shard_map/ppermute | solution.py:56
  99.7 3.7 %collective-permute-start.9 = (bf16[544,256]{1,0:T(8,128)(2,1)S(1)}, bf16[544,256]{1,0:T(8,128)(2,1)S(1)}, u32[]{:S(2)}, u32[]{:S(2)}) collective-permute-start(bf16[544,256]{1,0:T(8,128)(2,1)S(1)} %totals.3.refs_7_), channel_id=1, source_target_pairs={{0,16},{16,0},{32,48},{48,32},{64,80},{80,64},{96,112},{112,96},{1... | collective-permute-start | bytes 835592 | tf_op jit(solution)/shard_map/ppermute | solution.py:56
  100.7 9.9 %collective-permute-start.11 = (bf16[272,256]{1,0:T(8,128)(2,1)S(1)}, bf16[272,256]{1,0:T(8,128)(2,1)S(1)}, u32[]{:S(2)}, u32[]{:S(2)}) collective-permute-start(bf16[272,256]{1,0:T(8,128)(2,1)S(1)} %stay.4.refs_7_), channel_id=1, source_target_pairs={{0,64},{16,80},{32,96},{48,112},{64,0},{80,16},{96,32},{112,48},{1... | collective-permute-start | bytes 417800 | tf_op jit(solution)/shard_map/ppermute | solution.py:296
  102.4 8.2 %collective-permute-start.12 = (bf16[272,256]{1,0:T(8,128)(2,1)S(1)}, bf16[272,256]{1,0:T(8,128)(2,1)S(1)}, u32[]{:S(2)}, u32[]{:S(2)}) collective-permute-start(bf16[272,256]{1,0:T(8,128)(2,1)S(1)} %stay.5.refs_7_), channel_id=1, source_target_pairs={{0,32},{16,48},{32,64},{48,80},{64,96},{80,112},{96,0},{112,16},{1... | collective-permute-start | bytes 417800 | tf_op jit(solution)/shard_map/ppermute | solution.py:296
  104.3 4.3 %collective-permute-start.13 = (bf16[272,256]{1,0:T(8,128)(2,1)S(1)}, bf16[272,256]{1,0:T(8,128)(2,1)S(1)}, u32[]{:S(2)}, u32[]{:S(2)}) collective-permute-start(bf16[272,256]{1,0:T(8,128)(2,1)S(1)} %stay.6.refs_7_), channel_id=1, source_target_pairs={{0,96},{16,112},{32,0},{48,16},{64,32},{80,48},{96,64},{112,80},{1... | collective-permute-start | bytes 417800 | tf_op jit(solution)/shard_map/ppermute | solution.py:296
  110.8 5.8 %collective-permute-start.14 = (bf16[256,256]{1,0:T(8,128)(2,1)S(1)}, bf16[256,256]{1,0:T(8,128)(2,1)S(1)}, u32[]{:S(2)}, u32[]{:S(2)}) collective-permute-start(bf16[256,256]{1,0:T(8,128)(2,1)S(1)} %finish.1.refs_0_), channel_id=1, source_target_pairs={{0,64},{16,80},{32,96},{48,112},{64,0},{80,16},{96,32},{112,48},{1... | collective-permute-start | bytes 393224 | tf_op jit(solution)/shard_map/ppermute | solution.py:296
  111.4 8.2 %collective-permute-start.18 = (bf16[256,256]{1,0:T(8,128)(2,1)S(1)}, bf16[256,256]{1,0:T(8,128)(2,1)S(1)}, u32[]{:S(2)}, u32[]{:S(2)}) collective-permute-start(bf16[256,256]{1,0:T(8,128)(2,1)S(1)} %finish.1.refs_0_), channel_id=1, source_target_pairs={{0,96},{16,112},{32,0},{48,16},{64,32},{80,48},{96,64},{112,80},{1... | collective-permute-start | bytes 393224 | tf_op jit(solution)/shard_map/ppermute | solution.py:296
  112.5 7.1 %collective-permute-start.15 = (bf16[256,256]{1,0:T(8,128)(2,1)S(1)}, bf16[256,256]{1,0:T(8,128)(2,1)S(1)}, u32[]{:S(2)}, u32[]{:S(2)}) collective-permute-start(bf16[256,256]{1,0:T(8,128)(2,1)S(1)} %finish.1.refs_0_), channel_id=1, source_target_pairs={{0,32},{16,48},{32,64},{48,80},{64,96},{80,112},{96,0},{112,16},{1... | collective-permute-start | bytes 393224 | tf_op jit(solution)/shard_map/ppermute | solution.py:296
  112.9 8.2 %collective-permute-start.16 = (bf16[256,256]{1,0:T(8,128)(2,1)S(1)}, bf16[256,256]{1,0:T(8,128)(2,1)S(1)}, u32[]{:S(2)}, u32[]{:S(2)}) collective-permute-start(bf16[256,256]{1,0:T(8,128)(2,1)S(1)} %finish.1.refs_0_), channel_id=1, source_target_pairs={{0,16},{16,0},{32,48},{48,32},{64,80},{80,64},{96,112},{112,96},{1... | collective-permute-start | bytes 393224 | tf_op jit(solution)/shard_map/ppermute | solution.py:56
  116.6 4.5 %collective-permute-start.17 = (bf16[256,256]{1,0:T(8,128)(2,1)S(1)}, bf16[256,256]{1,0:T(8,128)(2,1)S(1)}, u32[]{:S(2)}, u32[]{:S(2)}) collective-permute-start(bf16[256,256]{1,0:T(8,128)(2,1)S(1)} %collective-permute-done.14.refs_1_), channel_id=1, source_target_pairs={{0,16},{16,0},{32,48},{48,32},{64,80},{80,64},{96,112},{112,96},{1... | collective-permute-start | bytes 393224 | tf_op jit(solution)/shard_map/ppermute | solution.py:56
  119.6 2.4 %collective-permute-start.20 = (bf16[256,256]{1,0:T(8,128)(2,1)S(1)}, bf16[256,256]{1,0:T(8,128)(2,1)S(1)}, u32[]{:S(2)}, u32[]{:S(2)}) collective-permute-start(bf16[256,256]{1,0:T(8,128)(2,1)S(1)} %collective-permute-done.18.refs_1_), channel_id=1, source_target_pairs={{0,16},{16,0},{32,48},{48,32},{64,80},{80,64},{96,112},{112,96},{1... | collective-permute-start | bytes 393224 | tf_op jit(solution)/shard_map/ppermute | solution.py:56
  119.6 2.5 %collective-permute-start.19 = (bf16[256,256]{1,0:T(8,128)(2,1)S(1)}, bf16[256,256]{1,0:T(8,128)(2,1)S(1)}, u32[]{:S(2)}, u32[]{:S(2)}) collective-permute-start(bf16[256,256]{1,0:T(8,128)(2,1)S(1)} %collective-permute-done.15.refs_2_), channel_id=1, source_target_pairs={{0,16},{16,0},{32,48},{48,32},{64,80},{80,64},{96,112},{112,96},{1... | collective-permute-start | bytes 393224 | tf_op jit(solution)/shard_map/ppermute | solution.py:56

commit v6 on v5

--- a/solution.py
+++ b/solution.py
@@ -15,6 +15,7 @@
 
 ITEM_DEV = 4096
 LIST_DEV = 2048
+HALF = ITEM_DEV // 2
 QUART = ITEM_DEV // 4
 N_ITEM = 8
 N_LIST = 16
@@ -72,12 +73,12 @@
 
 
 def gather(feat, own):
-    came = [shift_plane(feat, True, d) for d in (1, 3, 2)]
-    low, high = jnp.concatenate([own, came[0]], 0), jnp.concatenate(came[1:], 0)
-    left_low, right_high = shift_plane(low, False, 1), shift_plane(high, False, 3)
-    left_high, right_low = shift_plane(high, False, 1), shift_plane(low, False, 3)
-    far = [shift_plane(left_low, False, 1), shift_plane(right_high, False, 3)]
-    return [low, high, left_low, left_high, right_low, right_high] + far
+    came = [own] + [shift_plane(feat, True, d) for d in (1, 3, 2)]
+    one, two = (jnp.concatenate([c[:, HALF * h : HALF * (h + 1)] for c in came], 0) for h in range(2))
+    left_one, right_two = shift_plane(one, False, 1), shift_plane(two, False, 3)
+    left_two, right_one = shift_plane(two, False, 1), shift_plane(one, False, 3)
+    far_one, far_two = shift_plane(left_one, False, 1), shift_plane(right_two, False, 3)
+    return [one, left_one, right_one, far_one, two, left_two, right_two, far_two]
 
 
 def prep_body(cent_ref, feat_ref, list_ref, own_ref, raw_ref, sems):
@@ -116,13 +117,13 @@
 def gen_body(list_ref, *refs):
     piece_refs, (*kern_refs, item_ref, rows_ref, feat_ref) = refs[:8], refs[8:]
     core, _, y, x = place()
-    for i, outer in enumerate(ORDER):
+    for i, ref in enumerate(piece_refs):
+        outer, at = ORDER[i % 4], slice(HALF * (i // 4), HALF * (i // 4 + 1))
         for j, inner in enumerate(ORDER):
-            block = piece_refs[2 * i + j // 2][16 * (j % 2) : 16 * (j % 2 + 1), :]
             from_y = (y + jnp.where(core == 0, outer, inner) + 4) % 4
             from_x = (x + jnp.where(core == 0, inner, outer) + 4) % 4
             spot = from_y * 4 + from_x
-            feat_ref[pl.ds(pl.multiple_of(spot * 16, 16), 16), :] = block
+            feat_ref[pl.ds(pl.multiple_of(spot * 16, 16), 16), at] = ref[16 * j : 16 * (j + 1), :]
 
     totals = []
     for n, kern_ref in enumerate(kern_refs):
@@ -186,20 +187,21 @@
     for k in range(16):
         scale_ref[128 * k : 128 * (k + 1), :] = jnp.broadcast_to(scale[k : k + 1, :], (128, 128)).T
 
-    for h, ref in enumerate(kern_refs):
+    for h in range(0, 4, 2):
 
         def step(m, total):
             at = pl.ds(pl.multiple_of(m * 128, 128), 128)
             by = scale_ref[at, :].reshape(16, 8, 128)
-            block = ref[at, :].reshape(16, 8, QUART)
+            blocks = [ref[at, :].reshape(16, 8, QUART) for ref in kern_refs[h : h + 2]]
             total = list(total)
             for j in range(16):
-                for k in range(8):
-                    total[k] = total[k] + block[j, :, 128 * k : 128 * (k + 1)] * by[j]
+                for k in range(16):
+                    lanes = slice(128 * (k % 8), 128 * (k % 8 + 1))
+                    total[k] = total[k] + blocks[k // 8][j, :, lanes] * by[j]
             return tuple(total)
 
-        total = lax.fori_loop(0, LIST_DEV // 128, step, (jnp.zeros((8, 128), F32),) * 8)
-        for k in range(8):
+        total = lax.fori_loop(0, LIST_DEV // 128, step, (jnp.zeros((8, 128), F32),) * 16)
+        for k in range(16):
             first = QUART * h + 128 * k
             total_ref[:, first : first + 128] = total[k].sum(0, keepdims=True)
 

time: 123 us -> 123 us (level)
  starting transfers between devices: 29 us -> 27.5 us
    ppermute x9, starting transfers between devices: 13.7 us -> 12.2 us  [shift_plane(): return lax.ppermute(block, ('item', 'list'), pairs)]
  transfers between devices with their start and end apart: 21 -> 21, of which waited for: 10 -> 11; matrix products, arithmetic and copies ran while one was open for 0% -> 0% of each run, Pallas kernels for 5% -> 6%
where the time goes in v6:
time: 123 us
  blocking collectives  55.1 us (45%)
  starting transfers between devices  27.5 us (22%)
  Pallas kernels  24.9 us (20%)
  waiting for transfers between devices  12.7 us (10%)
  local copies, waits for them, and re-layouts  2.18 us (2%)
    all_to_all x3, blocking collectives, local(): parts = lax.all_to_all(parts, 'list', 0, 0)  30.4 us
    all_to_all x2, blocking collectives, local(): cols = lax.all_to_all(col_pass(kern, parts, weight), 'item', 0, 0)  24.7 us
    pallas_call x12, Pallas kernels, call(): pl.pallas_call(body, out_shape=out, in_specs=whole(len(args)), out_specs=...  22.3 us
    ppermute x9, starting transfers between devices, shift_plane(): return lax.ppermute(block, ('item', 'list'), pairs)  12.2 us
    ppermute x6, starting transfers between devices, swap_core(): return lax.ppermute(block, 'item', [(i, i ^ 1) for i in range(N_ITEM)])  9.43 us
    ppermute x9, waiting for transfers between devices, shift_plane(): return lax.ppermute(block, ('item', 'list'), pairs)  8.08 us
    ppermute x6, starting transfers between devices, shift_z(): lax.ppermute(block, 'item', [(i, (i + 2 * step) % N_ITEM) for i in range(...  5.91 us
    ppermute x6, waiting for transfers between devices, shift_z(): lax.ppermute(block, 'item', [(i, (i + 2 * step) % N_ITEM) for i in range(...  4.52 us
  transfers between devices with their start and end apart: 21, of which 11 were waited for; matrix products, arithmetic and copies ran while one was open for 0% of the time, Pallas kernels for 6%

profile of v6, /device:TPU:1, one launch (start us, length us, event | category | flops | bytes accessed | tf_op | source)
XLA Modules:
  0.0 122.8 jit_solution(14033826530967331433)
XLA Ops:
  0.0 3.7 %collective-permute-start.2 = (bf16[16,4096]{1,0:T(8,128)(2,1)}, bf16[16,4096]{1,0:T(8,128)(2,1)S(1)}, u32[]{:S(2)}, u32[]{:S(2)}) collective-permute-start(bf16[16,4096]{1,0:T(8,128)(2,1)} %bitcast.6), channel_id=1, source_target_pairs={{0,2},{1,3},{2,0},{3,1},{4,6},{5,7},{6,4},{7,5},{8,10},{9,11},{10,... | collective-permute-start | bytes 393224 | tf_op jit(solution)/shard_map/ppermute | solution.py:69
  3.7 0.8 collective-permute-start.1
  4.5 0.7 collective-permute-start
  5.2 1.2 copy-done
  6.4 0.9 copy-done.2
  7.3 0.9 lists.1
  8.4 1.3 %collective-permute-done = bf16[16,4096]{1,0:T(8,128)(2,1)S(1)} collective-permute-done((bf16[16,4096]{1,0:T(8,128)(2,1)}, bf16[16,4096]{1,0:T(8,128)(2,1)S(1)}, u32[]{:S(2)}, u32[]{:S(2)}) %collective-permute-start) | collective-permute-done | bytes 131104 | tf_op jit(solution)/shard_map/ppermute | solution.py:69
  9.8 1.3 %collective-permute-start.3 = (bf16[64,2048]{1,0:T(8,128)(2,1)S(1)}, bf16[64,2048]{1,0:T(8,128)(2,1)S(1)}, u32[]{:S(2)}, u32[]{:S(2)}) collective-permute-start(bf16[64,2048]{1,0:T(8,128)(2,1)S(1)} %pad_maximum_fusion.refs_0_), channel_id=1, source_target_pairs={{0,4},{1,5},{2,6},{3,7},{4,8},{5,9},{6,10},{7,11},{8,12},{9,13},{1... | collective-permute-start | bytes 786440 | tf_op jit(solution)/shard_map/ppermute | solution.py:69
  11.1 1.5 %collective-permute-start.7 = (bf16[64,2048]{1,0:T(8,128)(2,1)S(1)}, bf16[64,2048]{1,0:T(8,128)(2,1)S(1)}, u32[]{:S(2)}, u32[]{:S(2)}) collective-permute-start(bf16[64,2048]{1,0:T(8,128)(2,1)S(1)} %pad_maximum_fusion.1.refs_4_), channel_id=1, source_target_pairs={{0,12},{1,13},{2,14},{3,15},{4,0},{5,1},{6,2},{7,3},{8,4},{9,5},{1... | collective-permute-start | bytes 786440 | tf_op jit(solution)/shard_map/ppermute | solution.py:69
  12.7 1.3 %collective-permute-start.4 = (bf16[64,2048]{1,0:T(8,128)(2,1)S(1)}, bf16[64,2048]{1,0:T(8,128)(2,1)S(1)}, u32[]{:S(2)}, u32[]{:S(2)}) collective-permute-start(bf16[64,2048]{1,0:T(8,128)(2,1)S(1)} %pad_maximum_fusion.refs_0_), channel_id=1, source_target_pairs={{0,12},{1,13},{2,14},{3,15},{4,0},{5,1},{6,2},{7,3},{8,4},{9,5},{1... | collective-permute-start | bytes 786440 | tf_op jit(solution)/shard_map/ppermute | solution.py:69
  13.9 0.2 collective-permute-start.6
  14.1 2.5 %collective-permute-done.3.refs_1_ = bf16[64,2048]{1,0:T(8,128)(2,1)S(1)} collective-permute-done((bf16[64,2048]{1,0:T(8,128)(2,1)S(1)}, bf16[64,2048]{1,0:T(8,128)(2,1)S(1)}, u32[]{:S(2)}, u32[]{:S(2)}) %collective-permute-start.3) | collective-permute-done | bytes 262176 | tf_op jit(solution)/shard_map/ppermute | solution.py:69
  16.7 2.7 %collective-permute-start.8 = (bf16[64,2048]{1,0:T(8,128)(2,1)S(1)}, bf16[64,2048]{1,0:T(8,128)(2,1)S(1)}, u32[]{:S(2)}, u32[]{:S(2)}) collective-permute-start(bf16[64,2048]{1,0:T(8,128)(2,1)S(1)} %collective-permute-done.7.refs_6_), channel_id=1, source_target_pairs={{0,12},{1,13},{2,14},{3,15},{4,0},{5,1},{6,2},{7,3},{8,4},{9,5},{1... | collective-permute-start | bytes 786440 | tf_op jit(solution)/shard_map/ppermute | solution.py:69
  19.4 0.1 collective-permute-done.4.refs_2_
  19.5 0.8 collective-permute-done.6.refs_5_
  20.4 3.1 %collective-permute-done.5.refs_3_ = bf16[64,2048]{1,0:T(8,128)(2,1)S(1)} collective-permute-done((bf16[64,2048]{1,0:T(8,128)(2,1)S(1)}, bf16[64,2048]{1,0:T(8,128)(2,1)S(1)}, u32[]{:S(2)}, u32[]{:S(2)}) %collective-permute-start.5) | collective-permute-done | bytes 262176 | tf_op jit(solution)/shard_map/ppermute | solution.py:69
  23.5 5.6 %generate.1 = (f32[2048,1024]{1,0:T(8,128)S(1)}, f32[2048,1024]{1,0:T(8,128)S(1)}, f32[2048,1024]{1,0:T(8,128)S(1)}, f32[2048,1024]{1,0:T(8,128)S(1)}, bf16[4096...) custom-call(bf16[2048,256]{1,0:T(8,128)(2,1)S(1)} %get-tuple-element.15.list_ref, ...), custom_call_target="tpu_custom_call" | custom-call | flops 4294967296 | bytes 1048576 | tf_op jit(solution)/shard_map/generate/pallas_call | solution.py:33
  29.1 11.0 %all_to_all.25.refs_4_ = bf16[16,32,128]{2,1,0:T(8,128)(2,1)S(1)} all-to-all(bf16[16,32,128]{2,1,0:T(8,128)(2,1)S(1)} %get-tuple-element.22), channel_id=1, replica_groups=mesh['item'=8,'list'=16] {'list'}, dimensions={0} | all-to-all | bytes 262144 | tf_op jit(solution)/shard_map/all_to_all | solution.py:339
  40.1 2.3 %columns.2 = f32[8,16,128]{2,1,0:T(8,128)S(1)} custom-call(f32[2048,1024]{1,0:T(8,128)S(1)} %get-tuple-element.17.refs_0_, f32[2048,1024]{1,0:T(8,128)S(1)} %get-tuple-element.18.refs_1_, f32[2048,1024]{1,0:T(8,128)S(1)} %get-tuple-element.19.refs_2_, f32[2048,1024]{1,0:T(8,128)S(1)} %get-tuple-element.20.refs_3_, ...), custom_call_target="tpu_custom_call" | custom-call | flops 16777216 | bytes 1048576 | tf_op jit(solution)/shard_map/columns/pallas_call | solution.py:33
  42.4 15.3 %all_to_all.26.refs_4_ = f32[8,16,128]{2,1,0:T(8,128)S(1)} all-to-all(f32[8,16,128]{2,1,0:T(8,128)S(1)} %columns.2), channel_id=1, replica_groups=mesh['item'=8,'list'=16] {'item'}, dimensions={0} | all-to-all | bytes 131072 | tf_op jit(solution)/shard_map/all_to_all | solution.py:340
  57.8 2.8 %rows.2 = bf16[16,32,128]{2,1,0:T(8,128)(2,1)S(1)} custom-call(f32[2048,1024]{1,0:T(8,128)S(1)} %get-tuple-element.17.refs_0_, f32[2048,1024]{1,0:T(8,128)S(1)} %get-tuple-element.18.refs_1_, f32[2048,1024]{1,0:T(8,128)S(1)} %get-tuple-element.19.refs_2_, f32[2048,1024]{1,0:T(8,128)S(1)} %get-tuple-element.20.refs_3_, f32[8,16,128]{2,1,0:T(8,128)S(1)} %all_to_all.26.refs_4_, ...), custom_call_target="tpu_custom_call" | custom-call | flops 16777216 | bytes 1048576 | tf_op jit(solution)/shard_map/rows/pallas_call | solution.py:33
  60.5 9.7 %all_to_all.27.refs_4_ = bf16[16,32,128]{2,1,0:T(8,128)(2,1)S(1)} all-to-all(bf16[16,32,128]{2,1,0:T(8,128)(2,1)S(1)} %rows.2), channel_id=1, replica_groups=mesh['item'=8,'list'=16] {'list'}, dimensions={0} | all-to-all | bytes 262144 | tf_op jit(solution)/shard_map/all_to_all | solution.py:339
  70.2 2.3 %columns.3 = f32[8,16,128]{2,1,0:T(8,128)S(1)} custom-call(f32[2048,1024]{1,0:T(8,128)S(1)} %get-tuple-element.17.refs_0_, f32[2048,1024]{1,0:T(8,128)S(1)} %get-tuple-element.18.refs_1_, f32[2048,1024]{1,0:T(8,128)S(1)} %get-tuple-element.19.refs_2_, f32[2048,1024]{1,0:T(8,128)S(1)} %get-tuple-element.20.refs_3_, ...), custom_call_target="tpu_custom_call" | custom-call | flops 16777216 | bytes 1048576 | tf_op jit(solution)/shard_map/columns/pallas_call | solution.py:33
  72.5 9.4 %all_to_all.28.refs_4_ = f32[8,16,128]{2,1,0:T(8,128)S(1)} all-to-all(f32[8,16,128]{2,1,0:T(8,128)S(1)} %columns.3), channel_id=1, replica_groups=mesh['item'=8,'list'=16] {'item'}, dimensions={0} | all-to-all | bytes 131072 | tf_op jit(solution)/shard_map/all_to_all | solution.py:340
  81.9 2.8 %rows.3 = bf16[16,32,128]{2,1,0:T(8,128)(2,1)S(1)} custom-call(f32[2048,1024]{1,0:T(8,128)S(1)} %get-tuple-element.17.refs_0_, f32[2048,1024]{1,0:T(8,128)S(1)} %get-tuple-element.18.refs_1_, f32[2048,1024]{1,0:T(8,128)S(1)} %get-tuple-element.19.refs_2_, f32[2048,1024]{1,0:T(8,128)S(1)} %get-tuple-element.20.refs_3_, f32[8,16,128]{2,1,0:T(8,128)S(1)} %all_to_all.28.refs_4_, ...), custom_call_target="tpu_custom_call" | custom-call | flops 16777216 | bytes 1048576 | tf_op jit(solution)/shard_map/rows/pallas_call | solution.py:33
  84.6 9.7 %all_to_all.29.refs_5_ = bf16[16,32,128]{2,1,0:T(8,128)(2,1)S(1)} all-to-all(bf16[16,32,128]{2,1,0:T(8,128)(2,1)S(1)} %rows.3), channel_id=1, replica_groups=mesh['item'=8,'list'=16] {'list'}, dimensions={0} | all-to-all | bytes 262144 | tf_op jit(solution)/shard_map/all_to_all | solution.py:342
  94.3 1.4 %totals.2 = (bf16[544,256]{1,0:T(8,128)(2,1)S(1)}, f32[8,4096]{1,0:T(8,128)S(1)}) custom-call(f32[2048,1024]{1,0:T(8,128)S(1)} %get-tuple-element.17.refs_0_, f32[2048,1024]{1,0:T(8,128)S(1)} %get-tuple-element.18.refs_1_, f32[2048,1024]{1,0:T(8,128)S(1)} %get-tuple-element.19.refs_2_, f32[2048,1024]{1,0:T(8,128)S(1)} %get-tuple-element.20.refs_3_, ...), custom_call_target="tpu_custom_call" | custom-call | flops 2147483648 | bytes 1048576 | tf_op jit(solution)/shard_map/totals/pallas_call | solution.py:33
  95.8 2.2 %collective-permute-start.10 = (bf16[544,256]{1,0:T(8,128)(2,1)S(1)}, bf16[544,256]{1,0:T(8,128)(2,1)S(1)}, u32[]{:S(2)}, u32[]{:S(2)}) collective-permute-start(bf16[544,256]{1,0:T(8,128)(2,1)S(1)} %get-tuple-element.24.refs_6_), channel_id=1, source_target_pairs={{0,16},{16,0},{32,48},{48,32},{64,80},{80,64},{96,112},{112,96},{1... | collective-permute-start | bytes 835592 | tf_op jit(solution)/shard_map/ppermute | solution.py:57
  98.0 1.5 %totals.3.refs_7_ = bf16[544,256]{1,0:T(8,128)(2,1)S(1)} custom-call(f32[2048,1024]{1,0:T(8,128)S(1)} %get-tuple-element.17.refs_0_, f32[2048,1024]{1,0:T(8,128)S(1)} %get-tuple-element.18.refs_1_, f32[2048,1024]{1,0:T(8,128)S(1)} %get-tuple-element.19.refs_2_, f32[2048,1024]{1,0:T(8,128)S(1)} %get-tuple-element.20.refs_3_, ...), custom_call_target="tpu_custom_call" | custom-call | flops 2147483648 | bytes 1048576 | tf_op jit(solution)/shard_map/totals/pallas_call | solution.py:33
  99.6 0.9 stay.4.refs_7_
  100.5 0.8 collective-permute-start.11
  101.3 0.9 stay.5.refs_7_
  102.1 1.0 collective-permute-start.12
  103.2 0.9 stay.6.refs_7_
  104.0 2.0 %collective-permute-start.13 = (bf16[272,256]{1,0:T(8,128)(2,1)S(1)}, bf16[272,256]{1,0:T(8,128)(2,1)S(1)}, u32[]{:S(2)}, u32[]{:S(2)}) collective-permute-start(bf16[272,256]{1,0:T(8,128)(2,1)S(1)} %stay.6.refs_7_), channel_id=1, source_target_pairs={{0,96},{16,112},{32,0},{48,16},{64,32},{80,48},{96,64},{112,80},{1... | collective-permute-start | bytes 417800 | tf_op jit(solution)/shard_map/ppermute | solution.py:298
  106.1 0.9 stay.7.mine_ref
  106.9 1.4 %collective-permute-done.13.c_ref = bf16[272,256]{1,0:T(8,128)(2,1)S(1)} collective-permute-done((bf16[272,256]{1,0:T(8,128)(2,1)S(1)}, bf16[272,256]{1,0:T(8,128)(2,1)S(1)}, u32[]{:S(2)}, u32[]{:S(2)}) %collective-permute-start.13) | collective-permute-done | bytes 139296 | tf_op jit(solution)/shard_map/ppermute | solution.py:298
  108.3 2.0 %collective-permute-done.12.b_ref = bf16[272,256]{1,0:T(8,128)(2,1)S(1)} collective-permute-done((bf16[272,256]{1,0:T(8,128)(2,1)S(1)}, bf16[272,256]{1,0:T(8,128)(2,1)S(1)}, u32[]{:S(2)}, u32[]{:S(2)}) %collective-permute-start.12) | collective-permute-done | bytes 139296 | tf_op jit(solution)/shard_map/ppermute | solution.py:298
  110.3 0.2 finish.1.refs_0_
  110.5 0.6 collective-permute-start.14
  111.2 1.1 collective-permute-start.18
  112.2 0.4 collective-permute-start.15
  112.6 2.6 %collective-permute-start.16 = (bf16[256,256]{1,0:T(8,128)(2,1)S(1)}, bf16[256,256]{1,0:T(8,128)(2,1)S(1)}, u32[]{:S(2)}, u32[]{:S(2)}) collective-permute-start(bf16[256,256]{1,0:T(8,128)(2,1)S(1)} %finish.1.refs_0_), channel_id=1, source_target_pairs={{0,16},{16,0},{32,48},{48,32},{64,80},{80,64},{96,112},{112,96},{1... | collective-permute-start | bytes 393224 | tf_op jit(solution)/shard_map/ppermute | solution.py:57
  115.2 1.1 collective-permute-done.14.refs_1_
  116.4 3.0 %collective-permute-start.17 = (bf16[256,256]{1,0:T(8,128)(2,1)S(1)}, bf16[256,256]{1,0:T(8,128)(2,1)S(1)}, u32[]{:S(2)}, u32[]{:S(2)}) collective-permute-start(bf16[256,256]{1,0:T(8,128)(2,1)S(1)} %collective-permute-done.14.refs_1_), channel_id=1, source_target_pairs={{0,16},{16,0},{32,48},{48,32},{64,80},{80,64},{96,112},{112,96},{1... | collective-permute-start | bytes 393224 | tf_op jit(solution)/shard_map/ppermute | solution.py:57
  119.3 1.5 %collective-permute-start.19 = (bf16[256,256]{1,0:T(8,128)(2,1)S(1)}, bf16[256,256]{1,0:T(8,128)(2,1)S(1)}, u32[]{:S(2)}, u32[]{:S(2)}) collective-permute-start(bf16[256,256]{1,0:T(8,128)(2,1)S(1)} %collective-permute-done.15.refs_2_), channel_id=1, source_target_pairs={{0,16},{16,0},{32,48},{48,32},{64,80},{80,64},{96,112},{112,96},{1... | collective-permute-start | bytes 393224 | tf_op jit(solution)/shard_map/ppermute | solution.py:57
  120.9 0.9 lay.2.refs_0_
  121.8 0.8 lay.3
  (28 shorter events, 0.5 us)
Async XLA Ops:
  0.0 8.3 %collective-permute-start.2 = (bf16[16,4096]{1,0:T(8,128)(2,1)}, bf16[16,4096]{1,0:T(8,128)(2,1)S(1)}, u32[]{:S(2)}, u32[]{:S(2)}) collective-permute-start(bf16[16,4096]{1,0:T(8,128)(2,1)} %bitcast.6), channel_id=1, source_target_pairs={{0,2},{1,3},{2,0},{3,1},{4,6},{5,7},{6,4},{7,5},{8,10},{9,11},{10,... | collective-permute-start | bytes 393224 | tf_op jit(solution)/shard_map/ppermute | solution.py:69
  3.7 4.7 %collective-permute-start.1 = (bf16[16,4096]{1,0:T(8,128)(2,1)}, bf16[16,4096]{1,0:T(8,128)(2,1)S(1)}, u32[]{:S(2)}, u32[]{:S(2)}) collective-permute-start(bf16[16,4096]{1,0:T(8,128)(2,1)} %bitcast.7), channel_id=1, source_target_pairs={{0,3},{1,0},{2,1},{3,2},{4,7},{5,4},{6,5},{7,6},{8,11},{9,8},{10,9... | collective-permute-start | bytes 393224 | tf_op jit(solution)/shard_map/ppermute | solution.py:69
  4.5 5.2 %collective-permute-start = (bf16[16,4096]{1,0:T(8,128)(2,1)}, bf16[16,4096]{1,0:T(8,128)(2,1)S(1)}, u32[]{:S(2)}, u32[]{:S(2)}) collective-permute-start(bf16[16,4096]{1,0:T(8,128)(2,1)} %bitcast.8), channel_id=1, source_target_pairs={{0,1},{1,2},{2,3},{3,0},{4,5},{5,6},{6,7},{7,4},{8,9},{9,10},{10,1... | collective-permute-start | bytes 393224 | tf_op jit(solution)/shard_map/ppermute | solution.py:69
  5.2 1.2 copy-start
  6.4 0.9 copy-start.2
  9.8 30.3 %copy-start.1 = (f32[4096]{0:T(1024)S(1)}, f32[4096]{0:T(1024)}, u32[]{:S(2)}) copy-start(f32[4096]{0:T(1024)} %param.5) | copy-start | bytes 49156
  9.8 6.8 %collective-permute-start.3 = (bf16[64,2048]{1,0:T(8,128)(2,1)S(1)}, bf16[64,2048]{1,0:T(8,128)(2,1)S(1)}, u32[]{:S(2)}, u32[]{:S(2)}) collective-permute-start(bf16[64,2048]{1,0:T(8,128)(2,1)S(1)} %pad_maximum_fusion.refs_0_), channel_id=1, source_target_pairs={{0,4},{1,5},{2,6},{3,7},{4,8},{5,9},{6,10},{7,11},{8,12},{9,13},{1... | collective-permute-start | bytes 786440 | tf_op jit(solution)/shard_map/ppermute | solution.py:69
  11.1 5.6 %collective-permute-start.7 = (bf16[64,2048]{1,0:T(8,128)(2,1)S(1)}, bf16[64,2048]{1,0:T(8,128)(2,1)S(1)}, u32[]{:S(2)}, u32[]{:S(2)}) collective-permute-start(bf16[64,2048]{1,0:T(8,128)(2,1)S(1)} %pad_maximum_fusion.1.refs_4_), channel_id=1, source_target_pairs={{0,12},{1,13},{2,14},{3,15},{4,0},{5,1},{6,2},{7,3},{8,4},{9,5},{1... | collective-permute-start | bytes 786440 | tf_op jit(solution)/shard_map/ppermute | solution.py:69
  12.7 6.9 %collective-permute-start.4 = (bf16[64,2048]{1,0:T(8,128)(2,1)S(1)}, bf16[64,2048]{1,0:T(8,128)(2,1)S(1)}, u32[]{:S(2)}, u32[]{:S(2)}) collective-permute-start(bf16[64,2048]{1,0:T(8,128)(2,1)S(1)} %pad_maximum_fusion.refs_0_), channel_id=1, source_target_pairs={{0,12},{1,13},{2,14},{3,15},{4,0},{5,1},{6,2},{7,3},{8,4},{9,5},{1... | collective-permute-start | bytes 786440 | tf_op jit(solution)/shard_map/ppermute | solution.py:69
  13.9 6.4 %collective-permute-start.6 = (bf16[64,2048]{1,0:T(8,128)(2,1)S(1)}, bf16[64,2048]{1,0:T(8,128)(2,1)S(1)}, u32[]{:S(2)}, u32[]{:S(2)}) collective-permute-start(bf16[64,2048]{1,0:T(8,128)(2,1)S(1)} %pad_maximum_fusion.1.refs_4_), channel_id=1, source_target_pairs={{0,4},{1,5},{2,6},{3,7},{4,8},{5,9},{6,10},{7,11},{8,12},{9,13},{1... | collective-permute-start | bytes 786440 | tf_op jit(solution)/shard_map/ppermute | solution.py:69
  16.6 6.8 %collective-permute-start.5 = (bf16[64,2048]{1,0:T(8,128)(2,1)S(1)}, bf16[64,2048]{1,0:T(8,128)(2,1)S(1)}, u32[]{:S(2)}, u32[]{:S(2)}) collective-permute-start(bf16[64,2048]{1,0:T(8,128)(2,1)S(1)} %collective-permute-done.3.refs_1_), channel_id=1, source_target_pairs={{0,4},{1,5},{2,6},{3,7},{4,8},{5,9},{6,10},{7,11},{8,12},{9,13},{1... | collective-permute-start | bytes 786440 | tf_op jit(solution)/shard_map/ppermute | solution.py:69
  16.7 6.8 %collective-permute-start.8 = (bf16[64,2048]{1,0:T(8,128)(2,1)S(1)}, bf16[64,2048]{1,0:T(8,128)(2,1)S(1)}, u32[]{:S(2)}, u32[]{:S(2)}) collective-permute-start(bf16[64,2048]{1,0:T(8,128)(2,1)S(1)} %collective-permute-done.7.refs_6_), channel_id=1, source_target_pairs={{0,12},{1,13},{2,14},{3,15},{4,0},{5,1},{6,2},{7,3},{8,4},{9,5},{1... | collective-permute-start | bytes 786440 | tf_op jit(solution)/shard_map/ppermute | solution.py:69
  40.1 17.6 %copy-start.3 = (f32[2048]{0:T(1024)S(1)}, f32[2048]{0:T(1024)}, u32[]{:S(2)}) copy-start(f32[2048]{0:T(1024)} %param.6) | copy-start | bytes 24580
  95.8 3.8 %collective-permute-start.10 = (bf16[544,256]{1,0:T(8,128)(2,1)S(1)}, bf16[544,256]{1,0:T(8,128)(2,1)S(1)}, u32[]{:S(2)}, u32[]{:S(2)}) collective-permute-start(bf16[544,256]{1,0:T(8,128)(2,1)S(1)} %get-tuple-element.24.refs_6_), channel_id=1, source_target_pairs={{0,16},{16,0},{32,48},{48,32},{64,80},{80,64},{96,112},{112,96},{1... | collective-permute-start | bytes 835592 | tf_op jit(solution)/shard_map/ppermute | solution.py:57
  99.5 3.7 %collective-permute-start.9 = (bf16[544,256]{1,0:T(8,128)(2,1)S(1)}, bf16[544,256]{1,0:T(8,128)(2,1)S(1)}, u32[]{:S(2)}, u32[]{:S(2)}) collective-permute-start(bf16[544,256]{1,0:T(8,128)(2,1)S(1)} %totals.3.refs_7_), channel_id=1, source_target_pairs={{0,16},{16,0},{32,48},{48,32},{64,80},{80,64},{96,112},{112,96},{1... | collective-permute-start | bytes 835592 | tf_op jit(solution)/shard_map/ppermute | solution.py:57
  100.5 9.9 %collective-permute-start.11 = (bf16[272,256]{1,0:T(8,128)(2,1)S(1)}, bf16[272,256]{1,0:T(8,128)(2,1)S(1)}, u32[]{:S(2)}, u32[]{:S(2)}) collective-permute-start(bf16[272,256]{1,0:T(8,128)(2,1)S(1)} %stay.4.refs_7_), channel_id=1, source_target_pairs={{0,64},{16,80},{32,96},{48,112},{64,0},{80,16},{96,32},{112,48},{1... | collective-permute-start | bytes 417800 | tf_op jit(solution)/shard_map/ppermute | solution.py:298
  102.1 8.2 %collective-permute-start.12 = (bf16[272,256]{1,0:T(8,128)(2,1)S(1)}, bf16[272,256]{1,0:T(8,128)(2,1)S(1)}, u32[]{:S(2)}, u32[]{:S(2)}) collective-permute-start(bf16[272,256]{1,0:T(8,128)(2,1)S(1)} %stay.5.refs_7_), channel_id=1, source_target_pairs={{0,32},{16,48},{32,64},{48,80},{64,96},{80,112},{96,0},{112,16},{1... | collective-permute-start | bytes 417800 | tf_op jit(solution)/shard_map/ppermute | solution.py:298
  104.0 4.3 %collective-permute-start.13 = (bf16[272,256]{1,0:T(8,128)(2,1)S(1)}, bf16[272,256]{1,0:T(8,128)(2,1)S(1)}, u32[]{:S(2)}, u32[]{:S(2)}) collective-permute-start(bf16[272,256]{1,0:T(8,128)(2,1)S(1)} %stay.6.refs_7_), channel_id=1, source_target_pairs={{0,96},{16,112},{32,0},{48,16},{64,32},{80,48},{96,64},{112,80},{1... | collective-permute-start | bytes 417800 | tf_op jit(solution)/shard_map/ppermute | solution.py:298
  110.5 5.8 %collective-permute-start.14 = (bf16[256,256]{1,0:T(8,128)(2,1)S(1)}, bf16[256,256]{1,0:T(8,128)(2,1)S(1)}, u32[]{:S(2)}, u32[]{:S(2)}) collective-permute-start(bf16[256,256]{1,0:T(8,128)(2,1)S(1)} %finish.1.refs_0_), channel_id=1, source_target_pairs={{0,64},{16,80},{32,96},{48,112},{64,0},{80,16},{96,32},{112,48},{1... | collective-permute-start | bytes 393224 | tf_op jit(solution)/shard_map/ppermute | solution.py:298
  111.2 8.2 %collective-permute-start.18 = (bf16[256,256]{1,0:T(8,128)(2,1)S(1)}, bf16[256,256]{1,0:T(8,128)(2,1)S(1)}, u32[]{:S(2)}, u32[]{:S(2)}) collective-permute-start(bf16[256,256]{1,0:T(8,128)(2,1)S(1)} %finish.1.refs_0_), channel_id=1, source_target_pairs={{0,96},{16,112},{32,0},{48,16},{64,32},{80,48},{96,64},{112,80},{1... | collective-permute-start | bytes 393224 | tf_op jit(solution)/shard_map/ppermute | solution.py:298
  112.2 7.1 %collective-permute-start.15 = (bf16[256,256]{1,0:T(8,128)(2,1)S(1)}, bf16[256,256]{1,0:T(8,128)(2,1)S(1)}, u32[]{:S(2)}, u32[]{:S(2)}) collective-permute-start(bf16[256,256]{1,0:T(8,128)(2,1)S(1)} %finish.1.refs_0_), channel_id=1, source_target_pairs={{0,32},{16,48},{32,64},{48,80},{64,96},{80,112},{96,0},{112,16},{1... | collective-permute-start | bytes 393224 | tf_op jit(solution)/shard_map/ppermute | solution.py:298
  112.6 8.2 %collective-permute-start.16 = (bf16[256,256]{1,0:T(8,128)(2,1)S(1)}, bf16[256,256]{1,0:T(8,128)(2,1)S(1)}, u32[]{:S(2)}, u32[]{:S(2)}) collective-permute-start(bf16[256,256]{1,0:T(8,128)(2,1)S(1)} %finish.1.refs_0_), channel_id=1, source_target_pairs={{0,16},{16,0},{32,48},{48,32},{64,80},{80,64},{96,112},{112,96},{1... | collective-permute-start | bytes 393224 | tf_op jit(solution)/shard_map/ppermute | solution.py:57
  116.4 4.5 %collective-permute-start.17 = (bf16[256,256]{1,0:T(8,128)(2,1)S(1)}, bf16[256,256]{1,0:T(8,128)(2,1)S(1)}, u32[]{:S(2)}, u32[]{:S(2)}) collective-permute-start(bf16[256,256]{1,0:T(8,128)(2,1)S(1)} %collective-permute-done.14.refs_1_), channel_id=1, source_target_pairs={{0,16},{16,0},{32,48},{48,32},{64,80},{80,64},{96,112},{112,96},{1... | collective-permute-start | bytes 393224 | tf_op jit(solution)/shard_map/ppermute | solution.py:57
  119.3 2.4 %collective-permute-start.20 = (bf16[256,256]{1,0:T(8,128)(2,1)S(1)}, bf16[256,256]{1,0:T(8,128)(2,1)S(1)}, u32[]{:S(2)}, u32[]{:S(2)}) collective-permute-start(bf16[256,256]{1,0:T(8,128)(2,1)S(1)} %collective-permute-done.18.refs_1_), channel_id=1, source_target_pairs={{0,16},{16,0},{32,48},{48,32},{64,80},{80,64},{96,112},{112,96},{1... | collective-permute-start | bytes 393224 | tf_op jit(solution)/shard_map/ppermute | solution.py:57
  119.3 2.5 %collective-permute-start.19 = (bf16[256,256]{1,0:T(8,128)(2,1)S(1)}, bf16[256,256]{1,0:T(8,128)(2,1)S(1)}, u32[]{:S(2)}, u32[]{:S(2)}) collective-permute-start(bf16[256,256]{1,0:T(8,128)(2,1)S(1)} %collective-permute-done.15.refs_2_), channel_id=1, source_target_pairs={{0,16},{16,0},{32,48},{48,32},{64,80},{80,64},{96,112},{112,96},{1... | collective-permute-start | bytes 393224 | tf_op jit(solution)/shard_map/ppermute | solution.py:57

commit v7 on v6

--- a/solution.py
+++ b/solution.py
@@ -352,9 +352,9 @@
     mine = stay(0, QROWS, F32, *held, came_late, three)
     done = finish(mine, [shift_z(block, d) for block, d in ((two, 2), (one, 1), (three, 3))], lists)
 
-    two, one, three = (shift_z(done, d) for d in (2, 1, 3))
-    out = lay(((0, 0), (2, 0), (1, 0), (0, 1), (2, 1)), (done, two, one, swap_core(done), swap_core(two)))
-    return lay(((3, 0), (1, 1), (3, 1)), (three, swap_core(one), swap_core(three)), out)
+    three, one, two = (shift_z(done, d) for d in (3, 1, 2))
+    out = lay(((0, 0), (2, 0), (1, 0), (3, 0), (0, 1), (2, 1)), (done, two, one, three, swap_core(done), swap_core(two)))
+    return lay(((1, 1), (3, 1)), (swap_core(one), swap_core(three)), out)
 
 
 def solution(mesh):

time: 123 us -> 123 us (level)
  transfers between devices with their start and end apart: 21 -> 21, of which waited for: 11 -> 10; matrix products, arithmetic and copies ran while one was open for 0% -> 0% of each run, Pallas kernels for 6% -> 6%
where the time goes in v7:
time: 123 us
  blocking collectives  55.1 us (45%)
  starting transfers between devices  27.5 us (22%)
  Pallas kernels  24.9 us (20%)
  waiting for transfers between devices  12.6 us (10%)
  local copies, waits for them, and re-layouts  2.18 us (2%)
    all_to_all x3, blocking collectives, local(): parts = lax.all_to_all(parts, 'list', 0, 0)  30.4 us
    all_to_all x2, blocking collectives, local(): cols = lax.all_to_all(col_pass(kern, parts, weight), 'item', 0, 0)  24.7 us
    pallas_call x12, Pallas kernels, call(): pl.pallas_call(body, out_shape=out, in_specs=whole(len(args)), out_specs=...  22.3 us
    ppermute x9, starting transfers between devices, shift_plane(): return lax.ppermute(block, ('item', 'list'), pairs)  12.2 us
    ppermute x6, starting transfers between devices, swap_core(): return lax.ppermute(block, 'item', [(i, i ^ 1) for i in range(N_ITEM)])  9.43 us
    ppermute x9, waiting for transfers between devices, shift_plane(): return lax.ppermute(block, ('item', 'list'), pairs)  8.08 us
    ppermute x6, starting transfers between devices, shift_z(): lax.ppermute(block, 'item', [(i, (i + 2 * step) % N_ITEM) for i in range(...  5.91 us
    ppermute x6, waiting for transfers between devices, shift_z(): lax.ppermute(block, 'item', [(i, (i + 2 * step) % N_ITEM) for i in range(...  4.52 us
  transfers between devices with their start and end apart: 21, of which 10 were waited for; matrix products, arithmetic and copies ran while one was open for 0% of the time, Pallas kernels for 6%

profile of v7, /device:TPU:1, one launch (start us, length us, event | category | flops | bytes accessed | tf_op | source)
XLA Modules:
  0.0 122.7 jit_solution(18172758939514076778)
XLA Ops:
  0.0 3.7 %collective-permute-start.2 = (bf16[16,4096]{1,0:T(8,128)(2,1)}, bf16[16,4096]{1,0:T(8,128)(2,1)S(1)}, u32[]{:S(2)}, u32[]{:S(2)}) collective-permute-start(bf16[16,4096]{1,0:T(8,128)(2,1)} %bitcast.6), channel_id=1, source_target_pairs={{0,2},{1,3},{2,0},{3,1},{4,6},{5,7},{6,4},{7,5},{8,10},{9,11},{10,... | collective-permute-start | bytes 393224 | tf_op jit(solution)/shard_map/ppermute | solution.py:69
  3.7 0.8 collective-permute-start.1
  4.5 0.7 collective-permute-start
  5.2 1.2 copy-done
  6.4 0.9 copy-done.2
  7.3 0.9 lists.1
  8.4 1.3 %collective-permute-done = bf16[16,4096]{1,0:T(8,128)(2,1)S(1)} collective-permute-done((bf16[16,4096]{1,0:T(8,128)(2,1)}, bf16[16,4096]{1,0:T(8,128)(2,1)S(1)}, u32[]{:S(2)}, u32[]{:S(2)}) %collective-permute-start) | collective-permute-done | bytes 131104 | tf_op jit(solution)/shard_map/ppermute | solution.py:69
  9.8 1.3 %collective-permute-start.3 = (bf16[64,2048]{1,0:T(8,128)(2,1)S(1)}, bf16[64,2048]{1,0:T(8,128)(2,1)S(1)}, u32[]{:S(2)}, u32[]{:S(2)}) collective-permute-start(bf16[64,2048]{1,0:T(8,128)(2,1)S(1)} %pad_maximum_fusion.refs_0_), channel_id=1, source_target_pairs={{0,4},{1,5},{2,6},{3,7},{4,8},{5,9},{6,10},{7,11},{8,12},{9,13},{1... | collective-permute-start | bytes 786440 | tf_op jit(solution)/shard_map/ppermute | solution.py:69
  11.1 1.5 %collective-permute-start.7 = (bf16[64,2048]{1,0:T(8,128)(2,1)S(1)}, bf16[64,2048]{1,0:T(8,128)(2,1)S(1)}, u32[]{:S(2)}, u32[]{:S(2)}) collective-permute-start(bf16[64,2048]{1,0:T(8,128)(2,1)S(1)} %pad_maximum_fusion.1.refs_4_), channel_id=1, source_target_pairs={{0,12},{1,13},{2,14},{3,15},{4,0},{5,1},{6,2},{7,3},{8,4},{9,5},{1... | collective-permute-start | bytes 786440 | tf_op jit(solution)/shard_map/ppermute | solution.py:69
  12.7 1.3 %collective-permute-start.4 = (bf16[64,2048]{1,0:T(8,128)(2,1)S(1)}, bf16[64,2048]{1,0:T(8,128)(2,1)S(1)}, u32[]{:S(2)}, u32[]{:S(2)}) collective-permute-start(bf16[64,2048]{1,0:T(8,128)(2,1)S(1)} %pad_maximum_fusion.refs_0_), channel_id=1, source_target_pairs={{0,12},{1,13},{2,14},{3,15},{4,0},{5,1},{6,2},{7,3},{8,4},{9,5},{1... | collective-permute-start | bytes 786440 | tf_op jit(solution)/shard_map/ppermute | solution.py:69
  13.9 0.2 collective-permute-start.6
  14.1 2.5 %collective-permute-done.3.refs_1_ = bf16[64,2048]{1,0:T(8,128)(2,1)S(1)} collective-permute-done((bf16[64,2048]{1,0:T(8,128)(2,1)S(1)}, bf16[64,2048]{1,0:T(8,128)(2,1)S(1)}, u32[]{:S(2)}, u32[]{:S(2)}) %collective-permute-start.3) | collective-permute-done | bytes 262176 | tf_op jit(solution)/shard_map/ppermute | solution.py:69
  16.7 2.7 %collective-permute-start.8 = (bf16[64,2048]{1,0:T(8,128)(2,1)S(1)}, bf16[64,2048]{1,0:T(8,128)(2,1)S(1)}, u32[]{:S(2)}, u32[]{:S(2)}) collective-permute-start(bf16[64,2048]{1,0:T(8,128)(2,1)S(1)} %collective-permute-done.7.refs_6_), channel_id=1, source_target_pairs={{0,12},{1,13},{2,14},{3,15},{4,0},{5,1},{6,2},{7,3},{8,4},{9,5},{1... | collective-permute-start | bytes 786440 | tf_op jit(solution)/shard_map/ppermute | solution.py:69
  19.4 0.1 collective-permute-done.4.refs_2_
  19.5 0.8 collective-permute-done.6.refs_5_
  20.4 3.1 %collective-permute-done.5.refs_3_ = bf16[64,2048]{1,0:T(8,128)(2,1)S(1)} collective-permute-done((bf16[64,2048]{1,0:T(8,128)(2,1)S(1)}, bf16[64,2048]{1,0:T(8,128)(2,1)S(1)}, u32[]{:S(2)}, u32[]{:S(2)}) %collective-permute-start.5) | collective-permute-done | bytes 262176 | tf_op jit(solution)/shard_map/ppermute | solution.py:69
  23.5 5.6 %generate.1 = (f32[2048,1024]{1,0:T(8,128)S(1)}, f32[2048,1024]{1,0:T(8,128)S(1)}, f32[2048,1024]{1,0:T(8,128)S(1)}, f32[2048,1024]{1,0:T(8,128)S(1)}, bf16[4096...) custom-call(bf16[2048,256]{1,0:T(8,128)(2,1)S(1)} %get-tuple-element.15.list_ref, ...), custom_call_target="tpu_custom_call" | custom-call | flops 4294967296 | bytes 1048576 | tf_op jit(solution)/shard_map/generate/pallas_call | solution.py:33
  29.1 11.0 %all_to_all.25.refs_4_ = bf16[16,32,128]{2,1,0:T(8,128)(2,1)S(1)} all-to-all(bf16[16,32,128]{2,1,0:T(8,128)(2,1)S(1)} %get-tuple-element.22), channel_id=1, replica_groups=mesh['item'=8,'list'=16] {'list'}, dimensions={0} | all-to-all | bytes 262144 | tf_op jit(solution)/shard_map/all_to_all | solution.py:339
  40.1 2.3 %columns.2 = f32[8,16,128]{2,1,0:T(8,128)S(1)} custom-call(f32[2048,1024]{1,0:T(8,128)S(1)} %get-tuple-element.17.refs_0_, f32[2048,1024]{1,0:T(8,128)S(1)} %get-tuple-element.18.refs_1_, f32[2048,1024]{1,0:T(8,128)S(1)} %get-tuple-element.19.refs_2_, f32[2048,1024]{1,0:T(8,128)S(1)} %get-tuple-element.20.refs_3_, ...), custom_call_target="tpu_custom_call" | custom-call | flops 16777216 | bytes 1048576 | tf_op jit(solution)/shard_map/columns/pallas_call | solution.py:33
  42.4 15.3 %all_to_all.26.refs_4_ = f32[8,16,128]{2,1,0:T(8,128)S(1)} all-to-all(f32[8,16,128]{2,1,0:T(8,128)S(1)} %columns.2), channel_id=1, replica_groups=mesh['item'=8,'list'=16] {'item'}, dimensions={0} | all-to-all | bytes 131072 | tf_op jit(solution)/shard_map/all_to_all | solution.py:340
  57.8 2.8 %rows.2 = bf16[16,32,128]{2,1,0:T(8,128)(2,1)S(1)} custom-call(f32[2048,1024]{1,0:T(8,128)S(1)} %get-tuple-element.17.refs_0_, f32[2048,1024]{1,0:T(8,128)S(1)} %get-tuple-element.18.refs_1_, f32[2048,1024]{1,0:T(8,128)S(1)} %get-tuple-element.19.refs_2_, f32[2048,1024]{1,0:T(8,128)S(1)} %get-tuple-element.20.refs_3_, f32[8,16,128]{2,1,0:T(8,128)S(1)} %all_to_all.26.refs_4_, ...), custom_call_target="tpu_custom_call" | custom-call | flops 16777216 | bytes 1048576 | tf_op jit(solution)/shard_map/rows/pallas_call | solution.py:33
  60.5 9.7 %all_to_all.27.refs_4_ = bf16[16,32,128]{2,1,0:T(8,128)(2,1)S(1)} all-to-all(bf16[16,32,128]{2,1,0:T(8,128)(2,1)S(1)} %rows.2), channel_id=1, replica_groups=mesh['item'=8,'list'=16] {'list'}, dimensions={0} | all-to-all | bytes 262144 | tf_op jit(solution)/shard_map/all_to_all | solution.py:339
  70.2 2.3 %columns.3 = f32[8,16,128]{2,1,0:T(8,128)S(1)} custom-call(f32[2048,1024]{1,0:T(8,128)S(1)} %get-tuple-element.17.refs_0_, f32[2048,1024]{1,0:T(8,128)S(1)} %get-tuple-element.18.refs_1_, f32[2048,1024]{1,0:T(8,128)S(1)} %get-tuple-element.19.refs_2_, f32[2048,1024]{1,0:T(8,128)S(1)} %get-tuple-element.20.refs_3_, ...), custom_call_target="tpu_custom_call" | custom-call | flops 16777216 | bytes 1048576 | tf_op jit(solution)/shard_map/columns/pallas_call | solution.py:33
  72.5 9.4 %all_to_all.28.refs_4_ = f32[8,16,128]{2,1,0:T(8,128)S(1)} all-to-all(f32[8,16,128]{2,1,0:T(8,128)S(1)} %columns.3), channel_id=1, replica_groups=mesh['item'=8,'list'=16] {'item'}, dimensions={0} | all-to-all | bytes 131072 | tf_op jit(solution)/shard_map/all_to_all | solution.py:340
  81.9 2.8 %rows.3 = bf16[16,32,128]{2,1,0:T(8,128)(2,1)S(1)} custom-call(f32[2048,1024]{1,0:T(8,128)S(1)} %get-tuple-element.17.refs_0_, f32[2048,1024]{1,0:T(8,128)S(1)} %get-tuple-element.18.refs_1_, f32[2048,1024]{1,0:T(8,128)S(1)} %get-tuple-element.19.refs_2_, f32[2048,1024]{1,0:T(8,128)S(1)} %get-tuple-element.20.refs_3_, f32[8,16,128]{2,1,0:T(8,128)S(1)} %all_to_all.28.refs_4_, ...), custom_call_target="tpu_custom_call" | custom-call | flops 16777216 | bytes 1048576 | tf_op jit(solution)/shard_map/rows/pallas_call | solution.py:33
  84.6 9.7 %all_to_all.29.refs_5_ = bf16[16,32,128]{2,1,0:T(8,128)(2,1)S(1)} all-to-all(bf16[16,32,128]{2,1,0:T(8,128)(2,1)S(1)} %rows.3), channel_id=1, replica_groups=mesh['item'=8,'list'=16] {'list'}, dimensions={0} | all-to-all | bytes 262144 | tf_op jit(solution)/shard_map/all_to_all | solution.py:342
  94.3 1.4 %totals.2 = (bf16[544,256]{1,0:T(8,128)(2,1)S(1)}, f32[8,4096]{1,0:T(8,128)S(1)}) custom-call(f32[2048,1024]{1,0:T(8,128)S(1)} %get-tuple-element.17.refs_0_, f32[2048,1024]{1,0:T(8,128)S(1)} %get-tuple-element.18.refs_1_, f32[2048,1024]{1,0:T(8,128)S(1)} %get-tuple-element.19.refs_2_, f32[2048,1024]{1,0:T(8,128)S(1)} %get-tuple-element.20.refs_3_, ...), custom_call_target="tpu_custom_call" | custom-call | flops 2147483648 | bytes 1048576 | tf_op jit(solution)/shard_map/totals/pallas_call | solution.py:33
  95.8 2.2 %collective-permute-start.10 = (bf16[544,256]{1,0:T(8,128)(2,1)S(1)}, bf16[544,256]{1,0:T(8,128)(2,1)S(1)}, u32[]{:S(2)}, u32[]{:S(2)}) collective-permute-start(bf16[544,256]{1,0:T(8,128)(2,1)S(1)} %get-tuple-element.24.refs_6_), channel_id=1, source_target_pairs={{0,16},{16,0},{32,48},{48,32},{64,80},{80,64},{96,112},{112,96},{1... | collective-permute-start | bytes 835592 | tf_op jit(solution)/shard_map/ppermute | solution.py:57
  98.0 1.5 %totals.3.refs_7_ = bf16[544,256]{1,0:T(8,128)(2,1)S(1)} custom-call(f32[2048,1024]{1,0:T(8,128)S(1)} %get-tuple-element.17.refs_0_, f32[2048,1024]{1,0:T(8,128)S(1)} %get-tuple-element.18.refs_1_, f32[2048,1024]{1,0:T(8,128)S(1)} %get-tuple-element.19.refs_2_, f32[2048,1024]{1,0:T(8,128)S(1)} %get-tuple-element.20.refs_3_, ...), custom_call_target="tpu_custom_call" | custom-call | flops 2147483648 | bytes 1048576 | tf_op jit(solution)/shard_map/totals/pallas_call | solution.py:33
  99.6 0.9 stay.4.refs_7_
  100.5 0.8 collective-permute-start.11
  101.3 0.9 stay.5.refs_7_
  102.1 1.0 collective-permute-start.12
  103.2 0.9 stay.6.refs_7_
  104.0 2.0 %collective-permute-start.13 = (bf16[272,256]{1,0:T(8,128)(2,1)S(1)}, bf16[272,256]{1,0:T(8,128)(2,1)S(1)}, u32[]{:S(2)}, u32[]{:S(2)}) collective-permute-start(bf16[272,256]{1,0:T(8,128)(2,1)S(1)} %stay.6.refs_7_), channel_id=1, source_target_pairs={{0,96},{16,112},{32,0},{48,16},{64,32},{80,48},{96,64},{112,80},{1... | collective-permute-start | bytes 417800 | tf_op jit(solution)/shard_map/ppermute | solution.py:298
  106.1 0.9 stay.7.mine_ref
  106.9 1.4 %collective-permute-done.13.c_ref = bf16[272,256]{1,0:T(8,128)(2,1)S(1)} collective-permute-done((bf16[272,256]{1,0:T(8,128)(2,1)S(1)}, bf16[272,256]{1,0:T(8,128)(2,1)S(1)}, u32[]{:S(2)}, u32[]{:S(2)}) %collective-permute-start.13) | collective-permute-done | bytes 139296 | tf_op jit(solution)/shard_map/ppermute | solution.py:298
  108.3 2.0 %collective-permute-done.12.b_ref = bf16[272,256]{1,0:T(8,128)(2,1)S(1)} collective-permute-done((bf16[272,256]{1,0:T(8,128)(2,1)S(1)}, bf16[272,256]{1,0:T(8,128)(2,1)S(1)}, u32[]{:S(2)}, u32[]{:S(2)}) %collective-permute-start.12) | collective-permute-done | bytes 139296 | tf_op jit(solution)/shard_map/ppermute | solution.py:298
  110.3 0.2 finish.1.refs_0_
  110.5 0.6 collective-permute-start.14
  111.2 1.1 collective-permute-start.16
  112.2 0.4 collective-permute-start.15
  112.6 2.6 %collective-permute-start.17 = (bf16[256,256]{1,0:T(8,128)(2,1)S(1)}, bf16[256,256]{1,0:T(8,128)(2,1)S(1)}, u32[]{:S(2)}, u32[]{:S(2)}) collective-permute-start(bf16[256,256]{1,0:T(8,128)(2,1)S(1)} %finish.1.refs_0_), channel_id=1, source_target_pairs={{0,16},{16,0},{32,48},{48,32},{64,80},{80,64},{96,112},{112,96},{1... | collective-permute-start | bytes 393224 | tf_op jit(solution)/shard_map/ppermute | solution.py:57
  115.2 1.1 collective-permute-done.14.refs_1_
  116.4 3.0 %collective-permute-start.18 = (bf16[256,256]{1,0:T(8,128)(2,1)S(1)}, bf16[256,256]{1,0:T(8,128)(2,1)S(1)}, u32[]{:S(2)}, u32[]{:S(2)}) collective-permute-start(bf16[256,256]{1,0:T(8,128)(2,1)S(1)} %collective-permute-done.14.refs_1_), channel_id=1, source_target_pairs={{0,16},{16,0},{32,48},{48,32},{64,80},{80,64},{96,112},{112,96},{1... | collective-permute-start | bytes 393224 | tf_op jit(solution)/shard_map/ppermute | solution.py:57
  119.3 1.5 %collective-permute-start.19 = (bf16[256,256]{1,0:T(8,128)(2,1)S(1)}, bf16[256,256]{1,0:T(8,128)(2,1)S(1)}, u32[]{:S(2)}, u32[]{:S(2)}) collective-permute-start(bf16[256,256]{1,0:T(8,128)(2,1)S(1)} %collective-permute-done.15.refs_2_), channel_id=1, source_target_pairs={{0,16},{16,0},{32,48},{48,32},{64,80},{80,64},{96,112},{112,96},{1... | collective-permute-start | bytes 393224 | tf_op jit(solution)/shard_map/ppermute | solution.py:57
  120.9 0.9 lay.2.refs_0_
  121.8 0.7 lay.3
  (28 shorter events, 0.4 us)
Async XLA Ops:
  0.0 8.3 %collective-permute-start.2 = (bf16[16,4096]{1,0:T(8,128)(2,1)}, bf16[16,4096]{1,0:T(8,128)(2,1)S(1)}, u32[]{:S(2)}, u32[]{:S(2)}) collective-permute-start(bf16[16,4096]{1,0:T(8,128)(2,1)} %bitcast.6), channel_id=1, source_target_pairs={{0,2},{1,3},{2,0},{3,1},{4,6},{5,7},{6,4},{7,5},{8,10},{9,11},{10,... | collective-permute-start | bytes 393224 | tf_op jit(solution)/shard_map/ppermute | solution.py:69
  3.7 4.7 %collective-permute-start.1 = (bf16[16,4096]{1,0:T(8,128)(2,1)}, bf16[16,4096]{1,0:T(8,128)(2,1)S(1)}, u32[]{:S(2)}, u32[]{:S(2)}) collective-permute-start(bf16[16,4096]{1,0:T(8,128)(2,1)} %bitcast.7), channel_id=1, source_target_pairs={{0,3},{1,0},{2,1},{3,2},{4,7},{5,4},{6,5},{7,6},{8,11},{9,8},{10,9... | collective-permute-start | bytes 393224 | tf_op jit(solution)/shard_map/ppermute | solution.py:69
  4.5 5.2 %collective-permute-start = (bf16[16,4096]{1,0:T(8,128)(2,1)}, bf16[16,4096]{1,0:T(8,128)(2,1)S(1)}, u32[]{:S(2)}, u32[]{:S(2)}) collective-permute-start(bf16[16,4096]{1,0:T(8,128)(2,1)} %bitcast.8), channel_id=1, source_target_pairs={{0,1},{1,2},{2,3},{3,0},{4,5},{5,6},{6,7},{7,4},{8,9},{9,10},{10,1... | collective-permute-start | bytes 393224 | tf_op jit(solution)/shard_map/ppermute | solution.py:69
  5.2 1.2 copy-start
  6.4 0.9 copy-start.2
  9.8 30.3 %copy-start.1 = (f32[4096]{0:T(1024)S(1)}, f32[4096]{0:T(1024)}, u32[]{:S(2)}) copy-start(f32[4096]{0:T(1024)} %param.5) | copy-start | bytes 49156
  9.8 6.8 %collective-permute-start.3 = (bf16[64,2048]{1,0:T(8,128)(2,1)S(1)}, bf16[64,2048]{1,0:T(8,128)(2,1)S(1)}, u32[]{:S(2)}, u32[]{:S(2)}) collective-permute-start(bf16[64,2048]{1,0:T(8,128)(2,1)S(1)} %pad_maximum_fusion.refs_0_), channel_id=1, source_target_pairs={{0,4},{1,5},{2,6},{3,7},{4,8},{5,9},{6,10},{7,11},{8,12},{9,13},{1... | collective-permute-start | bytes 786440 | tf_op jit(solution)/shard_map/ppermute | solution.py:69
  11.1 5.6 %collective-permute-start.7 = (bf16[64,2048]{1,0:T(8,128)(2,1)S(1)}, bf16[64,2048]{1,0:T(8,128)(2,1)S(1)}, u32[]{:S(2)}, u32[]{:S(2)}) collective-permute-start(bf16[64,2048]{1,0:T(8,128)(2,1)S(1)} %pad_maximum_fusion.1.refs_4_), channel_id=1, source_target_pairs={{0,12},{1,13},{2,14},{3,15},{4,0},{5,1},{6,2},{7,3},{8,4},{9,5},{1... | collective-permute-start | bytes 786440 | tf_op jit(solution)/shard_map/ppermute | solution.py:69
  12.7 6.9 %collective-permute-start.4 = (bf16[64,2048]{1,0:T(8,128)(2,1)S(1)}, bf16[64,2048]{1,0:T(8,128)(2,1)S(1)}, u32[]{:S(2)}, u32[]{:S(2)}) collective-permute-start(bf16[64,2048]{1,0:T(8,128)(2,1)S(1)} %pad_maximum_fusion.refs_0_), channel_id=1, source_target_pairs={{0,12},{1,13},{2,14},{3,15},{4,0},{5,1},{6,2},{7,3},{8,4},{9,5},{1... | collective-permute-start | bytes 786440 | tf_op jit(solution)/shard_map/ppermute | solution.py:69
  13.9 6.4 %collective-permute-start.6 = (bf16[64,2048]{1,0:T(8,128)(2,1)S(1)}, bf16[64,2048]{1,0:T(8,128)(2,1)S(1)}, u32[]{:S(2)}, u32[]{:S(2)}) collective-permute-start(bf16[64,2048]{1,0:T(8,128)(2,1)S(1)} %pad_maximum_fusion.1.refs_4_), channel_id=1, source_target_pairs={{0,4},{1,5},{2,6},{3,7},{4,8},{5,9},{6,10},{7,11},{8,12},{9,13},{1... | collective-permute-start | bytes 786440 | tf_op jit(solution)/shard_map/ppermute | solution.py:69
  16.6 6.8 %collective-permute-start.5 = (bf16[64,2048]{1,0:T(8,128)(2,1)S(1)}, bf16[64,2048]{1,0:T(8,128)(2,1)S(1)}, u32[]{:S(2)}, u32[]{:S(2)}) collective-permute-start(bf16[64,2048]{1,0:T(8,128)(2,1)S(1)} %collective-permute-done.3.refs_1_), channel_id=1, source_target_pairs={{0,4},{1,5},{2,6},{3,7},{4,8},{5,9},{6,10},{7,11},{8,12},{9,13},{1... | collective-permute-start | bytes 786440 | tf_op jit(solution)/shard_map/ppermute | solution.py:69
  16.7 6.8 %collective-permute-start.8 = (bf16[64,2048]{1,0:T(8,128)(2,1)S(1)}, bf16[64,2048]{1,0:T(8,128)(2,1)S(1)}, u32[]{:S(2)}, u32[]{:S(2)}) collective-permute-start(bf16[64,2048]{1,0:T(8,128)(2,1)S(1)} %collective-permute-done.7.refs_6_), channel_id=1, source_target_pairs={{0,12},{1,13},{2,14},{3,15},{4,0},{5,1},{6,2},{7,3},{8,4},{9,5},{1... | collective-permute-start | bytes 786440 | tf_op jit(solution)/shard_map/ppermute | solution.py:69
  40.1 17.6 %copy-start.3 = (f32[2048]{0:T(1024)S(1)}, f32[2048]{0:T(1024)}, u32[]{:S(2)}) copy-start(f32[2048]{0:T(1024)} %param.6) | copy-start | bytes 24580
  95.8 3.8 %collective-permute-start.10 = (bf16[544,256]{1,0:T(8,128)(2,1)S(1)}, bf16[544,256]{1,0:T(8,128)(2,1)S(1)}, u32[]{:S(2)}, u32[]{:S(2)}) collective-permute-start(bf16[544,256]{1,0:T(8,128)(2,1)S(1)} %get-tuple-element.24.refs_6_), channel_id=1, source_target_pairs={{0,16},{16,0},{32,48},{48,32},{64,80},{80,64},{96,112},{112,96},{1... | collective-permute-start | bytes 835592 | tf_op jit(solution)/shard_map/ppermute | solution.py:57
  99.5 3.7 %collective-permute-start.9 = (bf16[544,256]{1,0:T(8,128)(2,1)S(1)}, bf16[544,256]{1,0:T(8,128)(2,1)S(1)}, u32[]{:S(2)}, u32[]{:S(2)}) collective-permute-start(bf16[544,256]{1,0:T(8,128)(2,1)S(1)} %totals.3.refs_7_), channel_id=1, source_target_pairs={{0,16},{16,0},{32,48},{48,32},{64,80},{80,64},{96,112},{112,96},{1... | collective-permute-start | bytes 835592 | tf_op jit(solution)/shard_map/ppermute | solution.py:57
  100.5 9.9 %collective-permute-start.11 = (bf16[272,256]{1,0:T(8,128)(2,1)S(1)}, bf16[272,256]{1,0:T(8,128)(2,1)S(1)}, u32[]{:S(2)}, u32[]{:S(2)}) collective-permute-start(bf16[272,256]{1,0:T(8,128)(2,1)S(1)} %stay.4.refs_7_), channel_id=1, source_target_pairs={{0,64},{16,80},{32,96},{48,112},{64,0},{80,16},{96,32},{112,48},{1... | collective-permute-start | bytes 417800 | tf_op jit(solution)/shard_map/ppermute | solution.py:298
  102.1 8.2 %collective-permute-start.12 = (bf16[272,256]{1,0:T(8,128)(2,1)S(1)}, bf16[272,256]{1,0:T(8,128)(2,1)S(1)}, u32[]{:S(2)}, u32[]{:S(2)}) collective-permute-start(bf16[272,256]{1,0:T(8,128)(2,1)S(1)} %stay.5.refs_7_), channel_id=1, source_target_pairs={{0,32},{16,48},{32,64},{48,80},{64,96},{80,112},{96,0},{112,16},{1... | collective-permute-start | bytes 417800 | tf_op jit(solution)/shard_map/ppermute | solution.py:298
  104.0 4.3 %collective-permute-start.13 = (bf16[272,256]{1,0:T(8,128)(2,1)S(1)}, bf16[272,256]{1,0:T(8,128)(2,1)S(1)}, u32[]{:S(2)}, u32[]{:S(2)}) collective-permute-start(bf16[272,256]{1,0:T(8,128)(2,1)S(1)} %stay.6.refs_7_), channel_id=1, source_target_pairs={{0,96},{16,112},{32,0},{48,16},{64,32},{80,48},{96,64},{112,80},{1... | collective-permute-start | bytes 417800 | tf_op jit(solution)/shard_map/ppermute | solution.py:298
  110.5 5.8 %collective-permute-start.14 = (bf16[256,256]{1,0:T(8,128)(2,1)S(1)}, bf16[256,256]{1,0:T(8,128)(2,1)S(1)}, u32[]{:S(2)}, u32[]{:S(2)}) collective-permute-start(bf16[256,256]{1,0:T(8,128)(2,1)S(1)} %finish.1.refs_0_), channel_id=1, source_target_pairs={{0,64},{16,80},{32,96},{48,112},{64,0},{80,16},{96,32},{112,48},{1... | collective-permute-start | bytes 393224 | tf_op jit(solution)/shard_map/ppermute | solution.py:298
  111.2 8.2 %collective-permute-start.16 = (bf16[256,256]{1,0:T(8,128)(2,1)S(1)}, bf16[256,256]{1,0:T(8,128)(2,1)S(1)}, u32[]{:S(2)}, u32[]{:S(2)}) collective-permute-start(bf16[256,256]{1,0:T(8,128)(2,1)S(1)} %finish.1.refs_0_), channel_id=1, source_target_pairs={{0,96},{16,112},{32,0},{48,16},{64,32},{80,48},{96,64},{112,80},{1... | collective-permute-start | bytes 393224 | tf_op jit(solution)/shard_map/ppermute | solution.py:298
  112.2 7.1 %collective-permute-start.15 = (bf16[256,256]{1,0:T(8,128)(2,1)S(1)}, bf16[256,256]{1,0:T(8,128)(2,1)S(1)}, u32[]{:S(2)}, u32[]{:S(2)}) collective-permute-start(bf16[256,256]{1,0:T(8,128)(2,1)S(1)} %finish.1.refs_0_), channel_id=1, source_target_pairs={{0,32},{16,48},{32,64},{48,80},{64,96},{80,112},{96,0},{112,16},{1... | collective-permute-start | bytes 393224 | tf_op jit(solution)/shard_map/ppermute | solution.py:298
  112.6 8.2 %collective-permute-start.17 = (bf16[256,256]{1,0:T(8,128)(2,1)S(1)}, bf16[256,256]{1,0:T(8,128)(2,1)S(1)}, u32[]{:S(2)}, u32[]{:S(2)}) collective-permute-start(bf16[256,256]{1,0:T(8,128)(2,1)S(1)} %finish.1.refs_0_), channel_id=1, source_target_pairs={{0,16},{16,0},{32,48},{48,32},{64,80},{80,64},{96,112},{112,96},{1... | collective-permute-start | bytes 393224 | tf_op jit(solution)/shard_map/ppermute | solution.py:57
  116.4 4.5 %collective-permute-start.18 = (bf16[256,256]{1,0:T(8,128)(2,1)S(1)}, bf16[256,256]{1,0:T(8,128)(2,1)S(1)}, u32[]{:S(2)}, u32[]{:S(2)}) collective-permute-start(bf16[256,256]{1,0:T(8,128)(2,1)S(1)} %collective-permute-done.14.refs_1_), channel_id=1, source_target_pairs={{0,16},{16,0},{32,48},{48,32},{64,80},{80,64},{96,112},{112,96},{1... | collective-permute-start | bytes 393224 | tf_op jit(solution)/shard_map/ppermute | solution.py:57
  119.3 2.5 %collective-permute-start.20 = (bf16[256,256]{1,0:T(8,128)(2,1)S(1)}, bf16[256,256]{1,0:T(8,128)(2,1)S(1)}, u32[]{:S(2)}, u32[]{:S(2)}) collective-permute-start(bf16[256,256]{1,0:T(8,128)(2,1)S(1)} %collective-permute-done.16.refs_3_), channel_id=1, source_target_pairs={{0,16},{16,0},{32,48},{48,32},{64,80},{80,64},{96,112},{112,96},{1... | collective-permute-start | bytes 393224 | tf_op jit(solution)/shard_map/ppermute | solution.py:57
  119.3 2.5 %collective-permute-start.19 = (bf16[256,256]{1,0:T(8,128)(2,1)S(1)}, bf16[256,256]{1,0:T(8,128)(2,1)S(1)}, u32[]{:S(2)}, u32[]{:S(2)}) collective-permute-start(bf16[256,256]{1,0:T(8,128)(2,1)S(1)} %collective-permute-done.15.refs_2_), channel_id=1, source_target_pairs={{0,16},{16,0},{32,48},{48,32},{64,80},{80,64},{96,112},{112,96},{1... | collective-permute-start | bytes 393224 | tf_op jit(solution)/shard_map/ppermute | solution.py:57

commit v8 on v7

--- a/solution.py
+++ b/solution.py
@@ -171,19 +171,19 @@
                 by = scale_ref[:, QUART * h + 128 * n : QUART * h + 128 * (n + 1)]
                 total = total + ref[at, 128 * n : 128 * (n + 1)].reshape(16, 8, 128) * by[None]
         cols.append(lane(total.reshape(128, 128)))
-    out_ref[...] = jnp.broadcast_to(jnp.concatenate(cols, 0)[None], (N_ITEM, 16, 128))
+    out_ref[...] = jnp.broadcast_to(jnp.concatenate(cols, 0).astype(BF16)[None], (N_ITEM, 16, 128))
 
 
 def col_pass(kern, parts, weight):
     return call(
-        col_body, (*kern, parts, weight), VMEM((N_ITEM, 16, 128), F32), [VMEM((8, ITEM_DEV), F32)],
+        col_body, (*kern, parts, weight), VMEM((N_ITEM, 16, 128), BF16), [VMEM((8, ITEM_DEV), F32)],
         "columns", 2 * LIST_DEV * ITEM_DEV,
     )
 
 
 def row_body(*refs):
     *kern_refs, cols_ref, cap_ref, out_ref, scale_ref, total_ref = refs
-    scale = cap_ref[...] / cols_ref[...].sum(0)
+    scale = cap_ref[...] / cols_ref[...].astype(F32).sum(0)
     for k in range(16):
         scale_ref[128 * k : 128 * (k + 1), :] = jnp.broadcast_to(scale[k : k + 1, :], (128, 128)).T
 

time: 123 us -> 123 us (level)
  no operation moved by 1% of the time
where the time goes in v8:
time: 123 us; the launch traced here: 122 us
  blocking collectives  54.8 us (45%)
  starting transfers between devices  27.7 us (23%)
  Pallas kernels  24.9 us (20%)
  waiting for transfers between devices  12.4 us (10%)
  local copies, waits for them, and re-layouts  2.18 us (2%)
    all_to_all x3, blocking collectives, local(): parts = lax.all_to_all(parts, 'list', 0, 0)  30.4 us
    all_to_all x2, blocking collectives, local(): cols = lax.all_to_all(col_pass(kern, parts, weight), 'item', 0, 0)  24.4 us
    pallas_call x12, Pallas kernels, call(): pl.pallas_call(body, out_shape=out, in_specs=whole(len(args)), out_specs=...  22.3 us
    ppermute x9, starting transfers between devices, shift_plane(): return lax.ppermute(block, ('item', 'list'), pairs)  12.2 us
    ppermute x6, starting transfers between devices, swap_core(): return lax.ppermute(block, 'item', [(i, i ^ 1) for i in range(N_ITEM)])  9.29 us
    ppermute x9, waiting for transfers between devices, shift_plane(): return lax.ppermute(block, ('item', 'list'), pairs)  8.08 us
    ppermute x6, starting transfers between devices, shift_z(): lax.ppermute(block, 'item', [(i, (i + 2 * step) % N_ITEM) for i in range(...  6.2 us
    ppermute x6, waiting for transfers between devices, shift_z(): lax.ppermute(block, 'item', [(i, (i + 2 * step) % N_ITEM) for i in range(...  4.28 us
  transfers between devices with their start and end apart: 21, of which 10 were waited for; matrix products, arithmetic and copies ran while one was open for 0% of the time, Pallas kernels for 6%

profile of v8, /device:TPU:1, one launch (start us, length us, event | category | flops | bytes accessed | tf_op | source)
XLA Modules:
  0.0 122.4 jit_solution(10555657549272230912)
XLA Ops:
  0.0 3.7 %collective-permute-start.2 = (bf16[16,4096]{1,0:T(8,128)(2,1)}, bf16[16,4096]{1,0:T(8,128)(2,1)S(1)}, u32[]{:S(2)}, u32[]{:S(2)}) collective-permute-start(bf16[16,4096]{1,0:T(8,128)(2,1)} %bitcast.6), channel_id=1, source_target_pairs={{0,2},{1,3},{2,0},{3,1},{4,6},{5,7},{6,4},{7,5},{8,10},{9,11},{10,... | collective-permute-start | bytes 393224 | tf_op jit(solution)/shard_map/ppermute | solution.py:69
  3.7 0.8 collective-permute-start.1
  4.5 0.7 collective-permute-start
  5.2 1.2 copy-done
  6.4 0.9 copy-done.2
  7.3 0.9 lists.1
  8.4 1.3 %collective-permute-done = bf16[16,4096]{1,0:T(8,128)(2,1)S(1)} collective-permute-done((bf16[16,4096]{1,0:T(8,128)(2,1)}, bf16[16,4096]{1,0:T(8,128)(2,1)S(1)}, u32[]{:S(2)}, u32[]{:S(2)}) %collective-permute-start) | collective-permute-done | bytes 131104 | tf_op jit(solution)/shard_map/ppermute | solution.py:69
  9.8 1.3 %collective-permute-start.3 = (bf16[64,2048]{1,0:T(8,128)(2,1)S(1)}, bf16[64,2048]{1,0:T(8,128)(2,1)S(1)}, u32[]{:S(2)}, u32[]{:S(2)}) collective-permute-start(bf16[64,2048]{1,0:T(8,128)(2,1)S(1)} %pad_maximum_fusion.refs_0_), channel_id=1, source_target_pairs={{0,4},{1,5},{2,6},{3,7},{4,8},{5,9},{6,10},{7,11},{8,12},{9,13},{1... | collective-permute-start | bytes 786440 | tf_op jit(solution)/shard_map/ppermute | solution.py:69
  11.1 1.5 %collective-permute-start.7 = (bf16[64,2048]{1,0:T(8,128)(2,1)S(1)}, bf16[64,2048]{1,0:T(8,128)(2,1)S(1)}, u32[]{:S(2)}, u32[]{:S(2)}) collective-permute-start(bf16[64,2048]{1,0:T(8,128)(2,1)S(1)} %pad_maximum_fusion.1.refs_4_), channel_id=1, source_target_pairs={{0,12},{1,13},{2,14},{3,15},{4,0},{5,1},{6,2},{7,3},{8,4},{9,5},{1... | collective-permute-start | bytes 786440 | tf_op jit(solution)/shard_map/ppermute | solution.py:69
  12.7 1.3 %collective-permute-start.4 = (bf16[64,2048]{1,0:T(8,128)(2,1)S(1)}, bf16[64,2048]{1,0:T(8,128)(2,1)S(1)}, u32[]{:S(2)}, u32[]{:S(2)}) collective-permute-start(bf16[64,2048]{1,0:T(8,128)(2,1)S(1)} %pad_maximum_fusion.refs_0_), channel_id=1, source_target_pairs={{0,12},{1,13},{2,14},{3,15},{4,0},{5,1},{6,2},{7,3},{8,4},{9,5},{1... | collective-permute-start | bytes 786440 | tf_op jit(solution)/shard_map/ppermute | solution.py:69
  13.9 0.2 collective-permute-start.6
  14.1 2.5 %collective-permute-done.3.refs_1_ = bf16[64,2048]{1,0:T(8,128)(2,1)S(1)} collective-permute-done((bf16[64,2048]{1,0:T(8,128)(2,1)S(1)}, bf16[64,2048]{1,0:T(8,128)(2,1)S(1)}, u32[]{:S(2)}, u32[]{:S(2)}) %collective-permute-start.3) | collective-permute-done | bytes 262176 | tf_op jit(solution)/shard_map/ppermute | solution.py:69
  16.7 2.7 %collective-permute-start.8 = (bf16[64,2048]{1,0:T(8,128)(2,1)S(1)}, bf16[64,2048]{1,0:T(8,128)(2,1)S(1)}, u32[]{:S(2)}, u32[]{:S(2)}) collective-permute-start(bf16[64,2048]{1,0:T(8,128)(2,1)S(1)} %collective-permute-done.7.refs_6_), channel_id=1, source_target_pairs={{0,12},{1,13},{2,14},{3,15},{4,0},{5,1},{6,2},{7,3},{8,4},{9,5},{1... | collective-permute-start | bytes 786440 | tf_op jit(solution)/shard_map/ppermute | solution.py:69
  19.4 0.1 collective-permute-done.4.refs_2_
  19.5 0.8 collective-permute-done.6.refs_5_
  20.4 3.1 %collective-permute-done.5.refs_3_ = bf16[64,2048]{1,0:T(8,128)(2,1)S(1)} collective-permute-done((bf16[64,2048]{1,0:T(8,128)(2,1)S(1)}, bf16[64,2048]{1,0:T(8,128)(2,1)S(1)}, u32[]{:S(2)}, u32[]{:S(2)}) %collective-permute-start.5) | collective-permute-done | bytes 262176 | tf_op jit(solution)/shard_map/ppermute | solution.py:69
  23.5 5.6 %generate.1 = (f32[2048,1024]{1,0:T(8,128)S(1)}, f32[2048,1024]{1,0:T(8,128)S(1)}, f32[2048,1024]{1,0:T(8,128)S(1)}, f32[2048,1024]{1,0:T(8,128)S(1)}, bf16[4096...) custom-call(bf16[2048,256]{1,0:T(8,128)(2,1)S(1)} %get-tuple-element.15.list_ref, ...), custom_call_target="tpu_custom_call" | custom-call | flops 4294967296 | bytes 1048576 | tf_op jit(solution)/shard_map/generate/pallas_call | solution.py:33
  29.1 11.0 %all_to_all.25.refs_4_ = bf16[16,32,128]{2,1,0:T(8,128)(2,1)S(1)} all-to-all(bf16[16,32,128]{2,1,0:T(8,128)(2,1)S(1)} %get-tuple-element.22), channel_id=1, replica_groups=mesh['item'=8,'list'=16] {'list'}, dimensions={0} | all-to-all | bytes 262144 | tf_op jit(solution)/shard_map/all_to_all | solution.py:339
  40.1 2.3 %columns.2 = bf16[8,16,128]{2,1,0:T(8,128)(2,1)S(1)} custom-call(f32[2048,1024]{1,0:T(8,128)S(1)} %get-tuple-element.17.refs_0_, f32[2048,1024]{1,0:T(8,128)S(1)} %get-tuple-element.18.refs_1_, f32[2048,1024]{1,0:T(8,128)S(1)} %get-tuple-element.19.refs_2_, f32[2048,1024]{1,0:T(8,128)S(1)} %get-tuple-element.20.refs_3_, ...), custom_call_target="tpu_custom_call" | custom-call | flops 16777216 | bytes 1048576 | tf_op jit(solution)/shard_map/columns/pallas_call | solution.py:33
  42.4 15.2 %all_to_all.26.refs_4_ = bf16[8,16,128]{2,1,0:T(8,128)(2,1)S(1)} all-to-all(bf16[8,16,128]{2,1,0:T(8,128)(2,1)S(1)} %columns.2), channel_id=1, replica_groups=mesh['item'=8,'list'=16] {'item'}, dimensions={0} | all-to-all | bytes 65536 | tf_op jit(solution)/shard_map/all_to_all | solution.py:340
  57.6 2.8 %rows.2 = bf16[16,32,128]{2,1,0:T(8,128)(2,1)S(1)} custom-call(f32[2048,1024]{1,0:T(8,128)S(1)} %get-tuple-element.17.refs_0_, f32[2048,1024]{1,0:T(8,128)S(1)} %get-tuple-element.18.refs_1_, f32[2048,1024]{1,0:T(8,128)S(1)} %get-tuple-element.19.refs_2_, f32[2048,1024]{1,0:T(8,128)S(1)} %get-tuple-element.20.refs_3_, ...), custom_call_target="tpu_custom_call" | custom-call | flops 16777216 | bytes 1048576 | tf_op jit(solution)/shard_map/rows/pallas_call | solution.py:33
  60.4 9.7 %all_to_all.27.refs_4_ = bf16[16,32,128]{2,1,0:T(8,128)(2,1)S(1)} all-to-all(bf16[16,32,128]{2,1,0:T(8,128)(2,1)S(1)} %rows.2), channel_id=1, replica_groups=mesh['item'=8,'list'=16] {'list'}, dimensions={0} | all-to-all | bytes 262144 | tf_op jit(solution)/shard_map/all_to_all | solution.py:339
  70.1 2.3 %columns.3 = bf16[8,16,128]{2,1,0:T(8,128)(2,1)S(1)} custom-call(f32[2048,1024]{1,0:T(8,128)S(1)} %get-tuple-element.17.refs_0_, f32[2048,1024]{1,0:T(8,128)S(1)} %get-tuple-element.18.refs_1_, f32[2048,1024]{1,0:T(8,128)S(1)} %get-tuple-element.19.refs_2_, f32[2048,1024]{1,0:T(8,128)S(1)} %get-tuple-element.20.refs_3_, ...), custom_call_target="tpu_custom_call" | custom-call | flops 16777216 | bytes 1048576 | tf_op jit(solution)/shard_map/columns/pallas_call | solution.py:33
  72.4 9.2 %all_to_all.28.refs_4_ = bf16[8,16,128]{2,1,0:T(8,128)(2,1)S(1)} all-to-all(bf16[8,16,128]{2,1,0:T(8,128)(2,1)S(1)} %columns.3), channel_id=1, replica_groups=mesh['item'=8,'list'=16] {'item'}, dimensions={0} | all-to-all | bytes 65536 | tf_op jit(solution)/shard_map/all_to_all | solution.py:340
  81.6 2.8 %rows.3 = bf16[16,32,128]{2,1,0:T(8,128)(2,1)S(1)} custom-call(f32[2048,1024]{1,0:T(8,128)S(1)} %get-tuple-element.17.refs_0_, f32[2048,1024]{1,0:T(8,128)S(1)} %get-tuple-element.18.refs_1_, f32[2048,1024]{1,0:T(8,128)S(1)} %get-tuple-element.19.refs_2_, f32[2048,1024]{1,0:T(8,128)S(1)} %get-tuple-element.20.refs_3_, ...), custom_call_target="tpu_custom_call" | custom-call | flops 16777216 | bytes 1048576 | tf_op jit(solution)/shard_map/rows/pallas_call | solution.py:33
  84.3 9.7 %all_to_all.29.refs_5_ = bf16[16,32,128]{2,1,0:T(8,128)(2,1)S(1)} all-to-all(bf16[16,32,128]{2,1,0:T(8,128)(2,1)S(1)} %rows.3), channel_id=1, replica_groups=mesh['item'=8,'list'=16] {'list'}, dimensions={0} | all-to-all | bytes 262144 | tf_op jit(solution)/shard_map/all_to_all | solution.py:342
  94.0 1.4 %totals.2 = (bf16[544,256]{1,0:T(8,128)(2,1)S(1)}, f32[8,4096]{1,0:T(8,128)S(1)}) custom-call(f32[2048,1024]{1,0:T(8,128)S(1)} %get-tuple-element.17.refs_0_, f32[2048,1024]{1,0:T(8,128)S(1)} %get-tuple-element.18.refs_1_, f32[2048,1024]{1,0:T(8,128)S(1)} %get-tuple-element.19.refs_2_, f32[2048,1024]{1,0:T(8,128)S(1)} %get-tuple-element.20.refs_3_, ...), custom_call_target="tpu_custom_call" | custom-call | flops 2147483648 | bytes 1048576 | tf_op jit(solution)/shard_map/totals/pallas_call | solution.py:33
  95.5 2.2 %collective-permute-start.10 = (bf16[544,256]{1,0:T(8,128)(2,1)S(1)}, bf16[544,256]{1,0:T(8,128)(2,1)S(1)}, u32[]{:S(2)}, u32[]{:S(2)}) collective-permute-start(bf16[544,256]{1,0:T(8,128)(2,1)S(1)} %get-tuple-element.24.refs_6_), channel_id=1, source_target_pairs={{0,16},{16,0},{32,48},{48,32},{64,80},{80,64},{96,112},{112,96},{1... | collective-permute-start | bytes 835592 | tf_op jit(solution)/shard_map/ppermute | solution.py:57
  97.6 1.5 %totals.3.refs_7_ = bf16[544,256]{1,0:T(8,128)(2,1)S(1)} custom-call(f32[2048,1024]{1,0:T(8,128)S(1)} %get-tuple-element.17.refs_0_, f32[2048,1024]{1,0:T(8,128)S(1)} %get-tuple-element.18.refs_1_, f32[2048,1024]{1,0:T(8,128)S(1)} %get-tuple-element.19.refs_2_, f32[2048,1024]{1,0:T(8,128)S(1)} %get-tuple-element.20.refs_3_, ...), custom_call_target="tpu_custom_call" | custom-call | flops 2147483648 | bytes 1048576 | tf_op jit(solution)/shard_map/totals/pallas_call | solution.py:33
  99.2 0.9 stay.4.refs_7_
  100.1 0.9 collective-permute-start.11
  101.0 0.9 stay.5.refs_7_
  101.9 0.9 collective-permute-start.12
  102.8 0.9 stay.6.refs_7_
  103.7 2.1 %collective-permute-start.13 = (bf16[272,256]{1,0:T(8,128)(2,1)S(1)}, bf16[272,256]{1,0:T(8,128)(2,1)S(1)}, u32[]{:S(2)}, u32[]{:S(2)}) collective-permute-start(bf16[272,256]{1,0:T(8,128)(2,1)S(1)} %stay.6.refs_7_), channel_id=1, source_target_pairs={{0,96},{16,112},{32,0},{48,16},{64,32},{80,48},{96,64},{112,80},{1... | collective-permute-start | bytes 417800 | tf_op jit(solution)/shard_map/ppermute | solution.py:298
  105.8 0.9 stay.7.mine_ref
  106.7 1.3 %collective-permute-done.13.c_ref = bf16[272,256]{1,0:T(8,128)(2,1)S(1)} collective-permute-done((bf16[272,256]{1,0:T(8,128)(2,1)S(1)}, bf16[272,256]{1,0:T(8,128)(2,1)S(1)}, u32[]{:S(2)}, u32[]{:S(2)}) %collective-permute-start.13) | collective-permute-done | bytes 139296 | tf_op jit(solution)/shard_map/ppermute | solution.py:298
  108.0 2.0 %collective-permute-done.12.b_ref = bf16[272,256]{1,0:T(8,128)(2,1)S(1)} collective-permute-done((bf16[272,256]{1,0:T(8,128)(2,1)S(1)}, bf16[272,256]{1,0:T(8,128)(2,1)S(1)}, u32[]{:S(2)}, u32[]{:S(2)}) %collective-permute-start.12) | collective-permute-done | bytes 139296 | tf_op jit(solution)/shard_map/ppermute | solution.py:298
  109.9 0.2 finish.1.refs_0_
  110.1 0.8 collective-permute-start.14
  111.0 0.9 collective-permute-start.16
  111.9 0.6 collective-permute-start.15
  112.4 2.5 %collective-permute-start.17 = (bf16[256,256]{1,0:T(8,128)(2,1)S(1)}, bf16[256,256]{1,0:T(8,128)(2,1)S(1)}, u32[]{:S(2)}, u32[]{:S(2)}) collective-permute-start(bf16[256,256]{1,0:T(8,128)(2,1)S(1)} %finish.1.refs_0_), channel_id=1, source_target_pairs={{0,16},{16,0},{32,48},{48,32},{64,80},{80,64},{96,112},{112,96},{1... | collective-permute-start | bytes 393224 | tf_op jit(solution)/shard_map/ppermute | solution.py:57
  114.9 1.0 collective-permute-done.14.refs_1_
  115.9 3.1 %collective-permute-start.18 = (bf16[256,256]{1,0:T(8,128)(2,1)S(1)}, bf16[256,256]{1,0:T(8,128)(2,1)S(1)}, u32[]{:S(2)}, u32[]{:S(2)}) collective-permute-start(bf16[256,256]{1,0:T(8,128)(2,1)S(1)} %collective-permute-done.14.refs_1_), channel_id=1, source_target_pairs={{0,16},{16,0},{32,48},{48,32},{64,80},{80,64},{96,112},{112,96},{1... | collective-permute-start | bytes 393224 | tf_op jit(solution)/shard_map/ppermute | solution.py:57
  119.0 1.4 %collective-permute-start.19 = (bf16[256,256]{1,0:T(8,128)(2,1)S(1)}, bf16[256,256]{1,0:T(8,128)(2,1)S(1)}, u32[]{:S(2)}, u32[]{:S(2)}) collective-permute-start(bf16[256,256]{1,0:T(8,128)(2,1)S(1)} %collective-permute-done.15.refs_2_), channel_id=1, source_target_pairs={{0,16},{16,0},{32,48},{48,32},{64,80},{80,64},{96,112},{112,96},{1... | collective-permute-start | bytes 393224 | tf_op jit(solution)/shard_map/ppermute | solution.py:57
  120.5 0.9 lay.2.refs_0_
  121.5 0.7 lay.3
  (28 shorter events, 0.5 us)
Async XLA Ops:
  0.0 8.3 %collective-permute-start.2 = (bf16[16,4096]{1,0:T(8,128)(2,1)}, bf16[16,4096]{1,0:T(8,128)(2,1)S(1)}, u32[]{:S(2)}, u32[]{:S(2)}) collective-permute-start(bf16[16,4096]{1,0:T(8,128)(2,1)} %bitcast.6), channel_id=1, source_target_pairs={{0,2},{1,3},{2,0},{3,1},{4,6},{5,7},{6,4},{7,5},{8,10},{9,11},{10,... | collective-permute-start | bytes 393224 | tf_op jit(solution)/shard_map/ppermute | solution.py:69
  3.7 4.7 %collective-permute-start.1 = (bf16[16,4096]{1,0:T(8,128)(2,1)}, bf16[16,4096]{1,0:T(8,128)(2,1)S(1)}, u32[]{:S(2)}, u32[]{:S(2)}) collective-permute-start(bf16[16,4096]{1,0:T(8,128)(2,1)} %bitcast.7), channel_id=1, source_target_pairs={{0,3},{1,0},{2,1},{3,2},{4,7},{5,4},{6,5},{7,6},{8,11},{9,8},{10,9... | collective-permute-start | bytes 393224 | tf_op jit(solution)/shard_map/ppermute | solution.py:69
  4.5 5.2 %collective-permute-start = (bf16[16,4096]{1,0:T(8,128)(2,1)}, bf16[16,4096]{1,0:T(8,128)(2,1)S(1)}, u32[]{:S(2)}, u32[]{:S(2)}) collective-permute-start(bf16[16,4096]{1,0:T(8,128)(2,1)} %bitcast.8), channel_id=1, source_target_pairs={{0,1},{1,2},{2,3},{3,0},{4,5},{5,6},{6,7},{7,4},{8,9},{9,10},{10,1... | collective-permute-start | bytes 393224 | tf_op jit(solution)/shard_map/ppermute | solution.py:69
  5.2 1.2 %copy-start = (bf16[2048,256]{1,0:T(8,128)(2,1)S(1)}, bf16[2048,256]{1,0:T(8,128)(2,1)}, u32[]{:S(2)}) copy-start(bf16[2048,256]{1,0:T(8,128)(2,1)} %cent_ref.1) | copy-start | bytes 3145732
  6.4 0.9 copy-start.2
  9.8 30.3 %copy-start.1 = (f32[4096]{0:T(1024)S(1)}, f32[4096]{0:T(1024)}, u32[]{:S(2)}) copy-start(f32[4096]{0:T(1024)} %param.5) | copy-start | bytes 49156
  9.8 6.8 %collective-permute-start.3 = (bf16[64,2048]{1,0:T(8,128)(2,1)S(1)}, bf16[64,2048]{1,0:T(8,128)(2,1)S(1)}, u32[]{:S(2)}, u32[]{:S(2)}) collective-permute-start(bf16[64,2048]{1,0:T(8,128)(2,1)S(1)} %pad_maximum_fusion.refs_0_), channel_id=1, source_target_pairs={{0,4},{1,5},{2,6},{3,7},{4,8},{5,9},{6,10},{7,11},{8,12},{9,13},{1... | collective-permute-start | bytes 786440 | tf_op jit(solution)/shard_map/ppermute | solution.py:69
  11.1 5.6 %collective-permute-start.7 = (bf16[64,2048]{1,0:T(8,128)(2,1)S(1)}, bf16[64,2048]{1,0:T(8,128)(2,1)S(1)}, u32[]{:S(2)}, u32[]{:S(2)}) collective-permute-start(bf16[64,2048]{1,0:T(8,128)(2,1)S(1)} %pad_maximum_fusion.1.refs_4_), channel_id=1, source_target_pairs={{0,12},{1,13},{2,14},{3,15},{4,0},{5,1},{6,2},{7,3},{8,4},{9,5},{1... | collective-permute-start | bytes 786440 | tf_op jit(solution)/shard_map/ppermute | solution.py:69
  12.7 6.9 %collective-permute-start.4 = (bf16[64,2048]{1,0:T(8,128)(2,1)S(1)}, bf16[64,2048]{1,0:T(8,128)(2,1)S(1)}, u32[]{:S(2)}, u32[]{:S(2)}) collective-permute-start(bf16[64,2048]{1,0:T(8,128)(2,1)S(1)} %pad_maximum_fusion.refs_0_), channel_id=1, source_target_pairs={{0,12},{1,13},{2,14},{3,15},{4,0},{5,1},{6,2},{7,3},{8,4},{9,5},{1... | collective-permute-start | bytes 786440 | tf_op jit(solution)/shard_map/ppermute | solution.py:69
  13.9 6.4 %collective-permute-start.6 = (bf16[64,2048]{1,0:T(8,128)(2,1)S(1)}, bf16[64,2048]{1,0:T(8,128)(2,1)S(1)}, u32[]{:S(2)}, u32[]{:S(2)}) collective-permute-start(bf16[64,2048]{1,0:T(8,128)(2,1)S(1)} %pad_maximum_fusion.1.refs_4_), channel_id=1, source_target_pairs={{0,4},{1,5},{2,6},{3,7},{4,8},{5,9},{6,10},{7,11},{8,12},{9,13},{1... | collective-permute-start | bytes 786440 | tf_op jit(solution)/shard_map/ppermute | solution.py:69
  16.6 6.8 %collective-permute-start.5 = (bf16[64,2048]{1,0:T(8,128)(2,1)S(1)}, bf16[64,2048]{1,0:T(8,128)(2,1)S(1)}, u32[]{:S(2)}, u32[]{:S(2)}) collective-permute-start(bf16[64,2048]{1,0:T(8,128)(2,1)S(1)} %collective-permute-done.3.refs_1_), channel_id=1, source_target_pairs={{0,4},{1,5},{2,6},{3,7},{4,8},{5,9},{6,10},{7,11},{8,12},{9,13},{1... | collective-permute-start | bytes 786440 | tf_op jit(solution)/shard_map/ppermute | solution.py:69
  16.7 6.8 %collective-permute-start.8 = (bf16[64,2048]{1,0:T(8,128)(2,1)S(1)}, bf16[64,2048]{1,0:T(8,128)(2,1)S(1)}, u32[]{:S(2)}, u32[]{:S(2)}) collective-permute-start(bf16[64,2048]{1,0:T(8,128)(2,1)S(1)} %collective-permute-done.7.refs_6_), channel_id=1, source_target_pairs={{0,12},{1,13},{2,14},{3,15},{4,0},{5,1},{6,2},{7,3},{8,4},{9,5},{1... | collective-permute-start | bytes 786440 | tf_op jit(solution)/shard_map/ppermute | solution.py:69
  40.1 17.5 %copy-start.3 = (f32[2048]{0:T(1024)S(1)}, f32[2048]{0:T(1024)}, u32[]{:S(2)}) copy-start(f32[2048]{0:T(1024)} %param.6) | copy-start | bytes 24580
  95.5 3.7 %collective-permute-start.10 = (bf16[544,256]{1,0:T(8,128)(2,1)S(1)}, bf16[544,256]{1,0:T(8,128)(2,1)S(1)}, u32[]{:S(2)}, u32[]{:S(2)}) collective-permute-start(bf16[544,256]{1,0:T(8,128)(2,1)S(1)} %get-tuple-element.24.refs_6_), channel_id=1, source_target_pairs={{0,16},{16,0},{32,48},{48,32},{64,80},{80,64},{96,112},{112,96},{1... | collective-permute-start | bytes 835592 | tf_op jit(solution)/shard_map/ppermute | solution.py:57
  99.1 3.7 %collective-permute-start.9 = (bf16[544,256]{1,0:T(8,128)(2,1)S(1)}, bf16[544,256]{1,0:T(8,128)(2,1)S(1)}, u32[]{:S(2)}, u32[]{:S(2)}) collective-permute-start(bf16[544,256]{1,0:T(8,128)(2,1)S(1)} %totals.3.refs_7_), channel_id=1, source_target_pairs={{0,16},{16,0},{32,48},{48,32},{64,80},{80,64},{96,112},{112,96},{1... | collective-permute-start | bytes 835592 | tf_op jit(solution)/shard_map/ppermute | solution.py:57
  100.1 9.8 %collective-permute-start.11 = (bf16[272,256]{1,0:T(8,128)(2,1)S(1)}, bf16[272,256]{1,0:T(8,128)(2,1)S(1)}, u32[]{:S(2)}, u32[]{:S(2)}) collective-permute-start(bf16[272,256]{1,0:T(8,128)(2,1)S(1)} %stay.4.refs_7_), channel_id=1, source_target_pairs={{0,64},{16,80},{32,96},{48,112},{64,0},{80,16},{96,32},{112,48},{1... | collective-permute-start | bytes 417800 | tf_op jit(solution)/shard_map/ppermute | solution.py:298
  101.9 8.0 %collective-permute-start.12 = (bf16[272,256]{1,0:T(8,128)(2,1)S(1)}, bf16[272,256]{1,0:T(8,128)(2,1)S(1)}, u32[]{:S(2)}, u32[]{:S(2)}) collective-permute-start(bf16[272,256]{1,0:T(8,128)(2,1)S(1)} %stay.5.refs_7_), channel_id=1, source_target_pairs={{0,32},{16,48},{32,64},{48,80},{64,96},{80,112},{96,0},{112,16},{1... | collective-permute-start | bytes 417800 | tf_op jit(solution)/shard_map/ppermute | solution.py:298
  103.7 4.3 %collective-permute-start.13 = (bf16[272,256]{1,0:T(8,128)(2,1)S(1)}, bf16[272,256]{1,0:T(8,128)(2,1)S(1)}, u32[]{:S(2)}, u32[]{:S(2)}) collective-permute-start(bf16[272,256]{1,0:T(8,128)(2,1)S(1)} %stay.6.refs_7_), channel_id=1, source_target_pairs={{0,96},{16,112},{32,0},{48,16},{64,32},{80,48},{96,64},{112,80},{1... | collective-permute-start | bytes 417800 | tf_op jit(solution)/shard_map/ppermute | solution.py:298
  110.1 5.8 %collective-permute-start.14 = (bf16[256,256]{1,0:T(8,128)(2,1)S(1)}, bf16[256,256]{1,0:T(8,128)(2,1)S(1)}, u32[]{:S(2)}, u32[]{:S(2)}) collective-permute-start(bf16[256,256]{1,0:T(8,128)(2,1)S(1)} %finish.1.refs_0_), channel_id=1, source_target_pairs={{0,64},{16,80},{32,96},{48,112},{64,0},{80,16},{96,32},{112,48},{1... | collective-permute-start | bytes 393224 | tf_op jit(solution)/shard_map/ppermute | solution.py:298
  111.0 8.0 %collective-permute-start.16 = (bf16[256,256]{1,0:T(8,128)(2,1)S(1)}, bf16[256,256]{1,0:T(8,128)(2,1)S(1)}, u32[]{:S(2)}, u32[]{:S(2)}) collective-permute-start(bf16[256,256]{1,0:T(8,128)(2,1)S(1)} %finish.1.refs_0_), channel_id=1, source_target_pairs={{0,96},{16,112},{32,0},{48,16},{64,32},{80,48},{96,64},{112,80},{1... | collective-permute-start | bytes 393224 | tf_op jit(solution)/shard_map/ppermute | solution.py:298
  111.9 7.2 %collective-permute-start.15 = (bf16[256,256]{1,0:T(8,128)(2,1)S(1)}, bf16[256,256]{1,0:T(8,128)(2,1)S(1)}, u32[]{:S(2)}, u32[]{:S(2)}) collective-permute-start(bf16[256,256]{1,0:T(8,128)(2,1)S(1)} %finish.1.refs_0_), channel_id=1, source_target_pairs={{0,32},{16,48},{32,64},{48,80},{64,96},{80,112},{96,0},{112,16},{1... | collective-permute-start | bytes 393224 | tf_op jit(solution)/shard_map/ppermute | solution.py:298
  112.4 8.1 %collective-permute-start.17 = (bf16[256,256]{1,0:T(8,128)(2,1)S(1)}, bf16[256,256]{1,0:T(8,128)(2,1)S(1)}, u32[]{:S(2)}, u32[]{:S(2)}) collective-permute-start(bf16[256,256]{1,0:T(8,128)(2,1)S(1)} %finish.1.refs_0_), channel_id=1, source_target_pairs={{0,16},{16,0},{32,48},{48,32},{64,80},{80,64},{96,112},{112,96},{1... | collective-permute-start | bytes 393224 | tf_op jit(solution)/shard_map/ppermute | solution.py:57
  115.9 4.6 %collective-permute-start.18 = (bf16[256,256]{1,0:T(8,128)(2,1)S(1)}, bf16[256,256]{1,0:T(8,128)(2,1)S(1)}, u32[]{:S(2)}, u32[]{:S(2)}) collective-permute-start(bf16[256,256]{1,0:T(8,128)(2,1)S(1)} %collective-permute-done.14.refs_1_), channel_id=1, source_target_pairs={{0,16},{16,0},{32,48},{48,32},{64,80},{80,64},{96,112},{112,96},{1... | collective-permute-start | bytes 393224 | tf_op jit(solution)/shard_map/ppermute | solution.py:57
  119.0 2.5 %collective-permute-start.20 = (bf16[256,256]{1,0:T(8,128)(2,1)S(1)}, bf16[256,256]{1,0:T(8,128)(2,1)S(1)}, u32[]{:S(2)}, u32[]{:S(2)}) collective-permute-start(bf16[256,256]{1,0:T(8,128)(2,1)S(1)} %collective-permute-done.16.refs_3_), channel_id=1, source_target_pairs={{0,16},{16,0},{32,48},{48,32},{64,80},{80,64},{96,112},{112,96},{1... | collective-permute-start | bytes 393224 | tf_op jit(solution)/shard_map/ppermute | solution.py:57
  119.0 2.4 %collective-permute-start.19 = (bf16[256,256]{1,0:T(8,128)(2,1)S(1)}, bf16[256,256]{1,0:T(8,128)(2,1)S(1)}, u32[]{:S(2)}, u32[]{:S(2)}) collective-permute-start(bf16[256,256]{1,0:T(8,128)(2,1)S(1)} %collective-permute-done.15.refs_2_), channel_id=1, source_target_pairs={{0,16},{16,0},{32,48},{48,32},{64,80},{80,64},{96,112},{112,96},{1... | collective-permute-start | bytes 393224 | tf_op jit(solution)/shard_map/ppermute | solution.py:57
